TPU v7x, 32 devices: a whole 2x2x4 slice. The times are simulated.
32 devices in a mesh: seq: 8 (over z, core), dp: 4 (over y, x).
Axes of the slice: x: 2, y: 2, z: 4, core: 2. Of those that a mesh axis runs over, the one named last changes fastest.
Arguments:
- tokens: bfloat16 [4, 2048, 1536], P('dp', 'seq'), may hold values from -6 to 6
- cotangent: bfloat16 [4, 2048, 1536], P('dp', 'seq'), may hold values from -6 to 6
- positions: int32 [4, 2048], P('dp'), may hold values from 0 to 2047, as said below
- qkv_master: float32 [1536, 2048], P(('seq', 'dp')), may hold values from -0.21875 to 0.21875
- qkv_first: float32 [1536, 2048], P(('seq', 'dp')), may hold values from -192 to 192
- qkv_second: float32 [1536, 2048], P(('seq', 'dp')), may hold values from 3850.24 to 15564.8
- out_master: float32 [1536, 1536], P(('seq', 'dp')), may hold values from -0.4375 to 0.4375
- out_first: float32 [1536, 1536], P(('seq', 'dp')), may hold values from -16 to 16
- out_second: float32 [1536, 1536], P(('seq', 'dp')), may hold values from 39.3216 to 155.648
- gate_up_master: float32 [2, 1536, 8960], P(None, ('seq', 'dp')), may hold values from -0.15625 to 0.15625
- gate_up_first: float32 [2, 1536, 8960], P(None, ('seq', 'dp')), may hold values from -14 to 14
- gate_up_second: float32 [2, 1536, 8960], P(None, ('seq', 'dp')), may hold values from 21.2992 to 83.5584
- down_master: float32 [8960, 1536], P(('seq', 'dp')), may hold values from -0.0625 to 0.0625
- down_first: float32 [8960, 1536], P(('seq', 'dp')), may hold values from -32 to 32
- down_second: float32 [8960, 1536], P(('seq', 'dp')), may hold values from 155.648 to 622.592
- small_master: float32 [5120], P(('seq', 'dp')), as said below
- small_first: float32 [5120], P(('seq', 'dp'))
- small_second: float32 [5120], P(('seq', 'dp')), as said below
Outputs:
- layer_out: bfloat16 [4, 2048, 1536], P('dp', 'seq')
- input_grad: float32 [4, 2048, 1536], P('dp', 'seq')
- qkv_first_new: float32 [1536, 2048], P(('seq', 'dp'))
- qkv_second_new: float32 [1536, 2048], P(('seq', 'dp'))
- qkv_master_new: float32 [1536, 2048], P(('seq', 'dp'))
- out_first_new: float32 [1536, 1536], P(('seq', 'dp'))
- out_second_new: float32 [1536, 1536], P(('seq', 'dp'))
- out_master_new: float32 [1536, 1536], P(('seq', 'dp'))
- gate_up_first_new: float32 [2, 1536, 8960], P(None, ('seq', 'dp'))
- gate_up_second_new: float32 [2, 1536, 8960], P(None, ('seq', 'dp'))
- gate_up_master_new: float32 [2, 1536, 8960], P(None, ('seq', 'dp'))
- down_first_new: float32 [8960, 1536], P(('seq', 'dp'))
- down_second_new: float32 [8960, 1536], P(('seq', 'dp'))
- down_master_new: float32 [8960, 1536], P(('seq', 'dp'))
- small_first_new: float32 [5120], P(('seq', 'dp'))
- small_second_new: float32 [5120], P(('seq', 'dp'))
- small_master_new: float32 [5120], P(('seq', 'dp'))
Inputs may be any that keep to these rules, and one draw needn't show every extreme that they name: Each row is a permutation of 0 to 2047 made of runs of 128 consecutive positions, in rising order within a run; runs start at multiples of 128. `small_master`: gains first, bias last. `small_second`: Positive.
All inputs are finite; a program needn't handle non-finite values.
Results may differ from a plain program's by a relative error of at most 0.018.
The roundings to bfloat16 on the way count: a program that leaves them out, or rounds other values in their place, can miss the bound.
Values may be sent and summed in bfloat16 or wider, within the bound.
No kernel may reach another device: no remote copies, remote signals or barrier semaphores. Data moves between devices by JAX's collectives and lax.ppermute only.
A program may use at most 576 MiB of HBM per device.

v0:
```python
import functools

import jax
import jax.numpy as jnp
from jax import lax
from jax.experimental import pallas as pl
from jax.experimental.pallas import tpu as pltpu
from jax.sharding import PartitionSpec as P

D = 1536
HEADS = 12
KVH = 2
HD = 128
STEP = 10
KVW = KVH * HD
PIECE = 128


norm_eps = 1e-06
rope_base = 1000000.0
beta_one = 0.9
beta_two = 0.95
adam_eps = 1e-08
masked_score = -1e30
log2_e = 1.4426950408889634
bf16 = jnp.bfloat16
f32 = jnp.float32
vmem = pl.BlockSpec(memory_space=pltpu.VMEM)
smem = pl.BlockSpec(memory_space=pltpu.SMEM)
anywhere = pl.BlockSpec(memory_space=pl.ANY)


def shape_of(dims, kind):
    return jax.ShapeDtypeStruct(dims, kind)


def kernel_call(kernel, name, out_shape, operands, megabytes=32, **options):
    return pl.pallas_call(
        kernel,
        name=name,
        out_shape=out_shape,
        compiler_params=pltpu.CompilerParams(vmem_limit_bytes=megabytes << 20),
        cost_estimate=pl.CostEstimate(flops=10**6, bytes_accessed=10**6, transcendentals=0),
        **options,
    )(*operands)


def after(values, *others):
    return lax.optimization_barrier((values,) + others)[0]


def fence(*groups):
    flat, tree = jax.tree.flatten(groups)
    return jax.tree.unflatten(tree, lax.optimization_barrier(tuple(flat)))


def dot(left, right):
    return jnp.dot(left, right, preferred_element_type=f32)


def dot_transposed(left, right):
    return lax.dot_general(left, right, (((1,), (1,)), ((), ())), preferred_element_type=f32)


def rotary_tables(places):
    half_size = HD // 2
    freqs = rope_base ** (-(jnp.arange(half_size).astype(f32) * (2.0 / HD)))
    angles = places.astype(f32)[:, None] * freqs[None, :]
    cosine, sine = jnp.cos(angles), jnp.sin(angles)
    return jnp.concatenate([cosine, cosine], axis=1), jnp.concatenate([-sine, sine], axis=1)


def rms_scale(values):
    return lax.rsqrt(jnp.mean(values * values, axis=-1, keepdims=True) + norm_eps)


def swap_halves(values):
    return pltpu.roll(values, HD // 2, 1)


def head(index):
    return slice(index * HD, (index + 1) * HD)


def project_kv_kernel(tokens, w_qkv, gain, bias, cosine, sine, normed_ref, kv_ref):
    inputs = tokens[...].astype(f32)
    normed = (inputs * rms_scale(inputs) * gain[...]).astype(bf16)
    normed_ref[...] = normed
    rows = dot(normed, w_qkv[...]) + bias[:, D:]
    for j in range(KVH):
        part = rows[:, head(j)]
        kv_ref[:, head(j)] = (part * cosine[...] + swap_halves(part) * sine[...]).astype(bf16)
    kv_ref[:, KVW:] = rows[:, KVW:].astype(bf16)


def project_q_kernel(normed, w_qkv, bias, cosine, sine, query_ref):
    rows = dot(normed[...], w_qkv[...]) + bias[:, :D]
    for j in range(HEADS):
        part = rows[:, head(j)]
        query_ref[:, head(j)] = (part * cosine[...] + swap_halves(part) * sine[...]).astype(bf16)


def project_kv(tokens, w_qkv, gain, bias, cosine, sine):
    rows = tokens.shape[0]
    return kernel_call(
        project_kv_kernel,
        "project_kv",
        (shape_of((rows, D), bf16), shape_of((rows, 2 * KVW), bf16)),
        (tokens, w_qkv, gain, bias, cosine, sine),
        megabytes=58,
        grid=(1,),
        in_specs=[vmem, pl.BlockSpec((D, 2 * KVW), lambda i: (0, D // (2 * KVW)))] + [vmem] * 4,
        out_specs=(vmem, vmem),
    )


def project_q(normed, w_qkv, bias, cosine, sine):
    return kernel_call(
        project_q_kernel,
        "project_q",
        shape_of(normed.shape, bf16),
        (normed, w_qkv, bias, cosine, sine),
        megabytes=58,
        grid=(1,),
        in_specs=[vmem, pl.BlockSpec((D, D), lambda i: (0, 0))] + [vmem] * 3,
        out_specs=vmem,
    )


def mask_keys(values, query_bases, key_bases, first_run, fill):
    later = lax.broadcasted_iota(jnp.int32, (PIECE, PIECE), 0) - lax.broadcasted_iota(
        jnp.int32, (PIECE, PIECE), 1
    )
    keys, queries = values.shape
    rows = []
    for r in range(keys // PIECE):
        down = slice(r * PIECE, (r + 1) * PIECE)
        row = []
        for q in range(queries // PIECE):
            gap = query_bases[q] - key_bases[first_run + r]
            row.append(jnp.where(later <= gap, values[down, q * PIECE : (q + 1) * PIECE], fill))
        rows.append(jnp.concatenate(row, axis=1))
    return jnp.concatenate(rows, axis=0)


def attend_kernel(query_bases, key_bases, q_ref, *refs):
    pieces, (out_ref, lse_ref, kv_ref) = refs[:-3], refs[-3:]
    rows = q_ref.shape[0]
    for i, piece in enumerate(pieces):
        kv_ref[i * rows : (i + 1) * rows, :] = piece[...]
    groups = HEADS // KVH
    scale = HD**-0.5 * log2_e
    for kv in range(KVH):
        values = kv_ref[:, head(KVH + kv)].T
        for h in range(kv * groups, (kv + 1) * groups):
            queries = q_ref[:, head(h)]
            scores = []
            for run in range(key_bases.shape[0]):
                keys = kv_ref[run * PIECE : (run + 1) * PIECE, head(kv)]
                part = dot_transposed(keys, queries)
                scores.append(mask_keys(part, query_bases, key_bases, run, masked_score))
            scores = jnp.concatenate(scores, axis=0)
            top = jnp.max(scores, axis=0, keepdims=True)
            weights = jnp.exp2((scores - top) * scale)
            total = jnp.sum(weights, axis=0, keepdims=True)
            mixed = dot(values, weights.astype(bf16))
            out_ref[:, head(h)] = (mixed / total).T
            lse_ref[h : h + 1, :] = top * scale + jnp.log2(total)


def attend(queries, pieces, query_bases, key_bases):
    rows, total = queries.shape[0], key_bases.shape[0] * PIECE
    return kernel_call(
        attend_kernel,
        "attend",
        (
            shape_of((rows, D), f32),
            shape_of((HEADS, rows), f32),
            shape_of((total, 2 * KVW), bf16),
        ),
        (query_bases, key_bases, queries, *pieces),
        in_specs=[smem] * 2 + [vmem] * (1 + len(pieces)),
    )


def out_kernel(tokens, attended, w_out, gain, residual_ref, normed_ref, low_ref):
    low = attended[...].astype(bf16)
    low_ref[...] = low
    residual = tokens[...].astype(f32) + dot(low, w_out[...])
    residual_ref[...] = residual
    normed_ref[...] = (residual * rms_scale(residual) * gain[...]).astype(bf16)


def out_project(tokens, attended, w_out, gain):
    dims = tokens.shape
    return kernel_call(
        out_kernel,
        "out_project",
        (shape_of(dims, f32), shape_of(dims, bf16), shape_of(dims, bf16)),
        (tokens, attended, w_out, gain),
    )


def ffn_kernel(
    normed_own, normed_other, grad_own, grad_other, w_gate_up, w_down, *refs, earlier
):
    refs = refs[earlier:]
    out_refs, grad_refs = refs[:2], refs[2:4]
    normed_ref, ffn_grad_ref, hidden_ref, gate_ref, up_ref = refs[4:]
    rows = normed_own.shape[0]
    for i, (normed_in, grad_in) in enumerate(((normed_own, grad_own), (normed_other, grad_other))):
        to = slice(i * rows, (i + 1) * rows)
        normed, ffn_grad = normed_in[...], grad_in[...]
        normed_ref[0, to, :] = normed
        ffn_grad_ref[0, to, :] = ffn_grad
        gate = dot(normed, w_gate_up[0])
        up = dot(normed, w_gate_up[1])
        sigmoid = 1.0 / (1.0 + jnp.exp(-gate))
        silu = gate * sigmoid
        hidden = (silu * up).astype(bf16)
        hidden_ref[0, to, :] = hidden
        out_refs[i][...] = dot(hidden, w_down[...]).astype(bf16)
        hidden_grad = dot_transposed(ffn_grad, w_down[...])
        gate_grad = (hidden_grad * up * sigmoid * (1.0 + gate * (1.0 - sigmoid))).astype(bf16)
        up_grad = (hidden_grad * silu).astype(bf16)
        gate_ref[0, to, :] = gate_grad
        up_ref[0, to, :] = up_grad
        grad_refs[i][...] = (
            dot_transposed(gate_grad, w_gate_up[0]) + dot_transposed(up_grad, w_gate_up[1])
        ).astype(bf16)


def feed_forward(normed, grads, w_gate_up, w_down, slot, slots, kept):
    rows, width = normed[0].shape
    ff_own = w_down.shape[0]
    token = shape_of((rows, width), bf16)
    widths = (width, width, ff_own, ff_own, ff_own)
    operands = (*normed, *grads, w_gate_up, w_down)
    return kernel_call(
        functools.partial(ffn_kernel, earlier=len(kept)),
        "feed_forward",
        (token,) * 4 + tuple(shape_of((slots, 2 * rows, w), bf16) for w in widths),
        (*operands, *kept),
        grid=(1,),
        in_specs=[vmem] * len(operands) + [anywhere] * len(kept),
        out_specs=(vmem,) * 4
        + tuple(pl.BlockSpec((1, 2 * rows, w), lambda i: (slot, 0, 0)) for w in widths),
        input_output_aliases={len(operands) + i: 4 + i for i in range(len(kept))},
    )


def norm_back_kernel(
    got, own, other, residual_ref, cotangent, gain, w_out, grad_ref, low_ref, back_ref, gain_ref
):
    normed_grad = got[...].astype(f32) + own[...].astype(f32) + other[...].astype(f32)
    residual = residual_ref[...]
    scale = rms_scale(residual)
    unit = residual * scale
    gain_ref[...] = jnp.sum(normed_grad * unit, axis=0, keepdims=True)
    weighted = normed_grad * gain[...]
    grad = cotangent[...].astype(f32) + scale * (
        weighted - unit * jnp.mean(weighted * unit, axis=-1, keepdims=True)
    )
    grad_ref[...] = grad
    low = grad.astype(bf16)
    low_ref[...] = low
    back_ref[...] = dot_transposed(low, w_out[...]).astype(bf16)


def norm_back(got, own, other, residual, cotangent, gain, w_out):
    dims = residual.shape
    return kernel_call(
        norm_back_kernel,
        "norm_back",
        (shape_of(dims, f32), shape_of(dims, bf16), shape_of(dims, bf16), shape_of((1, D), f32)),
        (got, own, other, residual, cotangent, gain, w_out),
    )


def attend_back_kernel(
    query_bases,
    key_bases,
    q_ref,
    kv_ref,
    grad_ref,
    out_ref,
    lse_ref,
    cosine,
    sine,
    q_grad_ref,
    kv_own_ref,
    kv_other_ref,
    q_rows,
    grad_rows,
    deltas,
    q_sums,
):
    rows = q_ref.shape[0]
    groups = HEADS // KVH
    scale = HD**-0.5
    for kv in range(KVH):
        for j in range(groups):
            part = slice(j * rows, (j + 1) * rows)
            columns = head(kv * groups + j)
            q_rows[part, :] = q_ref[:, columns]
            grads = grad_ref[:, columns]
            grad_rows[part, :] = grads
            product = grads.astype(f32) * out_ref[:, columns]
            deltas[:, part] = jnp.sum(product.T, axis=0, keepdims=True)
        q_sums[...] = jnp.zeros_like(q_sums)

        @pl.loop(0, kv_ref.shape[0] // (2 * rows), unroll=2)
        def _(step):
            at = pl.ds(pl.multiple_of(step * (2 * rows), 2 * rows), 2 * rows)
            runs = 2 * rows // PIECE
            keys = kv_ref[at, head(kv)]
            values = kv_ref[at, head(KVH + kv)]
            key_sum = value_sum = None
            for j in range(groups):
                part = slice(j * rows, (j + 1) * rows)
                h = kv * groups + j
                queries, grads = q_rows[part, :], grad_rows[part, :]
                scores = dot_transposed(keys, queries)
                weights = jnp.exp2(scores * (scale * log2_e) - lse_ref[h : h + 1, :])
                weights = mask_keys(weights, query_bases, key_bases, step * runs, 0.0)
                weight_grads = dot_transposed(values, grads)
                score_grads = (weights * (weight_grads - deltas[:, part])).astype(bf16)
                value_part = dot(weights.astype(bf16), grads)
                key_part = dot(score_grads, queries)
                key_sum = key_part if key_sum is None else key_sum + key_part
                value_sum = value_part if value_sum is None else value_sum + value_part
                q_sums[part, :] += lax.dot_general(
                    score_grads, keys, (((0,), (0,)), ((), ())), preferred_element_type=f32
                )
            key_sum = (key_sum * scale).astype(bf16)
            value_sum = value_sum.astype(bf16)
            to = pl.ds(pl.multiple_of(step * rows, rows), rows)
            for ref, mine in ((kv_own_ref, slice(0, rows)), (kv_other_ref, slice(rows, 2 * rows))):
                ref[to, head(kv)] = key_sum[mine, :]
                ref[to, head(KVH + kv)] = value_sum[mine, :]

        for j in range(groups):
            part = q_sums[j * rows : (j + 1) * rows, :] * scale
            q_grad_ref[:, head(kv * groups + j)] = (
                part * cosine[...] - swap_halves(part) * sine[...]
            ).astype(bf16)


def attend_back(queries, key_value, grads, attended, lse, query_bases, key_bases, cosine, sine):
    rows, total = queries.shape[0], key_value.shape[0]
    groups = HEADS // KVH
    return kernel_call(
        attend_back_kernel,
        "attend_back",
        (
            shape_of((rows, D), bf16),
            shape_of((total // 2, 2 * KVW), bf16),
            shape_of((total // 2, 2 * KVW), bf16),
        ),
        (query_bases, key_bases, queries, key_value, grads, attended, lse, cosine, sine),
        in_specs=[smem] * 2 + [vmem] * 7,
        scratch_shapes=[
            pltpu.VMEM((groups * rows, HD), bf16),
            pltpu.VMEM((groups * rows, HD), bf16),
            pltpu.VMEM((1, groups * rows), f32),
            pltpu.VMEM((groups * rows, HD), f32),
        ],
    )


def input_kernel(
    tokens, gain, w_qkv, query_grad, cosine, sine, residual_grad, own, *refs
):
    got, (kv_ref, input_ref, gain_ref, bias_ref) = refs[:-4], refs[-4:]
    rows = own[...].astype(f32)
    for piece in got:
        rows = rows + piece[...].astype(f32)
    for j in range(KVH):
        part = rows[:, head(j)]
        kv_ref[:, head(j)] = (part * cosine[...] - swap_halves(part) * sine[...]).astype(bf16)
    kv_ref[:, KVW:] = rows[:, KVW:].astype(bf16)
    kv_grad = kv_ref[...]
    q_grad = query_grad[...]
    bias_ref[:, :D] = jnp.sum(q_grad.astype(f32), axis=0, keepdims=True)
    bias_ref[:, D:] = jnp.sum(kv_grad.astype(f32), axis=0, keepdims=True)
    normed_grad = dot_transposed(q_grad, w_qkv[:, :D]) + dot_transposed(kv_grad, w_qkv[:, D:])
    inputs = tokens[...].astype(f32)
    scale = rms_scale(inputs)
    unit = inputs * scale
    gain_ref[...] = jnp.sum(normed_grad * unit, axis=0, keepdims=True)
    weighted = normed_grad * gain[...]
    input_ref[...] = residual_grad[...] + scale * (
        weighted - unit * jnp.mean(weighted * unit, axis=-1, keepdims=True)
    )


def input_back(tokens, gain, w_qkv, query_grad, cosine, sine, residual_grad, own, got):
    rows = tokens.shape[0]
    return kernel_call(
        input_kernel,
        "input_back",
        (
            shape_of((rows, 2 * KVW), bf16),
            shape_of((rows, D), f32),
            shape_of((1, D), f32),
            shape_of((1, D + 2 * KVW), f32),
        ),
        (tokens, gain, w_qkv, query_grad, cosine, sine, residual_grad, own, *got),
        megabytes=58,
    )


def split_kernel(sides, values, *outs, cuts, bits):
    blocks = values.shape[0]
    for i, ((lo, hi), bit) in enumerate(zip(cuts, bits)):
        for out, side in ((outs[2 * i], sides[i]), (outs[2 * i + 1], 1 - sides[i])):
            for o in range(blocks // (2 * bit)):
                for j in range(bit):
                    out[o * bit + j] = values[(2 * o + side) * bit + j, :, lo:hi]


def split_columns(values, sides, cuts, bits):
    blocks, rows, _ = values.shape
    outs = kernel_call(
        functools.partial(split_kernel, cuts=cuts, bits=bits),
        "split_columns",
        tuple(shape_of((blocks // 2, rows, hi - lo), bf16) for lo, hi in cuts for _ in range(2)),
        (sides, values),
        in_specs=[smem, vmem],
    )
    return [(outs[2 * i], outs[2 * i + 1]) for i in range(len(cuts))]


def weight_grad_kernel(sides, left, *refs, count, inners, based):
    rights, refs = refs[:count], refs[count:]
    bases, outs = refs[: count * based], refs[count * based :]
    turned = left[...].reshape(-1, left.shape[-1]).T
    for i, right in enumerate(rights):
        result = dot(turned, right[...].reshape(-1, right.shape[-1]))
        if based:
            result = result + bases[i][...]
        if not inners:
            outs[i][...] = result.astype(outs[i].dtype)
            continue
        stays, goes = outs[2 * i], outs[2 * i + 1]
        rows = stays.shape[2]
        result = result.astype(bf16)
        for side, refs_of in ((0, (stays, goes)), (1, (goes, stays))):

            @pl.when(sides[i] == side)
            def _():
                for o in range(stays.shape[0]):
                    for bit in range(2):
                        for j in range(inners[i]):
                            block = (o * 2 + bit) * inners[i] + j
                            refs_of[bit][o, j] = result[block * rows : (block + 1) * rows]


def weight_grad(
    left, rights, slots=(0, 1), bases=(), split=None, rows=0, part=(0, 1), kind=bf16
):
    n_slots, tokens, m = left.shape
    n_slots = n_slots // slots[1]
    m = m // part[1]
    block = 3 * HD if m % (3 * HD) == 0 else HD
    steps = m // block
    first = part[0] * steps
    whole = pl.Buffered(buffer_count=1)
    sides, inners = split if split else (jnp.zeros((1,), jnp.int32), ())
    out_shape, out_specs = [], []
    for i, right in enumerate(rights):
        n = right.shape[-1]
        if not inners:
            out_shape.append(shape_of((m, n), kind))
            out_specs.append(pl.BlockSpec((block, n), lambda i: (i, 0)))
            continue
        outer = block // (2 * inners[i] * rows)
        for _ in range(2):
            out_shape.append(shape_of((steps * outer, inners[i], rows, n), bf16))
            out_specs.append(pl.BlockSpec((outer, inners[i], rows, n), lambda i: (i, 0, 0, 0)))
    outs = kernel_call(
        functools.partial(
            weight_grad_kernel, count=len(rights), inners=inners, based=int(bool(bases))
        ),
        "weight_grad",
        tuple(out_shape),
        (sides, left, *rights, *bases),
        megabytes=44,
        grid=(steps,),
        in_specs=[
            smem,
            pl.BlockSpec((n_slots, tokens, block), lambda i: (slots[0], 0, i + first)),
        ]
        + [
            pl.BlockSpec(
                (n_slots, tokens, right.shape[-1]),
                lambda i: (slots[0], 0, 0),
                pipeline_mode=whole,
            )
            for right in rights
        ]
        + [pl.BlockSpec((block, base.shape[1]), lambda i: (i + first, 0)) for base in bases],
        out_specs=tuple(out_specs),
    )
    if not inners:
        return outs
    outs = [out.reshape((-1,) + out.shape[2:]) for out in outs]
    return [(outs[2 * i], outs[2 * i + 1]) for i in range(len(rights))]


def stack_kernel(*refs, cuts):
    pieces, outs = refs[: -len(cuts)], refs[-len(cuts) :]
    for i, piece in enumerate(pieces):
        for out, (lo, hi) in zip(outs, cuts):
            out[i] = piece[:, lo:hi]


def stack_columns(pieces, cuts):
    return kernel_call(
        functools.partial(stack_kernel, cuts=cuts),
        "stack_columns",
        tuple(shape_of((len(pieces), pieces[0].shape[0], hi - lo), bf16) for lo, hi in cuts),
        tuple(pieces),
    )


def cut_kernel(core, values, kept_ref, sent_ref, *, n_dp, own, padded):
    kept_ref[...] = jnp.zeros_like(kept_ref)
    sent_ref[...] = jnp.zeros_like(sent_ref)
    for side, refs in ((0, (kept_ref, sent_ref)), (1, (sent_ref, kept_ref))):

        @pl.when(core[0] == side)
        def _():
            for s in range(2 * kept_ref.shape[0]):
                for d in range(n_dp):
                    start = (s * n_dp + d) * own
                    refs[s % 2][s // 2, 0, :, d * padded : d * padded + own] = values[
                        0, :, start : start + own
                    ].astype(bf16)


def cut_hidden(values, core, n_chips, n_dp, padded):
    two, rows, ff = values.shape
    own = ff // (2 * n_chips * n_dp)
    dims = (n_chips, two, rows, n_dp * padded)
    return kernel_call(
        functools.partial(cut_kernel, n_dp=n_dp, own=own, padded=padded),
        "cut_hidden",
        (shape_of(dims, bf16),) * 2,
        (core, values),
        grid=(two,),
        in_specs=[smem, pl.BlockSpec((1, rows, ff), lambda g: (g, 0, 0))],
        out_specs=(pl.BlockSpec((n_chips, 1, rows, n_dp * padded), lambda g: (0, g, 0, 0)),) * 2,
    )


def turn_kernel(chip, *refs, n_chips):
    ins, outs = refs[: len(refs) - n_chips], refs[len(refs) - n_chips :]
    per_side = len(ins) // 2
    for t, out in enumerate(outs):
        at = lax.rem(chip[0] + t, n_chips)
        for side in range(2):
            if per_side == 1:
                out[side] = ins[side][at]
            else:
                for g in range(2):
                    out[side, g] = ins[2 * side + g][at]


def turn_pairs(kept, got, chip, n_chips):
    rows, width = kept[0].shape[-2:]
    return kernel_call(
        functools.partial(turn_kernel, n_chips=n_chips),
        "turn_pairs",
        (shape_of((2, 2, rows, width), bf16),) * n_chips,
        (chip, *kept, *got),
        in_specs=[smem] + [vmem] * (len(kept) + len(got)),
    )


def add_kernel(*refs):
    *ins, out = refs
    total = ins[0][...].astype(f32)
    for ref in ins[1:]:
        total = total + ref[...].astype(f32)
    out[...] = total.astype(bf16)


def add(*arrays):
    return kernel_call(add_kernel, "add", shape_of(arrays[0].shape, bf16), arrays)


def add_turn_kernel(chip, kept, got, *outs):
    n = kept.shape[0]
    for t, out in enumerate(outs):
        at = lax.rem(chip[0] + t, n)
        out[...] = (kept[at].astype(f32) + got[at].astype(f32)).astype(bf16)


def add_turn(kept, got, chip):
    n = kept.shape[0]
    return kernel_call(
        add_turn_kernel,
        "add_turn",
        (shape_of(kept.shape[1:], bf16),) * n,
        (chip, kept, got),
        in_specs=[smem, vmem, vmem],
    )


def add_halve_kernel(mine, *refs):
    parts, (stays, goes) = refs[:-2], refs[-2:]
    count = len(parts) // 2
    at = 0
    for kept, got in zip(parts[:count], parts[count:]):
        for o in range(kept.shape[0]):
            for out, side in ((stays, mine[0]), (goes, 1 - mine[0])):
                out[at] = (kept[o, side].astype(f32) + got[o, side].astype(f32)).astype(bf16)
            at += 1


def add_halve(kept, got, mine, outer):
    rows, width = kept[0].shape[1:]
    blocks = sum(part.shape[0] for part in kept)
    inner = blocks // (2 * outer)
    half = shape_of((outer, inner, rows, width), bf16)
    stays, goes = kernel_call(
        add_halve_kernel,
        "add_halve",
        (half, half),
        (mine, *[part.reshape(-1, 2, inner, rows, width) for part in (*kept, *got)]),
        in_specs=[smem] + [vmem] * (len(kept) + len(got)),
        megabytes=40,
    )
    return stays.reshape(-1, rows, width), goes.reshape(-1, rows, width)


def add_halve_columns_kernel(mine, *refs, cuts):
    parts, (stays, goes) = refs[:-2], refs[-2:]
    count = len(parts) // 2
    lo = 0
    for kept, got, (first, last) in zip(parts[:count], parts[count:], cuts):
        hi = lo + last - first
        for o in range(kept.shape[0]):
            for out, side in ((stays, mine[0]), (goes, 1 - mine[0])):
                total = kept[o, side, :, :, first:last].astype(f32) + got[
                    o, side, :, :, first:last
                ].astype(f32)
                out[o, :, :, lo:hi] = total.astype(bf16)
        lo = hi


def add_halve_columns(kept, got, cuts, mine, outer):
    blocks, rows, _ = kept[0].shape
    inner = blocks // (2 * outer)
    width = sum(last - first for first, last in cuts)
    half = shape_of((outer, inner, rows, width), bf16)
    stays, goes = kernel_call(
        functools.partial(add_halve_columns_kernel, cuts=cuts),
        "add_halve",
        (half, half),
        (mine, *[part.reshape(outer, 2, inner, rows, -1) for part in (*kept, *got)]),
        in_specs=[smem] + [vmem] * (len(kept) + len(got)),
        megabytes=44,
    )
    return stays.reshape(-1, rows, width), goes.reshape(-1, rows, width)


def adamw_update(master, moment_one, moment_two, gradient, step_rate, decay_weight):
    first_new = beta_one * moment_one + (1.0 - beta_one) * gradient
    second_new = beta_two * moment_two + (1.0 - beta_two) * gradient * gradient
    first_hat = first_new / (1.0 - beta_one**STEP)
    second_hat = second_new / (1.0 - beta_two**STEP)
    master_new = master - step_rate * (
        first_hat / (jnp.sqrt(second_hat) + adam_eps) + decay_weight * master
    )
    return (first_new, second_new, master_new)


def adamw_kernel(where, master, first, second, *refs, n_dp, own, padded, rate, decay):
    pieces, (first_ref, second_ref, master_ref, slots, joined) = refs[:-5], refs[-5:]
    for t, piece in enumerate(pieces):
        for o in range(2):
            slots[where[2 * t + o]] = piece[o, 0]
    for s in range(slots.shape[0]):
        for d in range(n_dp):
            start = (s * n_dp + d) * own
            joined[:, start : start + own] = slots[
                s, :, d * padded : d * padded + own
            ].astype(f32)
    first_ref[0], second_ref[0], master_ref[0] = adamw_update(
        master[0], first[0], second[0], joined[...], rate, decay
    )


def adamw_hidden(master, first, second, pieces, where, n_dp, padded, rate, decay):
    two, rows, ff = master.shape
    n_seq = 2 * len(pieces)
    own = ff // (n_seq * n_dp)
    block = pl.BlockSpec((1, rows, ff), lambda g: (g, 0, 0))
    part = pl.BlockSpec((2, 1, rows, n_dp * padded), lambda g: (0, g, 0, 0))
    return kernel_call(
        functools.partial(
            adamw_kernel, n_dp=n_dp, own=own, padded=padded, rate=rate, decay=decay
        ),
        "adamw_hidden",
        (shape_of(master.shape, f32),) * 3,
        (where, master, first, second, *pieces),
        megabytes=44,
        grid=(two,),
        in_specs=[smem] + [block] * 3 + [part] * len(pieces),
        out_specs=(block,) * 3,
        scratch_shapes=[
            pltpu.VMEM((n_seq, rows, n_dp * padded), bf16),
            pltpu.VMEM((rows, ff), f32),
        ],
    )


def assemble_kernel(where, *refs, splits, counts):
    ins, outs, sems = refs[: len(counts)], refs[len(counts) : -1], refs[-1]
    copies = []
    entry = 0
    for ref, (column, count) in zip(ins, counts):
        for i in range(count):
            for out, start, width in splits[column]:
                copies.append(
                    pltpu.make_async_copy(
                        ref.at[i, :, pl.ds(start, width)],
                        outs[out[0]].at[where[entry], :, pl.ds(out[1], width)],
                        sems.at[len(copies)],
                    )
                )
            entry += 1
    for copy in copies:
        copy.start()
    for copy in copies:
        copy.wait()


def assemble(pieces, where, splits, out_widths):
    counts = [(column, array.shape[0]) for array, column in pieces]
    rows = pieces[0][0].shape[1]
    blocks = sum(count for column, count in counts if column == 0)
    n_copies = sum(count * len(splits[column]) for column, count in counts)
    return kernel_call(
        functools.partial(assemble_kernel, splits=splits, counts=counts),
        "assemble",
        tuple(shape_of((blocks, rows, w), bf16) for w in out_widths),
        (where.astype(jnp.int32), *[array for array, _ in pieces]),
        in_specs=[smem] + [anywhere] * len(pieces),
        out_specs=(vmem,) * len(out_widths),
        scratch_shapes=[pltpu.SemaphoreType.DMA((n_copies,))],
    )


def seq_perm(values, chips, flip):
    count = lax.axis_size("seq")
    return lax.ppermute(
        values, "seq", [(i, ((i + 2 * chips) % count) ^ flip) for i in range(count)]
    )


def dp_perm(values, bit):
    return lax.ppermute(values, "dp", [(i, i ^ bit) for i in range(lax.axis_size("dp"))])


def dp_bits():
    return [1 << i for i in range(lax.axis_size("dp").bit_length() - 1)]


def pick(values, index, axis):
    return lax.dynamic_index_in_dim(values, index, axis, keepdims=False)


def places_of():
    n_chips = lax.axis_size("seq") // 2
    seq_at = lax.axis_index("seq")
    return n_chips, seq_at // 2, seq_at % 2, lax.axis_size("dp"), lax.axis_index("dp")


def swap(values):
    return seq_perm(values, 0, 1)


def sent_pieces(values):
    return [values] + [seq_perm(values, t, 0) for t in range(1, lax.axis_size("seq") // 2)]


def shards(
    tokens,
    cotangent,
    positions,
    qkv_master,
    qkv_first,
    qkv_second,
    out_master,
    out_first,
    out_second,
    gate_up_master,
    gate_up_first,
    gate_up_second,
    down_master,
    down_first,
    down_second,
    small_master,
    small_first,
    small_second,
):
    n_chips, chip_at, core_at, n_dp, dp_at = places_of()
    n_seq = 2 * n_chips
    n_all = n_seq * n_dp
    bits = dp_bits()
    rows_own, qkv_width = qkv_master.shape
    half = qkv_width // 2
    small_own = small_master.shape[0]
    ff_dev = down_master.shape[0]
    ff_pad = -(-ff_dev // 16) * 16
    ff_own = n_dp * ff_pad
    inputs = tokens[0]
    upstream = cotangent[0]
    tok_rows = inputs.shape[0]
    seq_length = positions.shape[1]
    shifts = list(range(1, n_chips))

    ring_chips = [(chip_at - t) % n_chips for t in range(n_chips)]
    ring_order = jnp.stack(
        [chip * 2 + (core_at ^ flip) for chip in ring_chips for flip in range(2)]
    ).astype(jnp.int32)
    bases = positions[0, ::PIECE].reshape(n_seq, tok_rows // PIECE)
    key_bases = jnp.take(bases, ring_order, axis=0)
    query_bases = key_bases[0]
    key_bases = key_bases.reshape(-1)
    own_places = lax.dynamic_slice_in_dim(
        positions[0], (chip_at * 2 + core_at) * tok_rows, tok_rows, 0
    )
    cosine, sine = rotary_tables(own_places)

    small_block = jnp.pad(
        small_master.astype(bf16), (0, rows_own * HD - small_own)
    ).reshape(rows_own, HD)
    packed = jnp.concatenate([small_block, qkv_master.astype(bf16)], axis=1)
    qkv_ring = sent_pieces(packed)
    core_side = core_at.reshape(1).astype(jnp.int32)
    chip_side = chip_at.reshape(1).astype(jnp.int32)
    bit_sides = {bit: ((dp_at // bit) % 2).reshape(1).astype(jnp.int32) for bit in bits}
    cut_kept, cut_sent = cut_hidden(gate_up_master, core_side, n_chips, n_dp, ff_pad)
    to_send = turn_pairs([cut_kept], [swap(cut_sent)], chip_side, n_chips)
    qkv_ring, to_send, cosine, sine = fence(qkv_ring, to_send, cosine, sine)

    def exchange(shift):
        return seq_perm(to_send[shift], shift, 0)

    w_out = lax.all_gather(out_master.astype(bf16), ("seq", "dp"), axis=0, tiled=True)

    columns = ((0, HD + half), (HD + half, HD + qkv_width))
    orders = (bits, bits[::-1])
    held = list(stack_columns(qkv_ring, columns))
    flips = [[0], [0]]
    gate_up_pieces = {0: to_send[0]}
    groups = [shifts[:1], shifts[-1:], shifts[1:-1]] if n_chips > 2 else [shifts, [], []]
    for stage in range(len(bits)):
        got = [dp_perm(h, order[stage]) for h, order in zip(held, orders)]
        if stage == len(bits) - 1:
            swapped = [swap(h) for h in held]
        for shift in groups[min(stage, 1)] if stage < 2 else []:
            gate_up_pieces[shift] = exchange(shift)
        got, held, gate_up_pieces = fence(got, held, gate_up_pieces)
        flips = [f + [k ^ order[stage] for k in f] for f, order in zip(flips, orders)]
        if stage < len(bits) - 1:
            held = [jnp.concatenate([h, g], axis=0) for h, g in zip(held, got)]
    (swapped,) = fence(swapped)
    for shift in groups[2]:
        gate_up_pieces[shift] = exchange(shift)
    down_share = jnp.pad(down_master.astype(bf16), ((0, ff_pad - ff_dev), (0, 0)))
    w_down = lax.all_gather(after(down_share, *got), "dp", axis=0, tiled=True)
    got_swapped = [swap(g) for g in got]
    pieces, where = [], []
    for column in range(2):
        for flip, part, ks in (
            (0, held[column], flips[column][: n_dp // 2]),
            (0, got[column], flips[column][n_dp // 2 :]),
            (1, swapped[column], flips[column][: n_dp // 2]),
            (1, got_swapped[column], flips[column][n_dp // 2 :]),
        ):
            pieces.append((part, column))
            where += [
                (chip * 2 + (core_at ^ flip)) * n_dp + (dp_at ^ k) for k in ks for chip in ring_chips
            ]
    w_qkv, small_blocks = assemble(
        pieces,
        jnp.stack(where),
        ((((1, 0), 0, HD), ((0, 0), HD, half)), (((0, half), 0, half),)),
        (qkv_width, HD),
    )
    w_qkv = w_qkv.reshape(D, qkv_width)
    small_params = small_blocks.reshape(n_all, rows_own * HD)[:, :small_own].reshape(1, -1)
    small_params = small_params.astype(f32)
    gain_one = small_params[:, :D]
    gain_two = small_params[:, D : 2 * D]
    qkv_bias = small_params[:, 2 * D :]
    normed_one, key_value = project_kv(inputs, w_qkv, gain_one, qkv_bias, cosine, sine)
    gate_up_held = [
        jnp.concatenate([gate_up_pieces[t] for t in ts], axis=0)
        for ts in (range(n_chips // 2), range(n_chips // 2, n_chips))
    ]
    normed_one, key_value, gate_up_held = fence(normed_one, key_value, gate_up_held)

    kv_ring = sent_pieces(key_value)
    gate_up_parts = [
        [held, dp_perm(held, order[0])] for held, order in zip(gate_up_held, orders)
    ]
    gate_up_flips = [[0, order[0]] for order in orders]
    queries = project_q(normed_one, w_qkv, qkv_bias, cosine, sine)
    kv_swapped = [swap(kv_ring[0])] + [swap(after(piece, queries)) for piece in kv_ring[1:]]
    kv_ring, kv_swapped, gate_up_parts, queries, upstream = fence(
        kv_ring, kv_swapped, gate_up_parts, queries, upstream
    )

    def cross(start, stop, stage):
        for parts, flips_of, order in zip(gate_up_parts, gate_up_flips, orders):
            parts += [dp_perm(piece, order[stage]) for piece in parts[start:stop]]
            flips_of += [k ^ order[stage] for k in flips_of[start:stop]]

    upstream_ring = [upstream, seq_perm(upstream, 1, 0)]
    cross(0, 1 if len(bits) == 2 else 2, 1)
    attended, logsum, key_value_all = attend(
        queries, [piece for pair in zip(kv_ring, kv_swapped) for piece in pair], query_bases, key_bases
    )
    gate_up_parts, upstream_ring, attended, logsum, key_value_all = fence(
        gate_up_parts, upstream_ring, attended, logsum, key_value_all
    )

    def ring_step(pieces):
        return pieces + [seq_perm(pieces[-1], 1, 0)] if len(pieces) < n_chips else pieces

    upstream_ring = ring_step(upstream_ring)
    if len(bits) == 2:
        cross(1, 2, 1)
    else:
        cross(0, 4, 2)
    upstream_swapped = [swap(piece) for piece in upstream_ring[:2]]
    residual, normed_two, attended_low = out_project(inputs, attended, w_out, gain_two)
    normed_ring, normed_swapped = [normed_two], [swap(normed_two)]
    gate_up_parts, upstream_ring, upstream_swapped, normed_ring, normed_swapped, residual = fence(
        gate_up_parts, upstream_ring, upstream_swapped, normed_ring, normed_swapped, residual
    )

    pieces, where = [], []
    for column, (parts, flips_of) in enumerate(zip(gate_up_parts, gate_up_flips)):
        slots = ring_order[:n_chips] if column == 0 else ring_order[n_chips:]
        for part, k in zip(parts, flips_of):
            pieces.append((part.reshape(-1, rows_own, ff_own), 0))
            block = slots * n_dp + (dp_at ^ k)
            where.append(jnp.stack([block, n_all + block], axis=1).reshape(-1))
    (w_gate_up,) = assemble(
        pieces, jnp.concatenate(where), ((((0, 0), 0, ff_own),),), (ff_own,)
    )
    w_gate_up = w_gate_up.reshape(2, D, ff_own)
    out_pairs, kept = [], ()
    running = None
    for slot in range(n_chips):
        sent = None if running is None else seq_perm(running, 1, 0)
        normed_ring = ring_step(normed_ring)
        upstream_ring = ring_step(upstream_ring)
        out_own, out_other, grad_own, grad_other, *kept = feed_forward(
            (normed_ring[slot], normed_swapped[slot]),
            (upstream_ring[slot], upstream_swapped[slot]),
            w_gate_up,
            w_down,
            slot,
            n_chips,
            kept,
        )
        grad_swapped = swap(grad_other)
        if slot + 1 < n_chips:
            normed_swapped = normed_swapped + [swap(after(normed_ring[slot + 1], grad_own))]
        if slot + 2 < n_chips and len(upstream_swapped) < slot + 3:
            upstream_swapped = upstream_swapped + [swap(after(upstream_ring[slot + 2], grad_own))]
        if slot == 0:
            grad_first = (grad_own, grad_swapped)
        elif sent is None:
            running = add(grad_own, grad_swapped)
        else:
            running = add(grad_own, grad_swapped, after(sent, grad_own))
        running, normed_ring, normed_swapped, upstream_ring, upstream_swapped, kept = fence(
            running, normed_ring, normed_swapped, upstream_ring, upstream_swapped, kept
        )
        out_pairs = out_pairs + [(out_own, out_other)]
        if 1 < slot:
            out_pairs[slot - 1] = (out_pairs[slot - 1][0], swap(out_pairs[slot - 1][1]))
        if slot == 2:
            ring_first = add(*out_pairs[1])

    grad_ring = jnp.zeros_like(grad_first[0]) if running is None else seq_perm(running, 1, 0)
    normed_all, ffn_all, hidden_all, gate_grads_all, up_grads_all = kept
    first_split = (
        jnp.concatenate([bit_sides[order[0]] for order in orders]),
        tuple(order[0] for order in orders),
    )
    halves = [
        weight_grad(
            normed_all,
            (gate_grads_all, up_grads_all),
            split=first_split,
            rows=rows_own,
            part=(part, 2),
        )
        for part in range(2)
    ]
    out_running = seq_perm(ring_first, 1, 0)
    out_running = add(after(out_running, *halves[0][0]), *out_pairs[2])
    grad_ring, halves, out_pairs, out_running = fence(grad_ring, halves, out_pairs, out_running)

    got_one = [dp_perm(goes, order[0]) for (_, goes), order in zip(halves[0], orders)]
    out_running = seq_perm(out_running, 1, 0)
    out_pairs[-1] = (out_pairs[-1][0], swap(out_pairs[-1][1]))
    residual_grads, branch_grads, attended_grads, gain_two_grad = norm_back(
        grad_ring, *grad_first, residual, upstream, gain_two, w_out
    )
    query_pre, kv_grad_own, kv_grad_other = attend_back(
        queries,
        key_value_all,
        attended_grads,
        attended,
        logsum,
        query_bases,
        key_bases,
        cosine,
        sine,
    )
    got_one, kv_grad_own, kv_grad_other, query_pre, branch_grads, out_running, out_pairs = fence(
        got_one, kv_grad_own, kv_grad_other, query_pre, branch_grads, out_running, out_pairs
    )
    own_parts = kv_grad_own.reshape(n_chips, tok_rows, 2 * KVW)
    other_parts = swap(kv_grad_other).reshape(n_chips, tok_rows, 2 * KVW)
    kv_sum = add_turn(own_parts, other_parts, jnp.zeros_like(chip_side))
    kv_sum, halves, query_pre, branch_grads, kept = fence(
        kv_sum, halves, query_pre, branch_grads, kept
    )

    def next_split(kept_parts, got, done_bits, left_bits):
        rest = [bit for bit in bits[::-1] if bit not in done_bits]
        bit = left_bits[0]
        lead = sum(part.shape[0] for part in kept_parts) // 2 ** len(rest)
        return add_halve(kept_parts, got, bit_sides[bit], lead * 2 ** rest.index(bit))

    kv_got = [seq_perm(kv_sum[t], n_chips - t, 0) for t in range(1, n_chips)]
    got_two = [dp_perm(goes, order[0]) for (_, goes), order in zip(halves[1], orders)]
    by_core = (core_side, (n_dp,))
    (query_split,) = weight_grad(normed_one[None], (query_pre[None],), split=by_core, rows=rows_own)
    (out_split,) = weight_grad(
        attended_low[None], (branch_grads[None],), split=by_core, rows=rows_own
    )
    (down_grad,) = weight_grad(kept[2], (kept[1],))
    out_running = add(out_running, *out_pairs[3])
    kv_got, got_two, query_split, out_split, down_grad, out_running = fence(
        kv_got, got_two, query_split, out_split, down_grad, out_running
    )

    out_running = seq_perm(out_running, 1, 0)
    gate_up_split = [
        next_split([one[0], two[0]], [got, other], order[:1], order[1:])
        for one, two, got, other, order in zip(*halves, got_one, got_two, orders)
    ]
    gate_up_sums = [dp_perm(goes, order[1]) for (_, goes), order in zip(gate_up_split, orders)]
    both = [(split[0], swap(split[1])) for split in (query_split, out_split)]
    key_value_pre, input_grads, gain_one_grad, bias_grad = input_back(
        inputs,
        gain_one,
        w_qkv,
        query_pre,
        cosine,
        sine,
        residual_grads,
        kv_sum[0],
        kv_got,
    )
    down_split = split_columns(
        down_grad.reshape(n_dp, ff_pad, D),
        first_split[0],
        ((0, D // 2), (D // 2, D)),
        tuple(order[0] for order in orders),
    )
    ((kv_stays, kv_goes),) = weight_grad(
        normed_one[None], (key_value_pre[None],), split=by_core, rows=rows_own
    )
    (
        gate_up_split,
        gate_up_sums,
        down_split,
        both,
        input_grads,
        kv_stays,
        kv_goes,
        out_running,
        small_parts,
    ) = fence(
        gate_up_split,
        gate_up_sums,
        down_split,
        both,
        input_grads,
        kv_stays,
        kv_goes,
        out_running,
        (gain_one_grad, gain_two_grad, bias_grad),
    )

    down_got = [dp_perm(goes, order[0]) for (_, goes), order in zip(down_split, orders)]
    ready = []
    for split, got, order in zip(gate_up_split, gate_up_sums, orders):
        kept_part = split[0]
        for i in range(2, len(order)):
            kept_part, goes = next_split([kept_part], [got], order[:i], order[i:])
            got = dp_perm(goes, order[i])
        ready.append(add_halve([kept_part], [got], core_side, n_chips))
    to_send = turn_pairs(
        [kept_part for kept_part, _ in ready],
        [swap(sent) for _, sent in ready],
        chip_side,
        n_chips,
    )
    small_grad = jnp.concatenate(small_parts, axis=1).astype(bf16)
    small_grad = jnp.pad(
        small_grad.reshape(n_all, small_own), ((0, 0), (0, rows_own * HD - small_own))
    ).reshape(n_chips, 2, n_dp, rows_own, HD)
    kv_stays = jnp.concatenate(
        [pick(small_grad, core_at, 1).reshape(-1, rows_own, HD), kv_stays], axis=2
    )
    kv_goes = jnp.concatenate(
        [pick(small_grad, 1 - core_at, 1).reshape(-1, rows_own, HD), kv_goes], axis=2
    )
    kv_got = swap(kv_goes)
    rest_cuts = (((0, D), (0, 3 * HD)), ((0, D), (3 * HD, HD + 2 * KVW)))
    rest = [
        add_halve_columns(
            [kept_part, kv_stays],
            [got, kv_got],
            cuts,
            bit_sides[order[0]],
            n_chips * n_dp // (2 * order[0]),
        )
        for (kept_part, got), cuts, order in zip(both, rest_cuts, orders)
    ]
    to_send, rest, out_running, down_got = fence(to_send, rest, out_running, down_got)

    gate_up_owned = {0: to_send[0]}
    rest_got = [dp_perm(goes, order[0]) for (_, goes), order in zip(rest, orders)]
    for shift in groups[0] + groups[2]:
        gate_up_owned[shift] = exchange(shift)
    if len(bits) > 1:
        down_split = [
            next_split([kept_part], [got], order[:1], order[1:])
            for (kept_part, _), got, order in zip(down_split, down_got, orders)
        ]
    out_pairs[0] = (out_pairs[0][0], swap(out_pairs[0][1]))
    gate_up_owned, rest_got, down_split, out_pairs = fence(
        gate_up_owned, rest_got, down_split, out_pairs
    )

    for shift in groups[1]:
        gate_up_owned[shift] = exchange(shift)
    rest_send = []
    for (kept_part, _), got, order in zip(rest, rest_got, orders):
        for i in range(1, len(order)):
            kept_part, goes = next_split([kept_part], [got], order[:i], order[i:])
            got = dp_perm(goes, order[i])
        rest_send.append(add_turn(kept_part, got, chip_side))
    gate_up_owned, rest_send, down_split = fence(gate_up_owned, rest_send, down_split)

    rest_send = [
        jnp.concatenate([parts[t] for parts in rest_send], axis=1) for t in range(n_chips)
    ]
    rest_ring = [rest_send[0]] + [seq_perm(rest_send[shift], shift, 0) for shift in shifts]
    down_owned = []
    for (kept_part, goes), got, order in zip(down_split, down_got, orders):
        for i in range(1, len(order)):
            if i > 1:
                kept_part, goes = next_split([kept_part], [got], order[:i], order[i:])
            got = dp_perm(goes, order[i])
        down_owned.append(kept_part[0, :ff_dev].astype(f32) + got[0, :ff_dev].astype(f32))
    down_owned = jnp.concatenate(down_owned, axis=1)
    down_new = adamw_update(down_master, down_first, down_second, down_owned, 0.026, 0.1)
    rest_ring, down_new = fence(rest_ring, down_new)
    total = sum(piece.astype(f32) for piece in rest_ring)
    for t in range(4, n_chips):
        out_running = seq_perm(add(out_running, *out_pairs[t]), 1, 0)
    outputs = residual + out_pairs[0][0].astype(f32) + out_pairs[0][1].astype(f32)
    outputs = outputs + out_running.astype(f32)
    outputs = outputs.astype(bf16)
    gate_up_new = adamw_hidden(
        gate_up_master,
        gate_up_first,
        gate_up_second,
        [gate_up_owned[t] for t in range(n_chips)],
        ring_order,
        n_dp,
        ff_pad,
        0.064,
        0.1,
    )
    wide = D + 3 * HD
    query_owned, out_owned = total[:, :D], total[:, wide : wide + D]
    small_owned = total[:, D : D + HD]
    qkv_owned = jnp.concatenate(
        [query_owned, total[:, D + HD : wide], total[:, wide + D :]], axis=1
    )
    small_owned = small_owned.reshape(-1)[:small_own]

    qkv_new = adamw_update(qkv_master, qkv_first, qkv_second, qkv_owned, 0.09, 0.1)
    out_new = adamw_update(out_master, out_first, out_second, out_owned, 0.18, 0.1)
    small_new = adamw_update(small_master, small_first, small_second, small_owned, 0.6, 0.0)
    return (
        outputs[None],
        input_grads[None],
        *qkv_new,
        *out_new,
        *gate_up_new,
        *down_new,
        *small_new,
    )


def solution(mesh):
    in_specs = (
        P("dp", "seq", None),
        P("dp", "seq", None),
        P("dp", None),
        P(("seq", "dp"), None),
        P(("seq", "dp"), None),
        P(("seq", "dp"), None),
        P(("seq", "dp"), None),
        P(("seq", "dp"), None),
        P(("seq", "dp"), None),
        P(None, ("seq", "dp"), None),
        P(None, ("seq", "dp"), None),
        P(None, ("seq", "dp"), None),
        P(("seq", "dp"), None),
        P(("seq", "dp"), None),
        P(("seq", "dp"), None),
        P(("seq", "dp")),
        P(("seq", "dp")),
        P(("seq", "dp")),
    )
    out_specs = (
        P("dp", "seq", None),
        P("dp", "seq", None),
        P(("seq", "dp"), None),
        P(("seq", "dp"), None),
        P(("seq", "dp"), None),
        P(("seq", "dp"), None),
        P(("seq", "dp"), None),
        P(("seq", "dp"), None),
        P(None, ("seq", "dp"), None),
        P(None, ("seq", "dp"), None),
        P(None, ("seq", "dp"), None),
        P(("seq", "dp"), None),
        P(("seq", "dp"), None),
        P(("seq", "dp"), None),
        P(("seq", "dp")),
        P(("seq", "dp")),
        P(("seq", "dp")),
    )
    return jax.shard_map(shards, mesh=mesh, in_specs=in_specs, out_specs=out_specs, check_vma=False)
```

profile of v0, /device:TPU:8, one launch (start us, length us, event | category | flops | bytes accessed | tf_op | source)
XLA Modules:
  0.0 586.5 jit_solution(10788883279703118559)
XLA Ops:
  9.0 2.0 copy-done.7
  20.5 2.2 collective-permute-done.refs_1_
  22.7 13.4 %collective-permute-done.1.refs_2_ = bf16[48,2176]{1,0:T(8,128)(2,1)S(1)} collective-permute-done((bf16[48,2176]{1,0:T(8,128)(2,1)S(1)}, bf16[48,2176]{1,0:T(8,128)(2,1)S(1)}, u32[]{:S(2)}, u32[]{:S(2)}) %collective-permute-start.1) | collective-permute-done | bytes 208928 | tf_op jit(solution)/shard_map/ppermute | solution.py:759
  41.0 11.3 %collective-permute-done.5 = bf16[4,48,1024]{2,1,0:T(8,128)(2,1)S(1)} collective-permute-done((bf16[4,48,1024]{2,1,0:T(8,128)(2,1)S(1)}, bf16[4,48,1024]{2,1,0:T(8,128)(2,1)S(1)}, u32[]{:S(2)}, u32[]{:S(2)}) %collective-permute-start.5) | collective-permute-done | bytes 393248 | tf_op jit(solution)/shard_map/ppermute | solution.py:765
  58.3 10.1 %collective-permute-done.9 = bf16[2,2,48,1152]{3,2,1,0:T(8,128)(2,1)S(1)} collective-permute-done((bf16[2,2,48,1152]{3,2,1,0:T(8,128)(2,1)S(1)}, bf16[2,2,48,1152]{3,2,1,0:T(8,128)(2,1)S(1)}, u32[]{:S(2)}, u32[]{:S(2)}) %collective-permute-start.9) | collective-permute-done | bytes 442400 | tf_op jit(solution)/shard_map/ppermute | solution.py:759
  68.3 5.3 collective-permute-done.8.refs_5_
  80.8 24.7 %collective-permute-done.14 = bf16[2,2,48,1152]{3,2,1,0:T(8,128)(2,1)} collective-permute-done((bf16[2,2,48,1152]{3,2,1,0:T(8,128)(2,1)}, bf16[2,2,48,1152]{3,2,1,0:T(8,128)(2,1)}, u32[]{:S(2)}, u32[]{:S(2)}) %collective-permute-start.14) | collective-permute-done | bytes 442400 | tf_op jit(solution)/shard_map/ppermute | solution.py:759
  106.8 4.0 assemble.2
  110.8 2.6 copy-done.5
  114.8 3.6 project_kv.1
  123.1 4.1 collective-permute-start.16
  127.2 5.0 collective-permute-done.15.refs_2_
  132.2 5.1 project_q.1.q_ref
  137.3 8.1 %collective-permute-done.16.refs_4_ = bf16[256,512]{1,0:T(8,128)(2,1)S(1)} collective-permute-done((bf16[256,512]{1,0:T(8,128)(2,1)}, bf16[256,512]{1,0:T(8,128)(2,1)S(1)}, u32[]{:S(2)}, u32[]{:S(2)}) %collective-permute-start.16) | collective-permute-done | bytes 262176 | tf_op jit(solution)/shard_map/ppermute | solution.py:759
  145.4 3.7 collective-permute-done.17.refs_6_
  162.4 11.5 %attend.1 = (f32[256,1536]{1,0:T(8,128)S(1)}, f32[12,256]{1,0:T(8,128)S(1)}, bf16[2048,512]{1,0:T(8,128)(2,1)S(1)}) custom-call(s32[2]{0:T(128)S(1)} %slice_bitcast_fusion.1.query_bases, s32[16]{0:T(128)S(1)} %select_n.83.key_bases, bf16[256,1536]{1,0:T(8,128)(2,1)S(1)} %copy-done.11, bf16[256,512]{1,0:T(8,128)(2,1)S(1)} %copy-done.60, ...), custom_call_target="tpu_custom_call" | custom-call | flops 1000000 | bytes 1000000 | tf_op jit(solution)/shard_map/attend/pallas_call | solution.py:38
  176.4 9.1 %collective-permute-done.24 = bf16[4,2,48,1152]{3,2,1,0:T(8,128)(2,1)} collective-permute-done((bf16[4,2,48,1152]{3,2,1,0:T(8,128)(2,1)S(1)}, bf16[4,2,48,1152]{3,2,1,0:T(8,128)(2,1)}, u32[]{:S(2)}, u32[]{:S(2)}) %collective-permute-start.24) | collective-permute-done | bytes 884768 | tf_op jit(solution)/shard_map/ppermute | solution.py:765
  189.5 2.3 copy-done.6
  193.2 2.4 out_project.1
  196.6 8.5 %collective-permute-done.29.grad_own = bf16[256,1536]{1,0:T(8,128)(2,1)} collective-permute-done((bf16[256,1536]{1,0:T(8,128)(2,1)}, bf16[256,1536]{1,0:T(8,128)(2,1)}, u32[]{:S(2)}, u32[]{:S(2)}) %collective-permute-start.29) | collective-permute-done | bytes 786464 | tf_op jit(solution)/shard_map/ppermute | solution.py:759
  205.7 2.3 collective-permute-done.27
  214.0 5.5 assemble.3
  219.5 2.9 copy-done
  222.4 2.0 copy-done.4
  225.5 17.2 %feed_forward.4 = (bf16[256,1536]{1,0:T(8,128)(2,1)S(1)}, bf16[256,1536]{1,0:T(8,128)(2,1)S(1)}, bf16[256,1536]{1,0:T(8,128)(2,1)S(1)}, bf16[256,1536]{1,0:T(8,1...) custom-call(bf16[256,1536]{1,0:T(8,128)(2,1)} %get-tuple-element.448, ...), custom_call_target="tpu_custom_call" | custom-call | flops 1000000 | bytes 1000000 | tf_op jit(solution)/shard_map/feed_forward/pallas_call | solution.py:38
  245.9 2.0 collective-permute-done.36.grad_other
  249.0 2.0 collective-permute-start.38
  251.0 17.4 %feed_forward.5 = (bf16[256,1536]{1,0:T(8,128)(2,1)S(1)}, bf16[256,1536]{1,0:T(8,128)(2,1)S(1)}, bf16[256,1536]{1,0:T(8,128)(2,1)S(1)}, bf16[256,1536]{1,0:T(8,1...) custom-call(bf16[256,1536]{1,0:T(8,128)(2,1)} %collective-permute-do, ...), custom_call_target="tpu_custom_call", output_to_operand_aliasing={{4}: (6, {}), {5}: (7, {}), {6}: (8, {}), {7}: (9, {}), {8}... | custom-call | flops 1000000 | bytes 1000000 | tf_op jit(solution)/shard_map/feed_forward/pallas_call | solution.py:38
  269.1 2.0 collective-permute-done.37.refs_1_
  275.8 16.8 %feed_forward.6 = (bf16[256,1536]{1,0:T(8,128)(2,1)S(1)}, bf16[256,1536]{1,0:T(8,128)(2,1)}, bf16[256,1536]{1,0:T(8,128)(2,1)S(1)}, bf16[256,1536]{1,0:T(8,128)(...) custom-call(bf16[256,1536]{1,0:T(8,128)(2,1)S(1)} %collective-permut, ...), custom_call_target="tpu_custom_call", output_to_operand_aliasing={{4}: (6, {}), {5}: (7, {}), {6}: (8, {}), {7}: (9, {}), {8}... | custom-call | flops 1000000 | bytes 1000000 | tf_op jit(solution)/shard_map/feed_forward/pallas_call | solution.py:38
  293.9 15.6 %collective-permute-done.42.refs_2_ = bf16[256,1536]{1,0:T(8,128)(2,1)S(1)} collective-permute-done((bf16[256,1536]{1,0:T(8,128)(2,1)S(1)}, bf16[256,1536]{1,0:T(8,128)(2,1)S(1)}, u32[]{:S(2)}, u32[]{:S(2)}) %collective-permute-start.42) | collective-permute-done | bytes 786464 | tf_op jit(solution)/shard_map/ppermute | solution.py:759
  311.3 16.8 %feed_forward.7 = (bf16[256,1536]{1,0:T(8,128)(2,1)S(1)}, bf16[256,1536]{1,0:T(8,128)(2,1)}, bf16[256,1536]{1,0:T(8,128)(2,1)S(1)}, bf16[256,1536]{1,0:T(8,128)(...) custom-call(bf16[256,1536]{1,0:T(8,128)(2,1)S(1)} %collective-permut, ...), custom_call_target="tpu_custom_call", output_to_operand_aliasing={{4}: (6, {}), {5}: (7, {}), {6}: (8, {}), {7}: (9, {}), {8}... | custom-call | flops 1000000 | bytes 1000000 | tf_op jit(solution)/shard_map/feed_forward/pallas_call | solution.py:38
  328.1 2.1 copy-done.3
  334.5 3.7 collective-permute-start.47
  338.3 2.3 copy-done.2
  340.6 13.7 %weight_grad.6 = (bf16[8,1,48,1152]{3,2,1,0:T(8,128)(2,1)S(1)}, bf16[8,1,48,1152]{3,2,1,0:T(8,128)(2,1)S(1)}, bf16[4,2,48,1152]{3,2,1,0:T(8,128)(2,1)S(1)}, bf16[4,2,48,1152]{3,2,1,0:T(8,128)(2,1)S(1)}) custom-call(s32[2]{0:T(128)S(1)} %pad_add_fusion.8.sides, bf16[4,512,1536]{2,1,0:T(8,128)(2,1)} %get-tuple-element.533.left, ...), custom_call_target="tpu_custom_call" | custom-call | flops 1000000 | bytes 1000000 | tf_op jit(solution)/shard_map/weight_grad/pallas_call | solution.py:38
  356.2 14.8 %weight_grad.7 = (bf16[8,1,48,1152]{3,2,1,0:T(8,128)(2,1)S(1)}, bf16[8,1,48,1152]{3,2,1,0:T(8,128)(2,1)}, bf16[4,2,48,1152]{3,2,1,0:T(8,128)(2,1)S(1)}, bf16[4,2,48,1152]{3,2,1,0:T(8,128)(2,1)}) custom-call(s32[2]{0:T(128)S(1)} %pad_add_fusion.8.sides, bf16[4,512,1536]{2,1,0:T(8,128)(2,1)} %get-tuple-element.533.left, bf16[4,512,1152]{2,1,0:T(8,128)(2,1)S(1)} %copy-done.2, ...), custom_call_target="tpu_custom_call" | custom-call | flops 1000000 | bytes 1000000 | tf_op jit(solution)/shard_map/weight_grad/pallas_call | solution.py:38
  377.9 3.4 norm_back.1
  382.2 21.0 %attend_back.1 = (bf16[256,1536]{1,0:T(8,128)(2,1)S(1)}, bf16[1024,512]{1,0:T(8,128)(2,1)S(1)}, bf16[1024,512]{1,0:T(8,128)(2,1)S(1)}) custom-call(s32[2]{0:T(128)S(1)} %copy-done.66, s32[16]{0:T(128)S(1)} %select_n.83.key_bases, bf16[256,1536]{1,0:T(8,128)(2,1)S(1)} %copy-done.12, bf16[2048,512]{1,0:T(8,128)(2,1)S(1)} %copy-done.31, ...), custom_call_target="tpu_custom_call" | custom-call | flops 1000000 | bytes 1000000 | tf_op jit(solution)/shard_map/attend_back/pallas_call | solution.py:38
  403.5 2.5 collective-permute-done.56
  408.7 2.1 collective-permute-start.58
  413.3 4.0 weight_grad.8
  418.7 3.6 weight_grad.9
  423.7 11.0 %weight_grad.10 = bf16[1152,1536]{1,0:T(8,128)(2,1)S(1)} custom-call(s32[1]{0:T(128)} %constant.163.clone.1.chip.sides, bf16[4,512,1152]{2,1,0:T(8,128)(2,1)S(1)} %bitcast.166, bf16[4,512,1536]{2,1,0:T(8,128)(2,1)} %get-tuple-element.601.refs_0_), custom_call_target="tpu_custom_call" | custom-call | flops 1000000 | bytes 1000000 | tf_op jit(solution)/shard_map/weight_grad/pallas_call | solution.py:38
  435.4 2.4 add_halve.10
  439.8 2.4 add_halve.11
  449.4 7.6 %input_back.1 = (bf16[256,512]{1,0:T(8,128)(2,1)}, f32[256,1536]{1,0:T(8,128)}, f32[1,1536]{1,0:T(1,128)}, f32[1,2048]{1,0:T(1,128)}) custom-call(bf16[256,1536]{1,0:T(8,128)(2,1)} %bitcast.176, f32[1,1536]{1,0:T(1,128)} %get-tuple-element.769.gain, bf16[1536,2048]{1,0:T(8,128)(2,1)} %bitcast.169, bf16[256,1536]{1,0:T(8,128)(2,1)} %copy-done.25, ...), custom_call_target="tpu_custom_call" | custom-call | flops 1000000 | bytes 1000000 | tf_op jit(solution)/shard_map/input_back/pallas_call | solution.py:38
  459.5 4.5 collective-permute-done.66
  476.9 2.5 add_halve.14
  479.5 2.4 add_halve.15
  481.9 6.9 %collective-permute-done.70 = bf16[2,288,768]{2,1,0:T(8,128)(2,1)S(1)} collective-permute-done((bf16[2,288,768]{2,1,0:T(8,128)(2,1)S(1)}, bf16[2,288,768]{2,1,0:T(8,128)(2,1)S(1)}, u32[]{:S(2)}, u32[]{:S(2)}) %collective-permute-start.70) | collective-permute-done | bytes 884768 | tf_op jit(solution)/shard_map/ppermute | solution.py:765
  492.0 3.4 collective-permute-start.73
  495.9 8.8 %collective-permute-done.72.refs_1_ = bf16[2,2,48,1152]{3,2,1,0:T(8,128)(2,1)S(1)} collective-permute-done((bf16[2,2,48,1152]{3,2,1,0:T(8,128)(2,1)S(1)}, bf16[2,2,48,1152]{3,2,1,0:T(8,128)(2,1)S(1)}, u32[]{:S(2)}, u32[]{:S(2)}) %collective-permute-start.72) | collective-permute-done | bytes 442400 | tf_op jit(solution)/shard_map/ppermute | solution.py:759
  504.7 16.3 %collective-permute-done.73.refs_2_ = bf16[2,2,48,1152]{3,2,1,0:T(8,128)(2,1)S(1)} collective-permute-done((bf16[2,2,48,1152]{3,2,1,0:T(8,128)(2,1)S(1)}, bf16[2,2,48,1152]{3,2,1,0:T(8,128)(2,1)S(1)}, u32[]{:S(2)}, u32[]{:S(2)}) %collective-permute-start.73) | collective-permute-done | bytes 442400 | tf_op jit(solution)/shard_map/ppermute | solution.py:759
  525.0 4.3 collective-permute-start.77
  529.2 2.6 fusion.1
  531.8 7.9 %collective-permute-done.79.got = bf16[4,48,1792]{2,1,0:T(8,128)(2,1)S(1)} collective-permute-done((bf16[4,48,1792]{2,1,0:T(8,128)(2,1)S(1)}, bf16[4,48,1792]{2,1,0:T(8,128)(2,1)S(1)}, u32[]{:S(2)}, u32[]{:S(2)}) %collective-permute-start.79) | collective-permute-done | bytes 688160 | tf_op jit(solution)/shard_map/ppermute | solution.py:765
  540.1 3.0 collective-permute-start.80
  543.2 4.4 collective-permute-start.81
  550.2 7.6 %adamw_hidden.1 = (f32[2,48,8960]{2,1,0:T(8,128)}, f32[2,48,8960]{2,1,0:T(8,128)}, f32[2,48,8960]{2,1,0:T(8,128)}) custom-call(s32[8]{0:T(128)S(1)} %stack.261.where, f32[2,48,8960]{2,1,0:T(8,128)S(1)} %copy-done.8, f32[2,48,8960]{2,1,0:T(8,128)S(1)} %copy-done.21, f32[2,48,8960]{2,1,0:T(8,128)} %second.1, ...), custom_call_target="tpu_custom_call" | custom-call | flops 1000000 | bytes 1000000 | tf_op jit(solution)/shard_map/adamw_hidden/pallas_call | solution.py:38
  559.8 3.2 multiply_subtract_fusion
  563.0 4.0 collective-permute-done.80
  567.0 5.2 collective-permute-done.81
  572.3 4.0 collective-permute-done.82
  (458 shorter events, 141.9 us)
Async XLA Ops:
  7.2 182.3 %all-gather.3.cloned.1.call-start = ((), (), s32[]{:S(2)}) async-start(), calls=%async_computation | async-start | bytes 4866048 | tf_op jit(solution)/shard_map/all_gather | solution.py:854
  8.9 213.5 %all-gather.5.cloned.1.call-start = ((), (), s32[]{:S(2)}) async-start(), calls=%async_computation.1 | async-start | bytes 4423680 | tf_op jit(solution)/shard_map/all_gather | solution.py:876
  14.5 21.6 %collective-permute-start.1 = (bf16[48,2176]{1,0:T(8,128)(2,1)S(1)}, bf16[48,2176]{1,0:T(8,128)(2,1)S(1)}, u32[]{:S(2)}, u32[]{:S(2)}) collective-permute-start(bf16[48,2176]{1,0:T(8,128)(2,1)S(1)} %pad_maximum_fusion.11.refs_0_), channel_id=1, source_target_pairs={{0,16},{4,20},{8,24},{12,28},{16,0},{20,4},{24,8},{28,12},{1,17},{... | collective-permute-start | bytes 626696 | tf_op jit(solution)/shard_map/ppermute | solution.py:759
  15.6 22.3 %collective-permute-start.2 = (bf16[48,2176]{1,0:T(8,128)(2,1)S(1)}, bf16[48,2176]{1,0:T(8,128)(2,1)S(1)}, u32[]{:S(2)}, u32[]{:S(2)}) collective-permute-start(bf16[48,2176]{1,0:T(8,128)(2,1)S(1)} %pad_maximum_fusion.11.refs_0_), channel_id=1, source_target_pairs={{0,24},{4,28},{8,0},{12,4},{16,8},{20,12},{24,16},{28,20},{1,25},{... | collective-permute-start | bytes 626696 | tf_op jit(solution)/shard_map/ppermute | solution.py:759
  37.9 16.2 %collective-permute-start.4 = (bf16[4,48,1152]{2,1,0:T(8,128)(2,1)S(1)}, bf16[4,48,1152]{2,1,0:T(8,128)(2,1)S(1)}, u32[]{:S(2)}, u32[]{:S(2)}) collective-permute-start(bf16[4,48,1152]{2,1,0:T(8,128)(2,1)S(1)} %get-tuple-element.389), channel_id=1, source_target_pairs={{0,1},{1,0},{2,3},{3,2},{4,5},{5,4},{6,7},{7,6},{8,9},{9,8},{10,11... | collective-permute-start | bytes 1327112 | tf_op jit(solution)/shard_map/ppermute | solution.py:765
  39.5 15.7 %collective-permute-start.6 = (bf16[2,2,48,1152]{3,2,1,0:T(8,128)(2,1)S(1)}, bf16[2,2,48,1152]{3,2,1,0:T(8,128)(2,1)S(1)}, u32[]{:S(2)}, u32[]{:S(2)}) collective-permute-start(bf16[2,2,48,1152]{3,2,1,0:T(8,128)(2,1)S(1)} %get-tuple-element.388), channel_id=1, source_target_pairs={{0,8},{4,12},{8,16},{12,20},{16,24},{20,28},{24,0},{28,4},{1,9},{5... | collective-permute-start | bytes 1327112 | tf_op jit(solution)/shard_map/ppermute | solution.py:759
  55.4 19.1 %collective-permute-start.7 = (bf16[8,48,1152]{2,1,0:T(8,128)(2,1)S(1)}, bf16[8,48,1152]{2,1,0:T(8,128)(2,1)}, u32[]{:S(2)}, u32[]{:S(2)}) collective-permute-start(bf16[8,48,1152]{2,1,0:T(8,128)(2,1)S(1)} %constant_dynamic-update-slice_fusion.refs_0_), channel_id=1, source_target_pairs={{0,2},{1,3},{2,0},{3,1},{4,6},{5,7},{6,4},{7,5},{8,10},{9,11},{10,... | collective-permute-start | bytes 2654216 | tf_op jit(solution)/shard_map/ppermute | solution.py:765
  57.1 16.6 %collective-permute-start.8 = (bf16[8,48,1024]{2,1,0:T(8,128)(2,1)S(1)}, bf16[8,48,1024]{2,1,0:T(8,128)(2,1)}, u32[]{:S(2)}, u32[]{:S(2)}) collective-permute-start(bf16[8,48,1024]{2,1,0:T(8,128)(2,1)S(1)} %constant_dynamic-update-slice_fusion.2.refs_4_), channel_id=1, source_target_pairs={{0,1},{1,0},{2,3},{3,2},{4,5},{5,4},{6,7},{7,6},{8,9},{9,8},{10,11... | collective-permute-start | bytes 2359304 | tf_op jit(solution)/shard_map/ppermute | solution.py:765
  57.8 23.0 %collective-permute-start.10 = (bf16[8,48,1152]{2,1,0:T(8,128)(2,1)S(1)}, bf16[8,48,1152]{2,1,0:T(8,128)(2,1)}, u32[]{:S(2)}, u32[]{:S(2)}) collective-permute-start(bf16[8,48,1152]{2,1,0:T(8,128)(2,1)S(1)} %constant_dynamic-update-slice_fusion.refs_0_), channel_id=1, source_target_pairs={{0,4},{4,0},{8,12},{12,8},{16,20},{20,16},{24,28},{28,24},{1,5},{5... | collective-permute-start | bytes 2654216 | tf_op jit(solution)/shard_map/ppermute | solution.py:759
  57.8 22.1 %collective-permute-start.11 = (bf16[8,48,1024]{2,1,0:T(8,128)(2,1)S(1)}, bf16[8,48,1024]{2,1,0:T(8,128)(2,1)S(1)}, u32[]{:S(2)}, u32[]{:S(2)}) collective-permute-start(bf16[8,48,1024]{2,1,0:T(8,128)(2,1)S(1)} %constant_dynamic-update-slice_fusion.2.refs_4_), channel_id=1, source_target_pairs={{0,4},{4,0},{8,12},{12,8},{16,20},{20,16},{24,28},{28,24},{1,5},{5... | collective-permute-start | bytes 2359304 | tf_op jit(solution)/shard_map/ppermute | solution.py:759
  74.4 32.3 %collective-permute-start.12 = (bf16[8,48,1152]{2,1,0:T(8,128)(2,1)}, bf16[8,48,1152]{2,1,0:T(8,128)(2,1)}, u32[]{:S(2)}, u32[]{:S(2)}) collective-permute-start(bf16[8,48,1152]{2,1,0:T(8,128)(2,1)} %collective-permute-done.7.refs_1_), channel_id=1, source_target_pairs={{0,4},{4,0},{8,12},{12,8},{16,20},{20,16},{24,28},{28,24},{1,5},{5... | collective-permute-start | bytes 2654216 | tf_op jit(solution)/shard_map/ppermute | solution.py:759
  74.4 32.3 %collective-permute-start.13 = (bf16[8,48,1024]{2,1,0:T(8,128)(2,1)}, bf16[8,48,1024]{2,1,0:T(8,128)(2,1)}, u32[]{:S(2)}, u32[]{:S(2)}) collective-permute-start(bf16[8,48,1024]{2,1,0:T(8,128)(2,1)} %collective-permute-done.8.refs_5_), channel_id=1, source_target_pairs={{0,4},{4,0},{8,12},{12,8},{16,20},{20,16},{24,28},{28,24},{1,5},{5... | collective-permute-start | bytes 2359304 | tf_op jit(solution)/shard_map/ppermute | solution.py:759
  75.0 30.5 %collective-permute-start.14 = (bf16[2,2,48,1152]{3,2,1,0:T(8,128)(2,1)}, bf16[2,2,48,1152]{3,2,1,0:T(8,128)(2,1)}, u32[]{:S(2)}, u32[]{:S(2)}) collective-permute-start(bf16[2,2,48,1152]{3,2,1,0:T(8,128)(2,1)} %get-tuple-element.410), channel_id=1, source_target_pairs={{0,16},{4,20},{8,24},{12,28},{16,0},{20,4},{24,8},{28,12},{1,17},{... | collective-permute-start | bytes 1327112 | tf_op jit(solution)/shard_map/ppermute | solution.py:759
  118.4 34.1 %collective-permute-start.22 = (bf16[4,2,48,1152]{3,2,1,0:T(8,128)(2,1)S(1)}, bf16[4,2,48,1152]{3,2,1,0:T(8,128)(2,1)}, u32[]{:S(2)}, u32[]{:S(2)}) collective-permute-start(bf16[4,2,48,1152]{3,2,1,0:T(8,128)(2,1)S(1)} %pad_maximum_fusion.4), channel_id=1, source_target_pairs={{0,1},{1,0},{2,3},{3,2},{4,5},{5,4},{6,7},{7,6},{8,9},{9,8},{10,11... | collective-permute-start | bytes 2654216 | tf_op jit(solution)/shard_map/ppermute | solution.py:765
  120.1 32.7 %collective-permute-start.23 = (bf16[4,2,48,1152]{3,2,1,0:T(8,128)(2,1)S(1)}, bf16[4,2,48,1152]{3,2,1,0:T(8,128)(2,1)}, u32[]{:S(2)}, u32[]{:S(2)}) collective-permute-start(bf16[4,2,48,1152]{3,2,1,0:T(8,128)(2,1)S(1)} %pad_maximum_fusion.5), channel_id=1, source_target_pairs={{0,2},{1,3},{2,0},{3,1},{4,6},{5,7},{6,4},{7,5},{8,10},{9,11},{10,... | collective-permute-start | bytes 2654216 | tf_op jit(solution)/shard_map/ppermute | solution.py:765
  123.1 22.3 %collective-permute-start.16 = (bf16[256,512]{1,0:T(8,128)(2,1)}, bf16[256,512]{1,0:T(8,128)(2,1)S(1)}, u32[]{:S(2)}, u32[]{:S(2)}) collective-permute-start(bf16[256,512]{1,0:T(8,128)(2,1)} %get-tuple-element.425.refs_0_), channel_id=1, source_target_pairs={{0,16},{4,20},{8,24},{12,28},{16,0},{20,4},{24,8},{28,12},{1,17},{... | collective-permute-start | bytes 786440 | tf_op jit(solution)/shard_map/ppermute | solution.py:759
  127.2 21.9 %collective-permute-start.17 = (bf16[256,512]{1,0:T(8,128)(2,1)}, bf16[256,512]{1,0:T(8,128)(2,1)}, u32[]{:S(2)}, u32[]{:S(2)}) collective-permute-start(bf16[256,512]{1,0:T(8,128)(2,1)} %get-tuple-element.425.refs_0_), channel_id=1, source_target_pairs={{0,24},{4,28},{8,0},{12,4},{16,8},{20,12},{24,16},{28,20},{1,25},{... | collective-permute-start | bytes 786440 | tf_op jit(solution)/shard_map/ppermute | solution.py:759
  132.2 17.5 %collective-permute-start.18 = (bf16[256,512]{1,0:T(8,128)(2,1)}, bf16[256,512]{1,0:T(8,128)(2,1)S(1)}, u32[]{:S(2)}, u32[]{:S(2)}) collective-permute-start(bf16[256,512]{1,0:T(8,128)(2,1)} %get-tuple-element.425.refs_0_), channel_id=1, source_target_pairs={{0,4},{4,0},{8,12},{12,8},{16,20},{20,16},{24,28},{28,24},{1,5},{5... | collective-permute-start | bytes 786440 | tf_op jit(solution)/shard_map/ppermute | solution.py:759
  152.8 32.7 %collective-permute-start.24 = (bf16[4,2,48,1152]{3,2,1,0:T(8,128)(2,1)S(1)}, bf16[4,2,48,1152]{3,2,1,0:T(8,128)(2,1)}, u32[]{:S(2)}, u32[]{:S(2)}) collective-permute-start(bf16[4,2,48,1152]{3,2,1,0:T(8,128)(2,1)S(1)} %pad_maximum_fusion.4), channel_id=1, source_target_pairs={{0,2},{1,3},{2,0},{3,1},{4,6},{5,7},{6,4},{7,5},{8,10},{9,11},{10,... | collective-permute-start | bytes 2654216 | tf_op jit(solution)/shard_map/ppermute | solution.py:765
  153.4 32.1 %collective-permute-start.25 = (bf16[4,2,48,1152]{3,2,1,0:T(8,128)(2,1)S(1)}, bf16[4,2,48,1152]{3,2,1,0:T(8,128)(2,1)}, u32[]{:S(2)}, u32[]{:S(2)}) collective-permute-start(bf16[4,2,48,1152]{3,2,1,0:T(8,128)(2,1)S(1)} %pad_maximum_fusion.5), channel_id=1, source_target_pairs={{0,1},{1,0},{2,3},{3,2},{4,5},{5,4},{6,7},{7,6},{8,9},{9,8},{10,11... | collective-permute-start | bytes 2654216 | tf_op jit(solution)/shard_map/ppermute | solution.py:765
  154.8 21.6 %collective-permute-start.26 = (bf16[256,1536]{1,0:T(8,128)(2,1)}, bf16[256,1536]{1,0:T(8,128)(2,1)}, u32[]{:S(2)}, u32[]{:S(2)}) collective-permute-start(bf16[256,1536]{1,0:T(8,128)(2,1)} %bitcast.184), channel_id=1, source_target_pairs={{0,8},{4,12},{8,16},{12,20},{16,24},{20,28},{24,0},{28,4},{1,9},{5... | collective-permute-start | bytes 2359304 | tf_op jit(solution)/shard_map/ppermute | solution.py:759
  185.5 19.6 %collective-permute-start.29 = (bf16[256,1536]{1,0:T(8,128)(2,1)}, bf16[256,1536]{1,0:T(8,128)(2,1)}, u32[]{:S(2)}, u32[]{:S(2)}) collective-permute-start(bf16[256,1536]{1,0:T(8,128)(2,1)} %collective-permute-done.26.grad_own), channel_id=1, source_target_pairs={{0,8},{4,12},{8,16},{12,20},{16,24},{20,28},{24,0},{28,4},{1,9},{5... | collective-permute-start | bytes 2359304 | tf_op jit(solution)/shard_map/ppermute | solution.py:759
  187.0 21.0 %collective-permute-start.27 = (bf16[4,2,48,1152]{3,2,1,0:T(8,128)(2,1)}, bf16[4,2,48,1152]{3,2,1,0:T(8,128)(2,1)}, u32[]{:S(2)}, u32[]{:S(2)}) collective-permute-start(bf16[4,2,48,1152]{3,2,1,0:T(8,128)(2,1)} %collective-permute-done.22), channel_id=1, source_target_pairs={{0,2},{1,3},{2,0},{3,1},{4,6},{5,7},{6,4},{7,5},{8,10},{9,11},{10,... | collective-permute-start | bytes 2654216 | tf_op jit(solution)/shard_map/ppermute | solution.py:765
  187.9 20.6 %collective-permute-start.28 = (bf16[4,2,48,1152]{3,2,1,0:T(8,128)(2,1)}, bf16[4,2,48,1152]{3,2,1,0:T(8,128)(2,1)}, u32[]{:S(2)}, u32[]{:S(2)}) collective-permute-start(bf16[4,2,48,1152]{3,2,1,0:T(8,128)(2,1)} %collective-permute-done.23), channel_id=1, source_target_pairs={{0,1},{1,0},{2,3},{3,2},{4,5},{5,4},{6,7},{7,6},{8,9},{9,8},{10,11... | collective-permute-start | bytes 2654216 | tf_op jit(solution)/shard_map/ppermute | solution.py:765
  189.0 16.7 %collective-permute-start.31 = (bf16[256,1536]{1,0:T(8,128)(2,1)}, bf16[256,1536]{1,0:T(8,128)(2,1)}, u32[]{:S(2)}, u32[]{:S(2)}) collective-permute-start(bf16[256,1536]{1,0:T(8,128)(2,1)} %collective-permute-done.26.grad_own), channel_id=1, source_target_pairs={{0,4},{4,0},{8,12},{12,8},{16,20},{20,16},{24,28},{28,24},{1,5},{5... | collective-permute-start | bytes 2359304 | tf_op jit(solution)/shard_map/ppermute | solution.py:759
  189.0 16.7 %collective-permute-start.30 = (bf16[256,1536]{1,0:T(8,128)(2,1)}, bf16[256,1536]{1,0:T(8,128)(2,1)}, u32[]{:S(2)}, u32[]{:S(2)}) collective-permute-start(bf16[256,1536]{1,0:T(8,128)(2,1)} %bitcast.185), channel_id=1, source_target_pairs={{0,4},{4,0},{8,12},{12,8},{16,20},{20,16},{24,28},{28,24},{1,5},{5... | collective-permute-start | bytes 2359304 | tf_op jit(solution)/shard_map/ppermute | solution.py:759
  209.4 35.9 %collective-permute-start.33 = (bf16[256,1536]{1,0:T(8,128)(2,1)}, bf16[256,1536]{1,0:T(8,128)(2,1)}, u32[]{:S(2)}, u32[]{:S(2)}) collective-permute-start(bf16[256,1536]{1,0:T(8,128)(2,1)} %get-tuple-element.448.normed_own), channel_id=1, source_target_pairs={{0,8},{4,12},{8,16},{12,20},{16,24},{20,28},{24,0},{28,4},{1,9},{5... | collective-permute-start | bytes 2359304 | tf_op jit(solution)/shard_map/ppermute | solution.py:759
  212.0 33.9 %collective-permute-start.35 = (bf16[256,1536]{1,0:T(8,128)(2,1)}, bf16[256,1536]{1,0:T(8,128)(2,1)}, u32[]{:S(2)}, u32[]{:S(2)}) collective-permute-start(bf16[256,1536]{1,0:T(8,128)(2,1)} %collective-permute-done.29.grad_own), channel_id=1, source_target_pairs={{0,8},{4,12},{8,16},{12,20},{16,24},{20,28},{24,0},{28,4},{1,9},{5... | collective-permute-start | bytes 2359304 | tf_op jit(solution)/shard_map/ppermute | solution.py:759
  249.0 20.0 %collective-permute-start.38 = (bf16[256,1536]{1,0:T(8,128)(2,1)}, bf16[256,1536]{1,0:T(8,128)(2,1)S(1)}, u32[]{:S(2)}, u32[]{:S(2)}) collective-permute-start(bf16[256,1536]{1,0:T(8,128)(2,1)} %collective-permute-done.33.normed_own), channel_id=1, source_target_pairs={{0,8},{4,12},{8,16},{12,20},{16,24},{20,28},{24,0},{28,4},{1,9},{5... | collective-permute-start | bytes 2359304 | tf_op jit(solution)/shard_map/ppermute | solution.py:759
  273.0 20.4 %collective-permute-start.43 = (bf16[256,1536]{1,0:T(8,128)(2,1)S(1)}, bf16[256,1536]{1,0:T(8,128)(2,1)S(1)}, u32[]{:S(2)}, u32[]{:S(2)}) collective-permute-start(bf16[256,1536]{1,0:T(8,128)(2,1)S(1)} %collective-permute-done.38.normed_own), channel_id=1, source_target_pairs={{0,8},{4,12},{8,16},{12,20},{16,24},{20,28},{24,0},{28,4},{1,9},{5... | collective-permute-start | bytes 2359304 | tf_op jit(solution)/shard_map/ppermute | solution.py:759
  274.1 35.4 %collective-permute-start.42 = (bf16[256,1536]{1,0:T(8,128)(2,1)S(1)}, bf16[256,1536]{1,0:T(8,128)(2,1)S(1)}, u32[]{:S(2)}, u32[]{:S(2)}) collective-permute-start(bf16[256,1536]{1,0:T(8,128)(2,1)S(1)} %add.775), channel_id=1, source_target_pairs={{0,8},{4,12},{8,16},{12,20},{16,24},{20,28},{24,0},{28,4},{1,9},{5... | collective-permute-start | bytes 2359304 | tf_op jit(solution)/shard_map/ppermute | solution.py:759
  292.6 16.9 %collective-permute-start.41 = (bf16[256,1536]{1,0:T(8,128)(2,1)S(1)}, bf16[256,1536]{1,0:T(8,128)(2,1)S(1)}, u32[]{:S(2)}, u32[]{:S(2)}) collective-permute-start(bf16[256,1536]{1,0:T(8,128)(2,1)S(1)} %get-tuple-element.503), channel_id=1, source_target_pairs={{0,4},{4,0},{8,12},{12,8},{16,20},{20,16},{24,28},{28,24},{1,5},{5... | collective-permute-start | bytes 2359304 | tf_op jit(solution)/shard_map/ppermute | solution.py:759
  293.4 16.4 %collective-permute-start.44 = (bf16[256,1536]{1,0:T(8,128)(2,1)S(1)}, bf16[256,1536]{1,0:T(8,128)(2,1)S(1)}, u32[]{:S(2)}, u32[]{:S(2)}) collective-permute-start(bf16[256,1536]{1,0:T(8,128)(2,1)S(1)} %collective-permute-done.43.normed_own), channel_id=1, source_target_pairs={{0,4},{4,0},{8,12},{12,8},{16,20},{20,16},{24,28},{28,24},{1,5},{5... | collective-permute-start | bytes 2359304 | tf_op jit(solution)/shard_map/ppermute | solution.py:759
  293.4 36.9 %collective-permute-start.48 = (bf16[256,1536]{1,0:T(8,128)(2,1)S(1)}, bf16[256,1536]{1,0:T(8,128)(2,1)S(1)}, u32[]{:S(2)}, u32[]{:S(2)}) collective-permute-start(bf16[256,1536]{1,0:T(8,128)(2,1)S(1)} %get-tuple-element.547), channel_id=1, source_target_pairs={{0,4},{4,0},{8,12},{12,8},{16,20},{20,16},{24,28},{28,24},{1,5},{5... | collective-permute-start | bytes 2359304 | tf_op jit(solution)/shard_map/ppermute | solution.py:759
  309.8 23.5 %collective-permute-start.46 = (bf16[256,1536]{1,0:T(8,128)(2,1)S(1)}, bf16[256,1536]{1,0:T(8,128)(2,1)S(1)}, u32[]{:S(2)}, u32[]{:S(2)}) collective-permute-start(bf16[256,1536]{1,0:T(8,128)(2,1)S(1)} %add.776), channel_id=1, source_target_pairs={{0,8},{4,12},{8,16},{12,20},{16,24},{20,28},{24,0},{28,4},{1,9},{5... | collective-permute-start | bytes 2359304 | tf_op jit(solution)/shard_map/ppermute | solution.py:759
  331.5 24.6 %collective-permute-start.50 = (bf16[256,1536]{1,0:T(8,128)(2,1)}, bf16[256,1536]{1,0:T(8,128)(2,1)}, u32[]{:S(2)}, u32[]{:S(2)}) collective-permute-start(bf16[256,1536]{1,0:T(8,128)(2,1)} %add.778), channel_id=1, source_target_pairs={{0,8},{4,12},{8,16},{12,20},{16,24},{20,28},{24,0},{28,4},{1,9},{5... | collective-permute-start | bytes 2359304 | tf_op jit(solution)/shard_map/ppermute | solution.py:759
  333.1 37.9 %collective-permute-start.49 = (bf16[256,1536]{1,0:T(8,128)(2,1)}, bf16[256,1536]{1,0:T(8,128)(2,1)}, u32[]{:S(2)}, u32[]{:S(2)}) collective-permute-start(bf16[256,1536]{1,0:T(8,128)(2,1)} %get-tuple-element.549), channel_id=1, source_target_pairs={{0,4},{4,0},{8,12},{12,8},{16,20},{20,16},{24,28},{28,24},{1,5},{5... | collective-permute-start | bytes 2359304 | tf_op jit(solution)/shard_map/ppermute | solution.py:759
  334.5 38.3 %collective-permute-start.47 = (bf16[256,1536]{1,0:T(8,128)(2,1)}, bf16[256,1536]{1,0:T(8,128)(2,1)}, u32[]{:S(2)}, u32[]{:S(2)}) collective-permute-start(bf16[256,1536]{1,0:T(8,128)(2,1)} %add.777), channel_id=1, source_target_pairs={{0,8},{4,12},{8,16},{12,20},{16,24},{20,28},{24,0},{28,4},{1,9},{5... | collective-permute-start | bytes 2359304 | tf_op jit(solution)/shard_map/ppermute | solution.py:759
  372.8 30.5 %collective-permute-start.51 = (bf16[8,48,1152]{2,1,0:T(8,128)(2,1)S(1)}, bf16[8,48,1152]{2,1,0:T(8,128)(2,1)S(1)}, u32[]{:S(2)}, u32[]{:S(2)}) collective-permute-start(bf16[8,48,1152]{2,1,0:T(8,128)(2,1)S(1)} %bitcast.223), channel_id=1, source_target_pairs={{0,1},{1,0},{2,3},{3,2},{4,5},{5,4},{6,7},{7,6},{8,9},{9,8},{10,11... | collective-permute-start | bytes 2654216 | tf_op jit(solution)/shard_map/ppermute | solution.py:765
  374.0 29.3 %collective-permute-start.52 = (bf16[8,48,1152]{2,1,0:T(8,128)(2,1)S(1)}, bf16[8,48,1152]{2,1,0:T(8,128)(2,1)S(1)}, u32[]{:S(2)}, u32[]{:S(2)}) collective-permute-start(bf16[8,48,1152]{2,1,0:T(8,128)(2,1)S(1)} %bitcast.222), channel_id=1, source_target_pairs={{0,2},{1,3},{2,0},{3,1},{4,6},{5,7},{6,4},{7,5},{8,10},{9,11},{10,... | collective-permute-start | bytes 2654216 | tf_op jit(solution)/shard_map/ppermute | solution.py:765
  375.6 27.6 %collective-permute-start.54 = (bf16[256,1536]{1,0:T(8,128)(2,1)S(1)}, bf16[256,1536]{1,0:T(8,128)(2,1)S(1)}, u32[]{:S(2)}, u32[]{:S(2)}) collective-permute-start(bf16[256,1536]{1,0:T(8,128)(2,1)S(1)} %add.779), channel_id=1, source_target_pairs={{0,8},{4,12},{8,16},{12,20},{16,24},{20,28},{24,0},{28,4},{1,9},{5... | collective-permute-start | bytes 2359304 | tf_op jit(solution)/shard_map/ppermute | solution.py:759
  376.5 26.7 %collective-permute-start.55 = (bf16[256,1536]{1,0:T(8,128)(2,1)}, bf16[256,1536]{1,0:T(8,128)(2,1)S(1)}, u32[]{:S(2)}, u32[]{:S(2)}) collective-permute-start(bf16[256,1536]{1,0:T(8,128)(2,1)} %get-tuple-element.568), channel_id=1, source_target_pairs={{0,4},{4,0},{8,12},{12,8},{16,20},{20,16},{24,28},{28,24},{1,5},{5... | collective-permute-start | bytes 2359304 | tf_op jit(solution)/shard_map/ppermute | solution.py:759
  407.0 27.7 %collective-permute-start.60 = (bf16[8,48,1152]{2,1,0:T(8,128)(2,1)}, bf16[8,48,1152]{2,1,0:T(8,128)(2,1)}, u32[]{:S(2)}, u32[]{:S(2)}) collective-permute-start(bf16[8,48,1152]{2,1,0:T(8,128)(2,1)} %bitcast.73), channel_id=1, source_target_pairs={{0,1},{1,0},{2,3},{3,2},{4,5},{5,4},{6,7},{7,6},{8,9},{9,8},{10,11... | collective-permute-start | bytes 2654216 | tf_op jit(solution)/shard_map/ppermute | solution.py:765
  407.6 27.2 %collective-permute-start.61 = (bf16[8,48,1152]{2,1,0:T(8,128)(2,1)}, bf16[8,48,1152]{2,1,0:T(8,128)(2,1)}, u32[]{:S(2)}, u32[]{:S(2)}) collective-permute-start(bf16[8,48,1152]{2,1,0:T(8,128)(2,1)} %bitcast.75), channel_id=1, source_target_pairs={{0,2},{1,3},{2,0},{3,1},{4,6},{5,7},{6,4},{7,5},{8,10},{9,11},{10,... | collective-permute-start | bytes 2654216 | tf_op jit(solution)/shard_map/ppermute | solution.py:765
  408.5 26.2 %collective-permute-start.57 = (bf16[256,512]{1,0:T(8,128)(2,1)}, bf16[256,512]{1,0:T(8,128)(2,1)}, u32[]{:S(2)}, u32[]{:S(2)}) collective-permute-start(bf16[256,512]{1,0:T(8,128)(2,1)} %get-tuple-element.588), channel_id=1, source_target_pairs={{0,24},{4,28},{8,0},{12,4},{16,8},{20,12},{24,16},{28,20},{1,25},{... | collective-permute-start | bytes 786440 | tf_op jit(solution)/shard_map/ppermute | solution.py:759
  408.7 26.1 %collective-permute-start.58 = (bf16[256,512]{1,0:T(8,128)(2,1)}, bf16[256,512]{1,0:T(8,128)(2,1)}, u32[]{:S(2)}, u32[]{:S(2)}) collective-permute-start(bf16[256,512]{1,0:T(8,128)(2,1)} %get-tuple-element.589), channel_id=1, source_target_pairs={{0,16},{4,20},{8,24},{12,28},{16,0},{20,4},{24,8},{28,12},{1,17},{... | collective-permute-start | bytes 786440 | tf_op jit(solution)/shard_map/ppermute | solution.py:759
  410.8 24.0 %collective-permute-start.59 = (bf16[256,512]{1,0:T(8,128)(2,1)}, bf16[256,512]{1,0:T(8,128)(2,1)}, u32[]{:S(2)}, u32[]{:S(2)}) collective-permute-start(bf16[256,512]{1,0:T(8,128)(2,1)} %get-tuple-element.590), channel_id=1, source_target_pairs={{0,8},{4,12},{8,16},{12,20},{16,24},{20,28},{24,0},{28,4},{1,9},{5... | collective-permute-start | bytes 786440 | tf_op jit(solution)/shard_map/ppermute | solution.py:759
  434.8 30.1 %collective-permute-start.64 = (bf16[16,48,1536]{2,1,0:T(8,128)(2,1)}, bf16[16,48,1536]{2,1,0:T(8,128)(2,1)}, u32[]{:S(2)}, u32[]{:S(2)}) collective-permute-start(bf16[16,48,1536]{2,1,0:T(8,128)(2,1)} %bitcast.84), channel_id=1, source_target_pairs={{0,4},{4,0},{8,12},{12,8},{16,20},{20,16},{24,28},{28,24},{1,5},{5... | collective-permute-start | bytes 7077896 | tf_op jit(solution)/shard_map/ppermute | solution.py:759
  434.9 30.0 %collective-permute-start.65 = (bf16[16,48,1536]{2,1,0:T(8,128)(2,1)}, bf16[16,48,1536]{2,1,0:T(8,128)(2,1)}, u32[]{:S(2)}, u32[]{:S(2)}) collective-permute-start(bf16[16,48,1536]{2,1,0:T(8,128)(2,1)} %bitcast.88), channel_id=1, source_target_pairs={{0,4},{4,0},{8,12},{12,8},{16,20},{20,16},{24,28},{28,24},{1,5},{5... | collective-permute-start | bytes 7077896 | tf_op jit(solution)/shard_map/ppermute | solution.py:759
  438.7 25.3 %collective-permute-start.62 = (bf16[8,48,1152]{2,1,0:T(8,128)(2,1)}, bf16[8,48,1152]{2,1,0:T(8,128)(2,1)}, u32[]{:S(2)}, u32[]{:S(2)}) collective-permute-start(bf16[8,48,1152]{2,1,0:T(8,128)(2,1)} %bitcast.91), channel_id=1, source_target_pairs={{0,2},{1,3},{2,0},{3,1},{4,6},{5,7},{6,4},{7,5},{8,10},{9,11},{10,... | collective-permute-start | bytes 2654216 | tf_op jit(solution)/shard_map/ppermute | solution.py:765
  443.2 21.7 %collective-permute-start.63 = (bf16[8,48,1152]{2,1,0:T(8,128)(2,1)}, bf16[8,48,1152]{2,1,0:T(8,128)(2,1)}, u32[]{:S(2)}, u32[]{:S(2)}) collective-permute-start(bf16[8,48,1152]{2,1,0:T(8,128)(2,1)} %bitcast.97), channel_id=1, source_target_pairs={{0,1},{1,0},{2,3},{3,2},{4,5},{5,4},{6,7},{7,6},{8,9},{9,8},{10,11... | collective-permute-start | bytes 2654216 | tf_op jit(solution)/shard_map/ppermute | solution.py:765
  444.7 19.3 %collective-permute-start.66 = (bf16[256,1536]{1,0:T(8,128)(2,1)}, bf16[256,1536]{1,0:T(8,128)(2,1)}, u32[]{:S(2)}, u32[]{:S(2)}) collective-permute-start(bf16[256,1536]{1,0:T(8,128)(2,1)} %add.780), channel_id=1, source_target_pairs={{0,8},{4,12},{8,16},{12,20},{16,24},{20,28},{24,0},{28,4},{1,9},{5... | collective-permute-start | bytes 2359304 | tf_op jit(solution)/shard_map/ppermute | solution.py:759
  467.6 21.2 %collective-permute-start.70 = (bf16[2,288,768]{2,1,0:T(8,128)(2,1)S(1)}, bf16[2,288,768]{2,1,0:T(8,128)(2,1)S(1)}, u32[]{:S(2)}, u32[]{:S(2)}) collective-permute-start(bf16[2,288,768]{2,1,0:T(8,128)(2,1)S(1)} %copy-done.70), channel_id=1, source_target_pairs={{0,1},{1,0},{2,3},{3,2},{4,5},{5,4},{6,7},{7,6},{8,9},{9,8},{10,11... | collective-permute-start | bytes 2654216 | tf_op jit(solution)/shard_map/ppermute | solution.py:765
  469.1 20.9 %collective-permute-start.71 = (bf16[2,288,768]{2,1,0:T(8,128)(2,1)S(1)}, bf16[2,288,768]{2,1,0:T(8,128)(2,1)S(1)}, u32[]{:S(2)}, u32[]{:S(2)}) collective-permute-start(bf16[2,288,768]{2,1,0:T(8,128)(2,1)S(1)} %copy-done.68), channel_id=1, source_target_pairs={{0,2},{1,3},{2,0},{3,1},{4,6},{5,7},{6,4},{7,5},{8,10},{9,11},{10,... | collective-permute-start | bytes 2654216 | tf_op jit(solution)/shard_map/ppermute | solution.py:765
  490.1 32.7 %collective-permute-start.74 = (bf16[8,48,1920]{2,1,0:T(8,128)(2,1)S(1)}, bf16[8,48,1920]{2,1,0:T(8,128)(2,1)S(1)}, u32[]{:S(2)}, u32[]{:S(2)}) collective-permute-start(bf16[8,48,1920]{2,1,0:T(8,128)(2,1)S(1)} %bitcast.220), channel_id=1, source_target_pairs={{0,1},{1,0},{2,3},{3,2},{4,5},{5,4},{6,7},{7,6},{8,9},{9,8},{10,11... | collective-permute-start | bytes 4423688 | tf_op jit(solution)/shard_map/ppermute | solution.py:765
  490.6 30.4 %collective-permute-start.75 = (bf16[8,48,1792]{2,1,0:T(8,128)(2,1)S(1)}, bf16[8,48,1792]{2,1,0:T(8,128)(2,1)S(1)}, u32[]{:S(2)}, u32[]{:S(2)}) collective-permute-start(bf16[8,48,1792]{2,1,0:T(8,128)(2,1)S(1)} %bitcast.221), channel_id=1, source_target_pairs={{0,2},{1,3},{2,0},{3,1},{4,6},{5,7},{6,4},{7,5},{8,10},{9,11},{10,... | collective-permute-start | bytes 4128776 | tf_op jit(solution)/shard_map/ppermute | solution.py:765
  491.5 13.2 %collective-permute-start.72 = (bf16[2,2,48,1152]{3,2,1,0:T(8,128)(2,1)S(1)}, bf16[2,2,48,1152]{3,2,1,0:T(8,128)(2,1)S(1)}, u32[]{:S(2)}, u32[]{:S(2)}) collective-permute-start(bf16[2,2,48,1152]{3,2,1,0:T(8,128)(2,1)S(1)} %copy-done.84), channel_id=1, source_target_pairs={{0,8},{4,12},{8,16},{12,20},{16,24},{20,28},{24,0},{28,4},{1,9},{5... | collective-permute-start | bytes 1327112 | tf_op jit(solution)/shard_map/ppermute | solution.py:759
  492.0 29.0 %collective-permute-start.73 = (bf16[2,2,48,1152]{3,2,1,0:T(8,128)(2,1)S(1)}, bf16[2,2,48,1152]{3,2,1,0:T(8,128)(2,1)S(1)}, u32[]{:S(2)}, u32[]{:S(2)}) collective-permute-start(bf16[2,2,48,1152]{3,2,1,0:T(8,128)(2,1)S(1)} %copy-done.82), channel_id=1, source_target_pairs={{0,16},{4,20},{8,24},{12,28},{16,0},{20,4},{24,8},{28,12},{1,17},{... | collective-permute-start | bytes 1327112 | tf_op jit(solution)/shard_map/ppermute | solution.py:759
  523.1 16.8 %collective-permute-start.78 = (bf16[4,48,1920]{2,1,0:T(8,128)(2,1)S(1)}, bf16[4,48,1920]{2,1,0:T(8,128)(2,1)S(1)}, u32[]{:S(2)}, u32[]{:S(2)}) collective-permute-start(bf16[4,48,1920]{2,1,0:T(8,128)(2,1)S(1)} %bitcast.224), channel_id=1, source_target_pairs={{0,2},{1,3},{2,0},{3,1},{4,6},{5,7},{6,4},{7,5},{8,10},{9,11},{10,... | collective-permute-start | bytes 2211848 | tf_op jit(solution)/shard_map/ppermute | solution.py:765
  524.0 15.7 %collective-permute-start.79 = (bf16[4,48,1792]{2,1,0:T(8,128)(2,1)S(1)}, bf16[4,48,1792]{2,1,0:T(8,128)(2,1)S(1)}, u32[]{:S(2)}, u32[]{:S(2)}) collective-permute-start(bf16[4,48,1792]{2,1,0:T(8,128)(2,1)S(1)} %bitcast.225), channel_id=1, source_target_pairs={{0,1},{1,0},{2,3},{3,2},{4,5},{5,4},{6,7},{7,6},{8,9},{9,8},{10,11... | collective-permute-start | bytes 2064392 | tf_op jit(solution)/shard_map/ppermute | solution.py:765
  525.0 15.1 %collective-permute-start.77 = (bf16[2,2,48,1152]{3,2,1,0:T(8,128)(2,1)S(1)}, bf16[2,2,48,1152]{3,2,1,0:T(8,128)(2,1)S(1)}, u32[]{:S(2)}, u32[]{:S(2)}) collective-permute-start(bf16[2,2,48,1152]{3,2,1,0:T(8,128)(2,1)S(1)} %copy-done.80), channel_id=1, source_target_pairs={{0,24},{4,28},{8,0},{12,4},{16,8},{20,12},{24,16},{28,20},{1,25},{... | collective-permute-start | bytes 1327112 | tf_op jit(solution)/shard_map/ppermute | solution.py:759
  540.1 26.9 %collective-permute-start.80 = (bf16[48,3712]{1,0:T(8,128)(2,1)S(1)}, bf16[48,3712]{1,0:T(8,128)(2,1)S(1)}, u32[]{:S(2)}, u32[]{:S(2)}) collective-permute-start(bf16[48,3712]{1,0:T(8,128)(2,1)S(1)} %pad_maximum_fusion.8), channel_id=1, source_target_pairs={{0,8},{4,12},{8,16},{12,20},{16,24},{20,28},{24,0},{28,4},{1,9},{5... | collective-permute-start | bytes 1069064 | tf_op jit(solution)/shard_map/ppermute | solution.py:759
  543.2 29.1 %collective-permute-start.81 = (bf16[48,3712]{1,0:T(8,128)(2,1)S(1)}, bf16[48,3712]{1,0:T(8,128)(2,1)S(1)}, u32[]{:S(2)}, u32[]{:S(2)}) collective-permute-start(bf16[48,3712]{1,0:T(8,128)(2,1)S(1)} %pad_maximum_fusion.9), channel_id=1, source_target_pairs={{0,16},{4,20},{8,24},{12,28},{16,0},{20,4},{24,8},{28,12},{1,17},{... | collective-permute-start | bytes 1069064 | tf_op jit(solution)/shard_map/ppermute | solution.py:759
  547.5 28.7 %collective-permute-start.82 = (bf16[48,3712]{1,0:T(8,128)(2,1)S(1)}, bf16[48,3712]{1,0:T(8,128)(2,1)S(1)}, u32[]{:S(2)}, u32[]{:S(2)}) collective-permute-start(bf16[48,3712]{1,0:T(8,128)(2,1)S(1)} %pad_maximum_fusion.10), channel_id=1, source_target_pairs={{0,24},{4,28},{8,0},{12,4},{16,8},{20,12},{24,16},{28,20},{1,25},{... | collective-permute-start | bytes 1069064 | tf_op jit(solution)/shard_map/ppermute | solution.py:759
  (128 other events, 1135.6 us)
Sparse Core Ops, SparseCore 0:
  11.5 92.7 all-gather.2
  106.7 70.6 all-gather.4
where the time goes:
time: 594 us; the launch traced here: 587 us
  Pallas kernels  213 us (36%)
  waiting for transfers between devices  203 us (34%)
  starting transfers between devices  81.3 us (14%)
  local copies, waits for them, and re-layouts  54.3 us (9%)
  other arithmetic  19.8 us (3%)
  between operations  15.5 us (3%)
    pallas_call x44, Pallas kernels, kernel_call(): pl.pallas_call(kernel, name=name, out_shape=out_shape, compiler_params=pl...  213 us
    ppermute x61, waiting for transfers between devices, seq_perm(): lax.ppermute(values, 'seq', [(i, (i + 2 * chips) % count ^ flip) for i in...  151 us
    ppermute x61, starting transfers between devices, seq_perm(): lax.ppermute(values, 'seq', [(i, (i + 2 * chips) % count ^ flip) for i in...  54.4 us
    ppermute x24, waiting for transfers between devices, dp_perm(): lax.ppermute(values, 'dp', [(i, i ^ bit) for i in range(lax.axis_size('dp...  51.7 us
    unnamed x215, local copies, waits for them, and re-layouts  47.9 us
    ppermute x24, starting transfers between devices, dp_perm(): lax.ppermute(values, 'dp', [(i, i ^ bit) for i in range(lax.axis_size('dp...  26.9 us
  transfers between devices with their start and end apart: 87, of which 42 were waited for; matrix products, arithmetic and copies ran while one was open for 3% of the time, Pallas kernels for 36%

commit v1 on v0

--- a/solution.py
+++ b/solution.py
@@ -485,14 +485,16 @@
         "weight_grad",
         tuple(out_shape),
         (sides, left, *rights, *bases),
-        megabytes=44,
+        megabytes=32,
         grid=(steps,),
         in_specs=[
             smem,
             pl.BlockSpec((n_slots, tokens, block), lambda i: (slots[0], 0, i + first)),
         ]
         + [
-            pl.BlockSpec(
+            vmem
+            if slots == (0, 1)
+            else pl.BlockSpec(
                 (n_slots, tokens, right.shape[-1]),
                 lambda i: (slots[0], 0, 0),
                 pipeline_mode=whole,
@@ -851,7 +853,9 @@
     def exchange(shift):
         return seq_perm(to_send[shift], shift, 0)
 
-    w_out = lax.all_gather(out_master.astype(bf16), ("seq", "dp"), axis=0, tiled=True)
+    w_out = lax.all_gather(
+        after(out_master.astype(bf16), *to_send), ("seq", "dp"), axis=0, tiled=True
+    )
 
     columns = ((0, HD + half), (HD + half, HD + qkv_width))
     orders = (bits, bits[::-1])

time: 594 us -> 580 us (0.976)
  Pallas kernels: 213 us -> 202 us
  local copies, waits for them, and re-layouts: 54.3 us -> 62.1 us
  starting transfers between devices: 81.3 us -> 74.7 us
    pallas_call x44, Pallas kernels: 213 us -> 202 us  [kernel_call(): pl.pallas_call(kernel, name=name, out_shape=out_shape, compiler_params=pl...]
    ppermute x61, waiting for transfers between devices: 151 us -> 141 us  [seq_perm(): lax.ppermute(values, 'seq', [(i, (i + 2 * chips) % count ^ flip) for i in...]
    unnamed x215 -> x233, local copies, waits for them, and re-layouts: 47.9 us -> 55.7 us
    ppermute x24, waiting for transfers between devices: 51.7 us -> 58.6 us  [dp_perm(): lax.ppermute(values, 'dp', [(i, i ^ bit) for i in range(lax.axis_size('dp...]
  transfers between devices with their start and end apart: 87 -> 87, of which waited for: 42 -> 42; matrix products, arithmetic and copies ran while one was open for 3% -> 4% of each run, Pallas kernels for 36% -> 35%
where the time goes in v1:
time: 580 us; the launch traced here: 573 us
  Pallas kernels  202 us (35%)
  waiting for transfers between devices  199 us (34%)
  starting transfers between devices  74.7 us (13%)
  local copies, waits for them, and re-layouts  62.1 us (11%)
  other arithmetic  18.8 us (3%)
  between operations  15.7 us (3%)
    pallas_call x44, Pallas kernels, kernel_call(): pl.pallas_call(kernel, name=name, out_shape=out_shape, compiler_params=pl...  202 us
    ppermute x61, waiting for transfers between devices, seq_perm(): lax.ppermute(values, 'seq', [(i, (i + 2 * chips) % count ^ flip) for i in...  141 us
    ppermute x24, waiting for transfers between devices, dp_perm(): lax.ppermute(values, 'dp', [(i, i ^ bit) for i in range(lax.axis_size('dp...  58.6 us
    unnamed x233, local copies, waits for them, and re-layouts  55.7 us
    ppermute x61, starting transfers between devices, seq_perm(): lax.ppermute(values, 'seq', [(i, (i + 2 * chips) % count ^ flip) for i in...  49.1 us
    ppermute x24, starting transfers between devices, dp_perm(): lax.ppermute(values, 'dp', [(i, i ^ bit) for i in range(lax.axis_size('dp...  25.5 us
  transfers between devices with their start and end apart: 87, of which 42 were waited for; matrix products, arithmetic and copies ran while one was open for 4% of the time, Pallas kernels for 35%

profile of v1, /device:TPU:8, one launch (start us, length us, event | category | flops | bytes accessed | tf_op | source)
XLA Modules:
  0.0 572.9 jit_solution(15313128001656653455)
XLA Ops:
  7.3 2.0 copy-done.9
  13.9 1.9 collective-permute-start.2
  20.2 6.8 %collective-permute-done.refs_1_ = bf16[48,2176]{1,0:T(8,128)(2,1)S(1)} collective-permute-done((bf16[48,2176]{1,0:T(8,128)(2,1)S(1)}, bf16[48,2176]{1,0:T(8,128)(2,1)S(1)}, u32[]{:S(2)}, u32[]{:S(2)}) %collective-permute-start) | collective-permute-done | bytes 208928 | tf_op jit(solution)/shard_map/ppermute | solution.py:761
  27.1 4.2 collective-permute-done.1.refs_2_
  36.3 10.3 %collective-permute-done.5 = bf16[4,48,1024]{2,1,0:T(8,128)(2,1)S(1)} collective-permute-done((bf16[4,48,1024]{2,1,0:T(8,128)(2,1)S(1)}, bf16[4,48,1024]{2,1,0:T(8,128)(2,1)S(1)}, u32[]{:S(2)}, u32[]{:S(2)}) %collective-permute-start.5) | collective-permute-done | bytes 393248 | tf_op jit(solution)/shard_map/ppermute | solution.py:767
  51.3 10.2 %collective-permute-done.9 = bf16[2,2,48,1152]{3,2,1,0:T(8,128)(2,1)S(1)} collective-permute-done((bf16[2,2,48,1152]{3,2,1,0:T(8,128)(2,1)S(1)}, bf16[2,2,48,1152]{3,2,1,0:T(8,128)(2,1)S(1)}, u32[]{:S(2)}, u32[]{:S(2)}) %collective-permute-start.9) | collective-permute-done | bytes 442400 | tf_op jit(solution)/shard_map/ppermute | solution.py:761
  61.5 6.3 %collective-permute-done.8.refs_5_ = bf16[8,48,1024]{2,1,0:T(8,128)(2,1)} collective-permute-done((bf16[8,48,1024]{2,1,0:T(8,128)(2,1)S(1)}, bf16[8,48,1024]{2,1,0:T(8,128)(2,1)}, u32[]{:S(2)}, u32[]{:S(2)}) %collective-permute-start.8) | collective-permute-done | bytes 786464 | tf_op jit(solution)/shard_map/ppermute | solution.py:767
  74.0 18.9 %collective-permute-done.14 = bf16[2,2,48,1152]{3,2,1,0:T(8,128)(2,1)} collective-permute-done((bf16[2,2,48,1152]{3,2,1,0:T(8,128)(2,1)}, bf16[2,2,48,1152]{3,2,1,0:T(8,128)(2,1)}, u32[]{:S(2)}, u32[]{:S(2)}) %collective-permute-start.14) | collective-permute-done | bytes 442400 | tf_op jit(solution)/shard_map/ppermute | solution.py:761
  94.2 4.1 assemble.2
  98.4 2.6 copy-done.7
  102.4 3.2 project_kv.1
  110.1 4.2 collective-permute-start.16
  114.4 5.1 collective-permute-done.15.refs_2_
  119.4 5.1 project_q.1.q_ref
  124.5 8.2 %collective-permute-done.16.refs_4_ = bf16[256,512]{1,0:T(8,128)(2,1)S(1)} collective-permute-done((bf16[256,512]{1,0:T(8,128)(2,1)}, bf16[256,512]{1,0:T(8,128)(2,1)S(1)}, u32[]{:S(2)}, u32[]{:S(2)}) %collective-permute-start.16) | collective-permute-done | bytes 262176 | tf_op jit(solution)/shard_map/ppermute | solution.py:761
  132.7 3.5 collective-permute-done.17.refs_6_
  147.3 11.5 %attend.1 = (f32[256,1536]{1,0:T(8,128)S(1)}, f32[12,256]{1,0:T(8,128)S(1)}, bf16[2048,512]{1,0:T(8,128)(2,1)S(1)}) custom-call(s32[2]{0:T(128)S(1)} %slice_bitcast_fusion.1.query_bases, s32[16]{0:T(128)S(1)} %select_n.83.key_bases, bf16[256,1536]{1,0:T(8,128)(2,1)S(1)} %copy-done.13, bf16[256,512]{1,0:T(8,128)(2,1)S(1)} %copy-done.64, ...), custom_call_target="tpu_custom_call" | custom-call | flops 1000000 | bytes 1000000 | tf_op jit(solution)/shard_map/attend/pallas_call | solution.py:38
  161.3 14.7 %collective-permute-done.24 = bf16[4,2,48,1152]{3,2,1,0:T(8,128)(2,1)} collective-permute-done((bf16[4,2,48,1152]{3,2,1,0:T(8,128)(2,1)S(1)}, bf16[4,2,48,1152]{3,2,1,0:T(8,128)(2,1)}, u32[]{:S(2)}, u32[]{:S(2)}) %collective-permute-start.24) | collective-permute-done | bytes 884768 | tf_op jit(solution)/shard_map/ppermute | solution.py:767
  180.0 2.3 copy-done.8
  183.8 2.4 out_project.1
  187.1 7.1 %collective-permute-done.29.grad_own = bf16[256,1536]{1,0:T(8,128)(2,1)} collective-permute-done((bf16[256,1536]{1,0:T(8,128)(2,1)}, bf16[256,1536]{1,0:T(8,128)(2,1)}, u32[]{:S(2)}, u32[]{:S(2)}) %collective-permute-start.29) | collective-permute-done | bytes 786464 | tf_op jit(solution)/shard_map/ppermute | solution.py:761
  194.9 4.6 collective-permute-done.27
  204.7 5.5 assemble.3
  210.2 2.9 copy-done
  213.1 2.0 copy-done.6
  216.3 17.2 %feed_forward.4 = (bf16[256,1536]{1,0:T(8,128)(2,1)S(1)}, bf16[256,1536]{1,0:T(8,128)(2,1)S(1)}, bf16[256,1536]{1,0:T(8,128)(2,1)S(1)}, bf16[256,1536]{1,0:T(8,1...) custom-call(bf16[256,1536]{1,0:T(8,128)(2,1)} %get-tuple-element.450, ...), custom_call_target="tpu_custom_call" | custom-call | flops 1000000 | bytes 1000000 | tf_op jit(solution)/shard_map/feed_forward/pallas_call | solution.py:38
  236.6 2.0 collective-permute-done.36.grad_other
  240.8 17.3 %feed_forward.5 = (bf16[256,1536]{1,0:T(8,128)(2,1)S(1)}, bf16[256,1536]{1,0:T(8,128)(2,1)S(1)}, bf16[256,1536]{1,0:T(8,128)(2,1)S(1)}, bf16[256,1536]{1,0:T(8,1...) custom-call(bf16[256,1536]{1,0:T(8,128)(2,1)} %collective-permute-do, ...), custom_call_target="tpu_custom_call", output_to_operand_aliasing={{4}: (6, {}), {5}: (7, {}), {6}: (8, {}), {7}: (9, {}), {8}... | custom-call | flops 1000000 | bytes 1000000 | tf_op jit(solution)/shard_map/feed_forward/pallas_call | solution.py:38
  262.7 2.7 collective-permute-start.43
  265.8 16.9 %feed_forward.6 = (bf16[256,1536]{1,0:T(8,128)(2,1)S(1)}, bf16[256,1536]{1,0:T(8,128)(2,1)}, bf16[256,1536]{1,0:T(8,128)(2,1)S(1)}, bf16[256,1536]{1,0:T(8,128)(...) custom-call(bf16[256,1536]{1,0:T(8,128)(2,1)S(1)} %collective-permut, ...), custom_call_target="tpu_custom_call", output_to_operand_aliasing={{4}: (6, {}), {5}: (7, {}), {6}: (8, {}), {7}: (9, {}), {8}... | custom-call | flops 1000000 | bytes 1000000 | tf_op jit(solution)/shard_map/feed_forward/pallas_call | solution.py:38
  283.8 15.6 %collective-permute-done.42.refs_2_ = bf16[256,1536]{1,0:T(8,128)(2,1)S(1)} collective-permute-done((bf16[256,1536]{1,0:T(8,128)(2,1)S(1)}, bf16[256,1536]{1,0:T(8,128)(2,1)S(1)}, u32[]{:S(2)}, u32[]{:S(2)}) %collective-permute-start.42) | collective-permute-done | bytes 786464 | tf_op jit(solution)/shard_map/ppermute | solution.py:761
  299.8 2.9 collective-permute-start.46
  302.7 16.8 %feed_forward.7 = (bf16[256,1536]{1,0:T(8,128)(2,1)S(1)}, bf16[256,1536]{1,0:T(8,128)(2,1)}, bf16[256,1536]{1,0:T(8,128)(2,1)S(1)}, bf16[256,1536]{1,0:T(8,128)(...) custom-call(bf16[256,1536]{1,0:T(8,128)(2,1)S(1)} %collective-permut, ...), custom_call_target="tpu_custom_call", output_to_operand_aliasing={{4}: (6, {}), {5}: (7, {}), {6}: (8, {}), {7}: (9, {}), {8}... | custom-call | flops 1000000 | bytes 1000000 | tf_op jit(solution)/shard_map/feed_forward/pallas_call | solution.py:38
  319.6 2.2 copy-done.5
  325.2 3.3 collective-permute-start.47
  328.6 2.8 copy-done.1
  331.3 2.3 copy-done.3
  333.7 2.3 copy-done.4
  336.0 12.4 %weight_grad.6 = (bf16[8,1,48,1152]{3,2,1,0:T(8,128)(2,1)S(1)}, bf16[8,1,48,1152]{3,2,1,0:T(8,128)(2,1)}, bf16[4,2,48,1152]{3,2,1,0:T(8,128)(2,1)S(1)}, bf16[4,2,48,1152]{3,2,1,0:T(8,128)(2,1)}) custom-call(s32[2]{0:T(128)S(1)} %pad_add_fusion.8.sides, bf16[4,512,1536]{2,1,0:T(8,128)(2,1)S(1)} %copy-done.1, bf16[4,512,1152]{2,1,0:T(8,128)(2,1)S(1)} %copy-done.3, ...), custom_call_target="tpu_custom_call" | custom-call | flops 1000000 | bytes 1000000 | tf_op jit(solution)/shard_map/weight_grad/pallas_call | solution.py:38
  348.5 11.6 %weight_grad.7 = (bf16[8,1,48,1152]{3,2,1,0:T(8,128)(2,1)S(1)}, bf16[8,1,48,1152]{3,2,1,0:T(8,128)(2,1)S(1)}, bf16[4,2,48,1152]{3,2,1,0:T(8,128)(2,1)S(1)}, bf16[4,2,48,1152]{3,2,1,0:T(8,128)(2,1)S(1)}) custom-call(s32[2]{0:T(128)S(1)} %pad_add_fusion.8.sides, bf16[4,512,1536]{2,1,0:T(8,128)(2,1)S(1)} %copy-done.1, bf16[4,512,1152]{2,1,0:T(8,128)(2,1)S(1)} %copy-done.3, ...), custom_call_target="tpu_custom_call" | custom-call | flops 1000000 | bytes 1000000 | tf_op jit(solution)/shard_map/weight_grad/pallas_call | solution.py:38
  367.4 3.5 norm_back.1
  371.9 21.0 %attend_back.1 = (bf16[256,1536]{1,0:T(8,128)(2,1)S(1)}, bf16[1024,512]{1,0:T(8,128)(2,1)S(1)}, bf16[1024,512]{1,0:T(8,128)(2,1)S(1)}) custom-call(s32[2]{0:T(128)S(1)} %copy-done.70, s32[16]{0:T(128)S(1)} %select_n.83.key_bases, bf16[256,1536]{1,0:T(8,128)(2,1)S(1)} %copy-done.14, bf16[2048,512]{1,0:T(8,128)(2,1)S(1)} %copy-done.33, ...), custom_call_target="tpu_custom_call" | custom-call | flops 1000000 | bytes 1000000 | tf_op jit(solution)/shard_map/attend_back/pallas_call | solution.py:38
  393.2 2.5 collective-permute-done.56
  404.6 3.9 weight_grad.8
  410.0 3.6 weight_grad.9
  415.0 8.4 %weight_grad.10 = bf16[1152,1536]{1,0:T(8,128)(2,1)S(1)} custom-call(s32[1]{0:T(128)} %constant.163.clone.1.chip.sides, bf16[4,512,1152]{2,1,0:T(8,128)(2,1)S(1)} %bitcast.168, bf16[4,512,1536]{2,1,0:T(8,128)(2,1)S(1)} %bitcast.166), custom_call_target="tpu_custom_call" | custom-call | flops 1000000 | bytes 1000000 | tf_op jit(solution)/shard_map/weight_grad/pallas_call | solution.py:38
  436.9 7.6 %input_back.1 = (bf16[256,512]{1,0:T(8,128)(2,1)}, f32[256,1536]{1,0:T(8,128)}, f32[1,1536]{1,0:T(1,128)}, f32[1,2048]{1,0:T(1,128)}) custom-call(bf16[256,1536]{1,0:T(8,128)(2,1)} %bitcast.178, f32[1,1536]{1,0:T(1,128)} %get-tuple-element.771.gain, bf16[1536,2048]{1,0:T(8,128)(2,1)} %bitcast.171, bf16[256,1536]{1,0:T(8,128)(2,1)} %copy-done.27, ...), custom_call_target="tpu_custom_call" | custom-call | flops 1000000 | bytes 1000000 | tf_op jit(solution)/shard_map/input_back/pallas_call | solution.py:38
  446.9 3.1 collective-permute-done.66
  462.8 2.5 add_halve.14
  465.4 2.4 add_halve.15
  467.8 7.7 %collective-permute-done.70 = bf16[2,288,768]{2,1,0:T(8,128)(2,1)S(1)} collective-permute-done((bf16[2,288,768]{2,1,0:T(8,128)(2,1)S(1)}, bf16[2,288,768]{2,1,0:T(8,128)(2,1)S(1)}, u32[]{:S(2)}, u32[]{:S(2)}) %collective-permute-start.70) | collective-permute-done | bytes 884768 | tf_op jit(solution)/shard_map/ppermute | solution.py:767
  477.9 1.8 collective-permute-start.72
  479.8 1.9 collective-permute-start.73
  482.1 17.5 %collective-permute-done.72.refs_1_ = bf16[2,2,48,1152]{3,2,1,0:T(8,128)(2,1)S(1)} collective-permute-done((bf16[2,2,48,1152]{3,2,1,0:T(8,128)(2,1)S(1)}, bf16[2,2,48,1152]{3,2,1,0:T(8,128)(2,1)S(1)}, u32[]{:S(2)}, u32[]{:S(2)}) %collective-permute-start.72) | collective-permute-done | bytes 442400 | tf_op jit(solution)/shard_map/ppermute | solution.py:761
  499.6 9.2 %collective-permute-done.73.refs_2_ = bf16[2,2,48,1152]{3,2,1,0:T(8,128)(2,1)S(1)} collective-permute-done((bf16[2,2,48,1152]{3,2,1,0:T(8,128)(2,1)S(1)}, bf16[2,2,48,1152]{3,2,1,0:T(8,128)(2,1)S(1)}, u32[]{:S(2)}, u32[]{:S(2)}) %collective-permute-start.73) | collective-permute-done | bytes 442400 | tf_op jit(solution)/shard_map/ppermute | solution.py:761
  511.9 3.5 collective-permute-start.77
  515.4 2.6 fusion.1
  518.0 9.7 %collective-permute-done.79.got = bf16[4,48,1792]{2,1,0:T(8,128)(2,1)S(1)} collective-permute-done((bf16[4,48,1792]{2,1,0:T(8,128)(2,1)S(1)}, bf16[4,48,1792]{2,1,0:T(8,128)(2,1)S(1)}, u32[]{:S(2)}, u32[]{:S(2)}) %collective-permute-start.79) | collective-permute-done | bytes 688160 | tf_op jit(solution)/shard_map/ppermute | solution.py:767
  529.7 4.4 collective-permute-start.81
  535.9 7.6 %adamw_hidden.1 = (f32[2,48,8960]{2,1,0:T(8,128)}, f32[2,48,8960]{2,1,0:T(8,128)}, f32[2,48,8960]{2,1,0:T(8,128)}) custom-call(s32[8]{0:T(128)S(1)} %stack.261.where, f32[2,48,8960]{2,1,0:T(8,128)S(1)} %copy-done.10, f32[2,48,8960]{2,1,0:T(8,128)S(1)} %copy-done.23, f32[2,48,8960]{2,1,0:T(8,128)} %second.1, ...), custom_call_target="tpu_custom_call" | custom-call | flops 1000000 | bytes 1000000 | tf_op jit(solution)/shard_map/adamw_hidden/pallas_call | solution.py:38
  545.4 3.2 multiply_subtract_fusion
  548.7 5.0 collective-permute-done.80
  553.7 5.0 collective-permute-done.81
  558.7 4.1 collective-permute-done.82
  (477 shorter events, 137.2 us)
Async XLA Ops:
  7.2 172.9 %all-gather.3.cloned.1.call-start = ((), (), s32[]{:S(2)}) async-start(), calls=%async_computation | async-start | bytes 4866048 | tf_op jit(solution)/shard_map/all_gather | solution.py:856
  11.1 15.9 %collective-permute-start = (bf16[48,2176]{1,0:T(8,128)(2,1)S(1)}, bf16[48,2176]{1,0:T(8,128)(2,1)S(1)}, u32[]{:S(2)}, u32[]{:S(2)}) collective-permute-start(bf16[48,2176]{1,0:T(8,128)(2,1)S(1)} %pad_maximum_fusion.11.refs_0_), channel_id=1, source_target_pairs={{0,8},{4,12},{8,16},{12,20},{16,24},{20,28},{24,0},{28,4},{1,9},{5... | collective-permute-start | bytes 626696 | tf_op jit(solution)/shard_map/ppermute | solution.py:761
  12.8 18.5 %collective-permute-start.1 = (bf16[48,2176]{1,0:T(8,128)(2,1)S(1)}, bf16[48,2176]{1,0:T(8,128)(2,1)S(1)}, u32[]{:S(2)}, u32[]{:S(2)}) collective-permute-start(bf16[48,2176]{1,0:T(8,128)(2,1)S(1)} %pad_maximum_fusion.11.refs_0_), channel_id=1, source_target_pairs={{0,16},{4,20},{8,24},{12,28},{16,0},{20,4},{24,8},{28,12},{1,17},{... | collective-permute-start | bytes 626696 | tf_op jit(solution)/shard_map/ppermute | solution.py:761
  13.9 19.2 %collective-permute-start.2 = (bf16[48,2176]{1,0:T(8,128)(2,1)S(1)}, bf16[48,2176]{1,0:T(8,128)(2,1)S(1)}, u32[]{:S(2)}, u32[]{:S(2)}) collective-permute-start(bf16[48,2176]{1,0:T(8,128)(2,1)S(1)} %pad_maximum_fusion.11.refs_0_), channel_id=1, source_target_pairs={{0,24},{4,28},{8,0},{12,4},{16,8},{20,12},{24,16},{28,20},{1,25},{... | collective-permute-start | bytes 626696 | tf_op jit(solution)/shard_map/ppermute | solution.py:761
  33.1 180.0 %all-gather.5.cloned.1.call-start = ((), (), s32[]{:S(2)}) async-start(), calls=%async_computation.1 | async-start | bytes 4423680 | tf_op jit(solution)/shard_map/all_gather | solution.py:880
  33.3 13.4 %collective-permute-start.4 = (bf16[4,48,1152]{2,1,0:T(8,128)(2,1)S(1)}, bf16[4,48,1152]{2,1,0:T(8,128)(2,1)S(1)}, u32[]{:S(2)}, u32[]{:S(2)}) collective-permute-start(bf16[4,48,1152]{2,1,0:T(8,128)(2,1)S(1)} %get-tuple-element.390), channel_id=1, source_target_pairs={{0,1},{1,0},{2,3},{3,2},{4,5},{5,4},{6,7},{7,6},{8,9},{9,8},{10,11... | collective-permute-start | bytes 1327112 | tf_op jit(solution)/shard_map/ppermute | solution.py:767
  47.9 20.6 %collective-permute-start.7 = (bf16[8,48,1152]{2,1,0:T(8,128)(2,1)S(1)}, bf16[8,48,1152]{2,1,0:T(8,128)(2,1)}, u32[]{:S(2)}, u32[]{:S(2)}) collective-permute-start(bf16[8,48,1152]{2,1,0:T(8,128)(2,1)S(1)} %constant_dynamic-update-slice_fusion.refs_0_), channel_id=1, source_target_pairs={{0,2},{1,3},{2,0},{3,1},{4,6},{5,7},{6,4},{7,5},{8,10},{9,11},{10,... | collective-permute-start | bytes 2654216 | tf_op jit(solution)/shard_map/ppermute | solution.py:767
  49.6 18.2 %collective-permute-start.8 = (bf16[8,48,1024]{2,1,0:T(8,128)(2,1)S(1)}, bf16[8,48,1024]{2,1,0:T(8,128)(2,1)}, u32[]{:S(2)}, u32[]{:S(2)}) collective-permute-start(bf16[8,48,1024]{2,1,0:T(8,128)(2,1)S(1)} %constant_dynamic-update-slice_fusion.2.refs_4_), channel_id=1, source_target_pairs={{0,1},{1,0},{2,3},{3,2},{4,5},{5,4},{6,7},{7,6},{8,9},{9,8},{10,11... | collective-permute-start | bytes 2359304 | tf_op jit(solution)/shard_map/ppermute | solution.py:767
  50.8 23.2 %collective-permute-start.10 = (bf16[8,48,1152]{2,1,0:T(8,128)(2,1)S(1)}, bf16[8,48,1152]{2,1,0:T(8,128)(2,1)}, u32[]{:S(2)}, u32[]{:S(2)}) collective-permute-start(bf16[8,48,1152]{2,1,0:T(8,128)(2,1)S(1)} %constant_dynamic-update-slice_fusion.refs_0_), channel_id=1, source_target_pairs={{0,4},{4,0},{8,12},{12,8},{16,20},{20,16},{24,28},{28,24},{1,5},{5... | collective-permute-start | bytes 2654216 | tf_op jit(solution)/shard_map/ppermute | solution.py:761
  50.8 22.3 %collective-permute-start.11 = (bf16[8,48,1024]{2,1,0:T(8,128)(2,1)S(1)}, bf16[8,48,1024]{2,1,0:T(8,128)(2,1)S(1)}, u32[]{:S(2)}, u32[]{:S(2)}) collective-permute-start(bf16[8,48,1024]{2,1,0:T(8,128)(2,1)S(1)} %constant_dynamic-update-slice_fusion.2.refs_4_), channel_id=1, source_target_pairs={{0,4},{4,0},{8,12},{12,8},{16,20},{20,16},{24,28},{28,24},{1,5},{5... | collective-permute-start | bytes 2359304 | tf_op jit(solution)/shard_map/ppermute | solution.py:761
  68.5 25.7 %collective-permute-start.12 = (bf16[8,48,1152]{2,1,0:T(8,128)(2,1)}, bf16[8,48,1152]{2,1,0:T(8,128)(2,1)}, u32[]{:S(2)}, u32[]{:S(2)}) collective-permute-start(bf16[8,48,1152]{2,1,0:T(8,128)(2,1)} %collective-permute-done.7.refs_1_), channel_id=1, source_target_pairs={{0,4},{4,0},{8,12},{12,8},{16,20},{20,16},{24,28},{28,24},{1,5},{5... | collective-permute-start | bytes 2654216 | tf_op jit(solution)/shard_map/ppermute | solution.py:761
  68.5 25.6 %collective-permute-start.13 = (bf16[8,48,1024]{2,1,0:T(8,128)(2,1)}, bf16[8,48,1024]{2,1,0:T(8,128)(2,1)}, u32[]{:S(2)}, u32[]{:S(2)}) collective-permute-start(bf16[8,48,1024]{2,1,0:T(8,128)(2,1)} %collective-permute-done.8.refs_5_), channel_id=1, source_target_pairs={{0,4},{4,0},{8,12},{12,8},{16,20},{20,16},{24,28},{28,24},{1,5},{5... | collective-permute-start | bytes 2359304 | tf_op jit(solution)/shard_map/ppermute | solution.py:761
  69.0 23.9 %collective-permute-start.14 = (bf16[2,2,48,1152]{3,2,1,0:T(8,128)(2,1)}, bf16[2,2,48,1152]{3,2,1,0:T(8,128)(2,1)}, u32[]{:S(2)}, u32[]{:S(2)}) collective-permute-start(bf16[2,2,48,1152]{3,2,1,0:T(8,128)(2,1)} %get-tuple-element.411), channel_id=1, source_target_pairs={{0,16},{4,20},{8,24},{12,28},{16,0},{20,4},{24,8},{28,12},{1,17},{... | collective-permute-start | bytes 1327112 | tf_op jit(solution)/shard_map/ppermute | solution.py:761
  105.6 34.0 %collective-permute-start.22 = (bf16[4,2,48,1152]{3,2,1,0:T(8,128)(2,1)S(1)}, bf16[4,2,48,1152]{3,2,1,0:T(8,128)(2,1)}, u32[]{:S(2)}, u32[]{:S(2)}) collective-permute-start(bf16[4,2,48,1152]{3,2,1,0:T(8,128)(2,1)S(1)} %pad_maximum_fusion.4), channel_id=1, source_target_pairs={{0,1},{1,0},{2,3},{3,2},{4,5},{5,4},{6,7},{7,6},{8,9},{9,8},{10,11... | collective-permute-start | bytes 2654216 | tf_op jit(solution)/shard_map/ppermute | solution.py:767
  107.1 32.5 %collective-permute-start.23 = (bf16[4,2,48,1152]{3,2,1,0:T(8,128)(2,1)S(1)}, bf16[4,2,48,1152]{3,2,1,0:T(8,128)(2,1)}, u32[]{:S(2)}, u32[]{:S(2)}) collective-permute-start(bf16[4,2,48,1152]{3,2,1,0:T(8,128)(2,1)S(1)} %pad_maximum_fusion.5), channel_id=1, source_target_pairs={{0,2},{1,3},{2,0},{3,1},{4,6},{5,7},{6,4},{7,5},{8,10},{9,11},{10,... | collective-permute-start | bytes 2654216 | tf_op jit(solution)/shard_map/ppermute | solution.py:767
  110.1 22.5 %collective-permute-start.16 = (bf16[256,512]{1,0:T(8,128)(2,1)}, bf16[256,512]{1,0:T(8,128)(2,1)S(1)}, u32[]{:S(2)}, u32[]{:S(2)}) collective-permute-start(bf16[256,512]{1,0:T(8,128)(2,1)} %get-tuple-element.426.refs_0_), channel_id=1, source_target_pairs={{0,16},{4,20},{8,24},{12,28},{16,0},{20,4},{24,8},{28,12},{1,17},{... | collective-permute-start | bytes 786440 | tf_op jit(solution)/shard_map/ppermute | solution.py:761
  114.4 21.8 %collective-permute-start.17 = (bf16[256,512]{1,0:T(8,128)(2,1)}, bf16[256,512]{1,0:T(8,128)(2,1)}, u32[]{:S(2)}, u32[]{:S(2)}) collective-permute-start(bf16[256,512]{1,0:T(8,128)(2,1)} %get-tuple-element.426.refs_0_), channel_id=1, source_target_pairs={{0,24},{4,28},{8,0},{12,4},{16,8},{20,12},{24,16},{28,20},{1,25},{... | collective-permute-start | bytes 786440 | tf_op jit(solution)/shard_map/ppermute | solution.py:761
  119.4 17.5 %collective-permute-start.18 = (bf16[256,512]{1,0:T(8,128)(2,1)}, bf16[256,512]{1,0:T(8,128)(2,1)S(1)}, u32[]{:S(2)}, u32[]{:S(2)}) collective-permute-start(bf16[256,512]{1,0:T(8,128)(2,1)} %get-tuple-element.426.refs_0_), channel_id=1, source_target_pairs={{0,4},{4,0},{8,12},{12,8},{16,20},{20,16},{24,28},{28,24},{1,5},{5... | collective-permute-start | bytes 786440 | tf_op jit(solution)/shard_map/ppermute | solution.py:761
  139.6 36.4 %collective-permute-start.24 = (bf16[4,2,48,1152]{3,2,1,0:T(8,128)(2,1)S(1)}, bf16[4,2,48,1152]{3,2,1,0:T(8,128)(2,1)}, u32[]{:S(2)}, u32[]{:S(2)}) collective-permute-start(bf16[4,2,48,1152]{3,2,1,0:T(8,128)(2,1)S(1)} %pad_maximum_fusion.4), channel_id=1, source_target_pairs={{0,2},{1,3},{2,0},{3,1},{4,6},{5,7},{6,4},{7,5},{8,10},{9,11},{10,... | collective-permute-start | bytes 2654216 | tf_op jit(solution)/shard_map/ppermute | solution.py:767
  140.3 36.7 %collective-permute-start.25 = (bf16[4,2,48,1152]{3,2,1,0:T(8,128)(2,1)S(1)}, bf16[4,2,48,1152]{3,2,1,0:T(8,128)(2,1)}, u32[]{:S(2)}, u32[]{:S(2)}) collective-permute-start(bf16[4,2,48,1152]{3,2,1,0:T(8,128)(2,1)S(1)} %pad_maximum_fusion.5), channel_id=1, source_target_pairs={{0,1},{1,0},{2,3},{3,2},{4,5},{5,4},{6,7},{7,6},{8,9},{9,8},{10,11... | collective-permute-start | bytes 2654216 | tf_op jit(solution)/shard_map/ppermute | solution.py:767
  140.8 20.5 %collective-permute-start.26 = (bf16[256,1536]{1,0:T(8,128)(2,1)}, bf16[256,1536]{1,0:T(8,128)(2,1)}, u32[]{:S(2)}, u32[]{:S(2)}) collective-permute-start(bf16[256,1536]{1,0:T(8,128)(2,1)} %bitcast.186), channel_id=1, source_target_pairs={{0,8},{4,12},{8,16},{12,20},{16,24},{20,28},{24,0},{28,4},{1,9},{5... | collective-permute-start | bytes 2359304 | tf_op jit(solution)/shard_map/ppermute | solution.py:761
  177.0 17.3 %collective-permute-start.29 = (bf16[256,1536]{1,0:T(8,128)(2,1)}, bf16[256,1536]{1,0:T(8,128)(2,1)}, u32[]{:S(2)}, u32[]{:S(2)}) collective-permute-start(bf16[256,1536]{1,0:T(8,128)(2,1)} %collective-permute-done.26.grad_own), channel_id=1, source_target_pairs={{0,8},{4,12},{8,16},{12,20},{16,24},{20,28},{24,0},{28,4},{1,9},{5... | collective-permute-start | bytes 2359304 | tf_op jit(solution)/shard_map/ppermute | solution.py:761
  177.0 22.6 %collective-permute-start.27 = (bf16[4,2,48,1152]{3,2,1,0:T(8,128)(2,1)}, bf16[4,2,48,1152]{3,2,1,0:T(8,128)(2,1)}, u32[]{:S(2)}, u32[]{:S(2)}) collective-permute-start(bf16[4,2,48,1152]{3,2,1,0:T(8,128)(2,1)} %collective-permute-done.22), channel_id=1, source_target_pairs={{0,2},{1,3},{2,0},{3,1},{4,6},{5,7},{6,4},{7,5},{8,10},{9,11},{10,... | collective-permute-start | bytes 2654216 | tf_op jit(solution)/shard_map/ppermute | solution.py:767
  178.4 21.5 %collective-permute-start.28 = (bf16[4,2,48,1152]{3,2,1,0:T(8,128)(2,1)}, bf16[4,2,48,1152]{3,2,1,0:T(8,128)(2,1)}, u32[]{:S(2)}, u32[]{:S(2)}) collective-permute-start(bf16[4,2,48,1152]{3,2,1,0:T(8,128)(2,1)} %collective-permute-done.23), channel_id=1, source_target_pairs={{0,1},{1,0},{2,3},{3,2},{4,5},{5,4},{6,7},{7,6},{8,9},{9,8},{10,11... | collective-permute-start | bytes 2654216 | tf_op jit(solution)/shard_map/ppermute | solution.py:767
  179.5 15.4 %collective-permute-start.31 = (bf16[256,1536]{1,0:T(8,128)(2,1)}, bf16[256,1536]{1,0:T(8,128)(2,1)}, u32[]{:S(2)}, u32[]{:S(2)}) collective-permute-start(bf16[256,1536]{1,0:T(8,128)(2,1)} %collective-permute-done.26.grad_own), channel_id=1, source_target_pairs={{0,4},{4,0},{8,12},{12,8},{16,20},{20,16},{24,28},{28,24},{1,5},{5... | collective-permute-start | bytes 2359304 | tf_op jit(solution)/shard_map/ppermute | solution.py:761
  179.5 15.4 %collective-permute-start.30 = (bf16[256,1536]{1,0:T(8,128)(2,1)}, bf16[256,1536]{1,0:T(8,128)(2,1)}, u32[]{:S(2)}, u32[]{:S(2)}) collective-permute-start(bf16[256,1536]{1,0:T(8,128)(2,1)} %bitcast.187), channel_id=1, source_target_pairs={{0,4},{4,0},{8,12},{12,8},{16,20},{20,16},{24,28},{28,24},{1,5},{5... | collective-permute-start | bytes 2359304 | tf_op jit(solution)/shard_map/ppermute | solution.py:761
  200.8 35.3 %collective-permute-start.33 = (bf16[256,1536]{1,0:T(8,128)(2,1)}, bf16[256,1536]{1,0:T(8,128)(2,1)}, u32[]{:S(2)}, u32[]{:S(2)}) collective-permute-start(bf16[256,1536]{1,0:T(8,128)(2,1)} %get-tuple-element.450.normed_own), channel_id=1, source_target_pairs={{0,8},{4,12},{8,16},{12,20},{16,24},{20,28},{24,0},{28,4},{1,9},{5... | collective-permute-start | bytes 2359304 | tf_op jit(solution)/shard_map/ppermute | solution.py:761
  201.9 34.8 %collective-permute-start.35 = (bf16[256,1536]{1,0:T(8,128)(2,1)}, bf16[256,1536]{1,0:T(8,128)(2,1)}, u32[]{:S(2)}, u32[]{:S(2)}) collective-permute-start(bf16[256,1536]{1,0:T(8,128)(2,1)} %collective-permute-done.29.grad_own), channel_id=1, source_target_pairs={{0,8},{4,12},{8,16},{12,20},{16,24},{20,28},{24,0},{28,4},{1,9},{5... | collective-permute-start | bytes 2359304 | tf_op jit(solution)/shard_map/ppermute | solution.py:761
  239.7 19.9 %collective-permute-start.38 = (bf16[256,1536]{1,0:T(8,128)(2,1)}, bf16[256,1536]{1,0:T(8,128)(2,1)S(1)}, u32[]{:S(2)}, u32[]{:S(2)}) collective-permute-start(bf16[256,1536]{1,0:T(8,128)(2,1)} %collective-permute-done.33.normed_own), channel_id=1, source_target_pairs={{0,8},{4,12},{8,16},{12,20},{16,24},{20,28},{24,0},{28,4},{1,9},{5... | collective-permute-start | bytes 2359304 | tf_op jit(solution)/shard_map/ppermute | solution.py:761
  262.7 20.6 %collective-permute-start.43 = (bf16[256,1536]{1,0:T(8,128)(2,1)S(1)}, bf16[256,1536]{1,0:T(8,128)(2,1)S(1)}, u32[]{:S(2)}, u32[]{:S(2)}) collective-permute-start(bf16[256,1536]{1,0:T(8,128)(2,1)S(1)} %collective-permute-done.38.normed_own), channel_id=1, source_target_pairs={{0,8},{4,12},{8,16},{12,20},{16,24},{20,28},{24,0},{28,4},{1,9},{5... | collective-permute-start | bytes 2359304 | tf_op jit(solution)/shard_map/ppermute | solution.py:761
  265.4 34.1 %collective-permute-start.42 = (bf16[256,1536]{1,0:T(8,128)(2,1)S(1)}, bf16[256,1536]{1,0:T(8,128)(2,1)S(1)}, u32[]{:S(2)}, u32[]{:S(2)}) collective-permute-start(bf16[256,1536]{1,0:T(8,128)(2,1)S(1)} %add.775), channel_id=1, source_target_pairs={{0,8},{4,12},{8,16},{12,20},{16,24},{20,28},{24,0},{28,4},{1,9},{5... | collective-permute-start | bytes 2359304 | tf_op jit(solution)/shard_map/ppermute | solution.py:761
  282.7 16.7 %collective-permute-start.41 = (bf16[256,1536]{1,0:T(8,128)(2,1)S(1)}, bf16[256,1536]{1,0:T(8,128)(2,1)S(1)}, u32[]{:S(2)}, u32[]{:S(2)}) collective-permute-start(bf16[256,1536]{1,0:T(8,128)(2,1)S(1)} %get-tuple-element.505), channel_id=1, source_target_pairs={{0,4},{4,0},{8,12},{12,8},{16,20},{20,16},{24,28},{28,24},{1,5},{5... | collective-permute-start | bytes 2359304 | tf_op jit(solution)/shard_map/ppermute | solution.py:761
  283.3 16.5 %collective-permute-start.44 = (bf16[256,1536]{1,0:T(8,128)(2,1)S(1)}, bf16[256,1536]{1,0:T(8,128)(2,1)S(1)}, u32[]{:S(2)}, u32[]{:S(2)}) collective-permute-start(bf16[256,1536]{1,0:T(8,128)(2,1)S(1)} %collective-permute-done.43.normed_own), channel_id=1, source_target_pairs={{0,4},{4,0},{8,12},{12,8},{16,20},{20,16},{24,28},{28,24},{1,5},{5... | collective-permute-start | bytes 2359304 | tf_op jit(solution)/shard_map/ppermute | solution.py:761
  283.3 38.4 %collective-permute-start.48 = (bf16[256,1536]{1,0:T(8,128)(2,1)S(1)}, bf16[256,1536]{1,0:T(8,128)(2,1)S(1)}, u32[]{:S(2)}, u32[]{:S(2)}) collective-permute-start(bf16[256,1536]{1,0:T(8,128)(2,1)S(1)} %get-tuple-element.549), channel_id=1, source_target_pairs={{0,4},{4,0},{8,12},{12,8},{16,20},{20,16},{24,28},{28,24},{1,5},{5... | collective-permute-start | bytes 2359304 | tf_op jit(solution)/shard_map/ppermute | solution.py:761
  299.8 23.9 %collective-permute-start.46 = (bf16[256,1536]{1,0:T(8,128)(2,1)S(1)}, bf16[256,1536]{1,0:T(8,128)(2,1)S(1)}, u32[]{:S(2)}, u32[]{:S(2)}) collective-permute-start(bf16[256,1536]{1,0:T(8,128)(2,1)S(1)} %add.776), channel_id=1, source_target_pairs={{0,8},{4,12},{8,16},{12,20},{16,24},{20,28},{24,0},{28,4},{1,9},{5... | collective-permute-start | bytes 2359304 | tf_op jit(solution)/shard_map/ppermute | solution.py:761
  323.0 25.5 %collective-permute-start.50 = (bf16[256,1536]{1,0:T(8,128)(2,1)}, bf16[256,1536]{1,0:T(8,128)(2,1)}, u32[]{:S(2)}, u32[]{:S(2)}) collective-permute-start(bf16[256,1536]{1,0:T(8,128)(2,1)} %add.778), channel_id=1, source_target_pairs={{0,8},{4,12},{8,16},{12,20},{16,24},{20,28},{24,0},{28,4},{1,9},{5... | collective-permute-start | bytes 2359304 | tf_op jit(solution)/shard_map/ppermute | solution.py:761
  323.3 36.8 %collective-permute-start.49 = (bf16[256,1536]{1,0:T(8,128)(2,1)}, bf16[256,1536]{1,0:T(8,128)(2,1)}, u32[]{:S(2)}, u32[]{:S(2)}) collective-permute-start(bf16[256,1536]{1,0:T(8,128)(2,1)} %get-tuple-element.551), channel_id=1, source_target_pairs={{0,4},{4,0},{8,12},{12,8},{16,20},{20,16},{24,28},{28,24},{1,5},{5... | collective-permute-start | bytes 2359304 | tf_op jit(solution)/shard_map/ppermute | solution.py:761
  325.2 37.4 %collective-permute-start.47 = (bf16[256,1536]{1,0:T(8,128)(2,1)}, bf16[256,1536]{1,0:T(8,128)(2,1)}, u32[]{:S(2)}, u32[]{:S(2)}) collective-permute-start(bf16[256,1536]{1,0:T(8,128)(2,1)} %add.777), channel_id=1, source_target_pairs={{0,8},{4,12},{8,16},{12,20},{16,24},{20,28},{24,0},{28,4},{1,9},{5... | collective-permute-start | bytes 2359304 | tf_op jit(solution)/shard_map/ppermute | solution.py:761
  362.6 30.3 %collective-permute-start.51 = (bf16[8,48,1152]{2,1,0:T(8,128)(2,1)}, bf16[8,48,1152]{2,1,0:T(8,128)(2,1)S(1)}, u32[]{:S(2)}, u32[]{:S(2)}) collective-permute-start(bf16[8,48,1152]{2,1,0:T(8,128)(2,1)} %bitcast.69), channel_id=1, source_target_pairs={{0,1},{1,0},{2,3},{3,2},{4,5},{5,4},{6,7},{7,6},{8,9},{9,8},{10,11... | collective-permute-start | bytes 2654216 | tf_op jit(solution)/shard_map/ppermute | solution.py:767
  363.3 29.6 %collective-permute-start.52 = (bf16[8,48,1152]{2,1,0:T(8,128)(2,1)}, bf16[8,48,1152]{2,1,0:T(8,128)(2,1)S(1)}, u32[]{:S(2)}, u32[]{:S(2)}) collective-permute-start(bf16[8,48,1152]{2,1,0:T(8,128)(2,1)} %bitcast.71), channel_id=1, source_target_pairs={{0,2},{1,3},{2,0},{3,1},{4,6},{5,7},{6,4},{7,5},{8,10},{9,11},{10,... | collective-permute-start | bytes 2654216 | tf_op jit(solution)/shard_map/ppermute | solution.py:767
  365.1 27.8 %collective-permute-start.54 = (bf16[256,1536]{1,0:T(8,128)(2,1)S(1)}, bf16[256,1536]{1,0:T(8,128)(2,1)S(1)}, u32[]{:S(2)}, u32[]{:S(2)}) collective-permute-start(bf16[256,1536]{1,0:T(8,128)(2,1)S(1)} %add.779), channel_id=1, source_target_pairs={{0,8},{4,12},{8,16},{12,20},{16,24},{20,28},{24,0},{28,4},{1,9},{5... | collective-permute-start | bytes 2359304 | tf_op jit(solution)/shard_map/ppermute | solution.py:761
  366.0 26.9 %collective-permute-start.55 = (bf16[256,1536]{1,0:T(8,128)(2,1)}, bf16[256,1536]{1,0:T(8,128)(2,1)S(1)}, u32[]{:S(2)}, u32[]{:S(2)}) collective-permute-start(bf16[256,1536]{1,0:T(8,128)(2,1)} %get-tuple-element.570), channel_id=1, source_target_pairs={{0,4},{4,0},{8,12},{12,8},{16,20},{20,16},{24,28},{28,24},{1,5},{5... | collective-permute-start | bytes 2359304 | tf_op jit(solution)/shard_map/ppermute | solution.py:761
  396.6 26.8 %collective-permute-start.60 = (bf16[8,48,1152]{2,1,0:T(8,128)(2,1)}, bf16[8,48,1152]{2,1,0:T(8,128)(2,1)S(1)}, u32[]{:S(2)}, u32[]{:S(2)}) collective-permute-start(bf16[8,48,1152]{2,1,0:T(8,128)(2,1)} %bitcast.227), channel_id=1, source_target_pairs={{0,1},{1,0},{2,3},{3,2},{4,5},{5,4},{6,7},{7,6},{8,9},{9,8},{10,11... | collective-permute-start | bytes 2654216 | tf_op jit(solution)/shard_map/ppermute | solution.py:767
  397.9 25.6 %collective-permute-start.61 = (bf16[8,48,1152]{2,1,0:T(8,128)(2,1)}, bf16[8,48,1152]{2,1,0:T(8,128)(2,1)S(1)}, u32[]{:S(2)}, u32[]{:S(2)}) collective-permute-start(bf16[8,48,1152]{2,1,0:T(8,128)(2,1)} %bitcast.226), channel_id=1, source_target_pairs={{0,2},{1,3},{2,0},{3,1},{4,6},{5,7},{6,4},{7,5},{8,10},{9,11},{10,... | collective-permute-start | bytes 2654216 | tf_op jit(solution)/shard_map/ppermute | solution.py:767
  398.5 25.0 %collective-permute-start.57 = (bf16[256,512]{1,0:T(8,128)(2,1)S(1)}, bf16[256,512]{1,0:T(8,128)(2,1)S(1)}, u32[]{:S(2)}, u32[]{:S(2)}) collective-permute-start(bf16[256,512]{1,0:T(8,128)(2,1)S(1)} %get-tuple-element.590), channel_id=1, source_target_pairs={{0,24},{4,28},{8,0},{12,4},{16,8},{20,12},{24,16},{28,20},{1,25},{... | collective-permute-start | bytes 786440 | tf_op jit(solution)/shard_map/ppermute | solution.py:761
  399.0 24.4 %collective-permute-start.58 = (bf16[256,512]{1,0:T(8,128)(2,1)S(1)}, bf16[256,512]{1,0:T(8,128)(2,1)S(1)}, u32[]{:S(2)}, u32[]{:S(2)}) collective-permute-start(bf16[256,512]{1,0:T(8,128)(2,1)S(1)} %get-tuple-element.591), channel_id=1, source_target_pairs={{0,16},{4,20},{8,24},{12,28},{16,0},{20,4},{24,8},{28,12},{1,17},{... | collective-permute-start | bytes 786440 | tf_op jit(solution)/shard_map/ppermute | solution.py:761
  400.8 22.7 %collective-permute-start.59 = (bf16[256,512]{1,0:T(8,128)(2,1)S(1)}, bf16[256,512]{1,0:T(8,128)(2,1)S(1)}, u32[]{:S(2)}, u32[]{:S(2)}) collective-permute-start(bf16[256,512]{1,0:T(8,128)(2,1)S(1)} %get-tuple-element.592), channel_id=1, source_target_pairs={{0,8},{4,12},{8,16},{12,20},{16,24},{20,28},{24,0},{28,4},{1,9},{5... | collective-permute-start | bytes 786440 | tf_op jit(solution)/shard_map/ppermute | solution.py:761
  423.5 28.0 %collective-permute-start.64 = (bf16[16,48,1536]{2,1,0:T(8,128)(2,1)}, bf16[16,48,1536]{2,1,0:T(8,128)(2,1)}, u32[]{:S(2)}, u32[]{:S(2)}) collective-permute-start(bf16[16,48,1536]{2,1,0:T(8,128)(2,1)} %bitcast.84), channel_id=1, source_target_pairs={{0,4},{4,0},{8,12},{12,8},{16,20},{20,16},{24,28},{28,24},{1,5},{5... | collective-permute-start | bytes 7077896 | tf_op jit(solution)/shard_map/ppermute | solution.py:761
  423.6 28.0 %collective-permute-start.65 = (bf16[16,48,1536]{2,1,0:T(8,128)(2,1)}, bf16[16,48,1536]{2,1,0:T(8,128)(2,1)}, u32[]{:S(2)}, u32[]{:S(2)}) collective-permute-start(bf16[16,48,1536]{2,1,0:T(8,128)(2,1)} %bitcast.88), channel_id=1, source_target_pairs={{0,4},{4,0},{8,12},{12,8},{16,20},{20,16},{24,28},{28,24},{1,5},{5... | collective-permute-start | bytes 7077896 | tf_op jit(solution)/shard_map/ppermute | solution.py:761
  426.3 23.8 %collective-permute-start.62 = (bf16[8,48,1152]{2,1,0:T(8,128)(2,1)}, bf16[8,48,1152]{2,1,0:T(8,128)(2,1)}, u32[]{:S(2)}, u32[]{:S(2)}) collective-permute-start(bf16[8,48,1152]{2,1,0:T(8,128)(2,1)} %bitcast.91), channel_id=1, source_target_pairs={{0,2},{1,3},{2,0},{3,1},{4,6},{5,7},{6,4},{7,5},{8,10},{9,11},{10,... | collective-permute-start | bytes 2654216 | tf_op jit(solution)/shard_map/ppermute | solution.py:767
  429.9 21.7 %collective-permute-start.63 = (bf16[8,48,1152]{2,1,0:T(8,128)(2,1)}, bf16[8,48,1152]{2,1,0:T(8,128)(2,1)}, u32[]{:S(2)}, u32[]{:S(2)}) collective-permute-start(bf16[8,48,1152]{2,1,0:T(8,128)(2,1)} %bitcast.97), channel_id=1, source_target_pairs={{0,1},{1,0},{2,3},{3,2},{4,5},{5,4},{6,7},{7,6},{8,9},{9,8},{10,11... | collective-permute-start | bytes 2654216 | tf_op jit(solution)/shard_map/ppermute | solution.py:767
  430.7 19.3 %collective-permute-start.66 = (bf16[256,1536]{1,0:T(8,128)(2,1)}, bf16[256,1536]{1,0:T(8,128)(2,1)}, u32[]{:S(2)}, u32[]{:S(2)}) collective-permute-start(bf16[256,1536]{1,0:T(8,128)(2,1)} %add.780), channel_id=1, source_target_pairs={{0,8},{4,12},{8,16},{12,20},{16,24},{20,28},{24,0},{28,4},{1,9},{5... | collective-permute-start | bytes 2359304 | tf_op jit(solution)/shard_map/ppermute | solution.py:761
  454.3 21.2 %collective-permute-start.70 = (bf16[2,288,768]{2,1,0:T(8,128)(2,1)S(1)}, bf16[2,288,768]{2,1,0:T(8,128)(2,1)S(1)}, u32[]{:S(2)}, u32[]{:S(2)}) collective-permute-start(bf16[2,288,768]{2,1,0:T(8,128)(2,1)S(1)} %copy-done.76), channel_id=1, source_target_pairs={{0,1},{1,0},{2,3},{3,2},{4,5},{5,4},{6,7},{7,6},{8,9},{9,8},{10,11... | collective-permute-start | bytes 2654216 | tf_op jit(solution)/shard_map/ppermute | solution.py:767
  455.2 20.9 %collective-permute-start.71 = (bf16[2,288,768]{2,1,0:T(8,128)(2,1)S(1)}, bf16[2,288,768]{2,1,0:T(8,128)(2,1)S(1)}, u32[]{:S(2)}, u32[]{:S(2)}) collective-permute-start(bf16[2,288,768]{2,1,0:T(8,128)(2,1)S(1)} %copy-done.73), channel_id=1, source_target_pairs={{0,2},{1,3},{2,0},{3,1},{4,6},{5,7},{6,4},{7,5},{8,10},{9,11},{10,... | collective-permute-start | bytes 2654216 | tf_op jit(solution)/shard_map/ppermute | solution.py:767
  476.2 32.7 %collective-permute-start.74 = (bf16[8,48,1920]{2,1,0:T(8,128)(2,1)S(1)}, bf16[8,48,1920]{2,1,0:T(8,128)(2,1)S(1)}, u32[]{:S(2)}, u32[]{:S(2)}) collective-permute-start(bf16[8,48,1920]{2,1,0:T(8,128)(2,1)S(1)} %bitcast.224), channel_id=1, source_target_pairs={{0,1},{1,0},{2,3},{3,2},{4,5},{5,4},{6,7},{7,6},{8,9},{9,8},{10,11... | collective-permute-start | bytes 4423688 | tf_op jit(solution)/shard_map/ppermute | solution.py:767
  477.3 31.5 %collective-permute-start.75 = (bf16[8,48,1792]{2,1,0:T(8,128)(2,1)S(1)}, bf16[8,48,1792]{2,1,0:T(8,128)(2,1)S(1)}, u32[]{:S(2)}, u32[]{:S(2)}) collective-permute-start(bf16[8,48,1792]{2,1,0:T(8,128)(2,1)S(1)} %bitcast.225), channel_id=1, source_target_pairs={{0,2},{1,3},{2,0},{3,1},{4,6},{5,7},{6,4},{7,5},{8,10},{9,11},{10,... | collective-permute-start | bytes 4128776 | tf_op jit(solution)/shard_map/ppermute | solution.py:767
  477.9 21.7 %collective-permute-start.72 = (bf16[2,2,48,1152]{3,2,1,0:T(8,128)(2,1)S(1)}, bf16[2,2,48,1152]{3,2,1,0:T(8,128)(2,1)S(1)}, u32[]{:S(2)}, u32[]{:S(2)}) collective-permute-start(bf16[2,2,48,1152]{3,2,1,0:T(8,128)(2,1)S(1)} %copy-done.88), channel_id=1, source_target_pairs={{0,8},{4,12},{8,16},{12,20},{16,24},{20,28},{24,0},{28,4},{1,9},{5... | collective-permute-start | bytes 1327112 | tf_op jit(solution)/shard_map/ppermute | solution.py:761
  479.8 29.0 %collective-permute-start.73 = (bf16[2,2,48,1152]{3,2,1,0:T(8,128)(2,1)S(1)}, bf16[2,2,48,1152]{3,2,1,0:T(8,128)(2,1)S(1)}, u32[]{:S(2)}, u32[]{:S(2)}) collective-permute-start(bf16[2,2,48,1152]{3,2,1,0:T(8,128)(2,1)S(1)} %copy-done.86), channel_id=1, source_target_pairs={{0,16},{4,20},{8,24},{12,28},{16,0},{20,4},{24,8},{28,12},{1,17},{... | collective-permute-start | bytes 1327112 | tf_op jit(solution)/shard_map/ppermute | solution.py:761
  509.2 18.7 %collective-permute-start.78 = (bf16[4,48,1920]{2,1,0:T(8,128)(2,1)S(1)}, bf16[4,48,1920]{2,1,0:T(8,128)(2,1)S(1)}, u32[]{:S(2)}, u32[]{:S(2)}) collective-permute-start(bf16[4,48,1920]{2,1,0:T(8,128)(2,1)S(1)} %bitcast.228), channel_id=1, source_target_pairs={{0,2},{1,3},{2,0},{3,1},{4,6},{5,7},{6,4},{7,5},{8,10},{9,11},{10,... | collective-permute-start | bytes 2211848 | tf_op jit(solution)/shard_map/ppermute | solution.py:767
  510.9 16.8 %collective-permute-start.79 = (bf16[4,48,1792]{2,1,0:T(8,128)(2,1)S(1)}, bf16[4,48,1792]{2,1,0:T(8,128)(2,1)S(1)}, u32[]{:S(2)}, u32[]{:S(2)}) collective-permute-start(bf16[4,48,1792]{2,1,0:T(8,128)(2,1)S(1)} %bitcast.229), channel_id=1, source_target_pairs={{0,1},{1,0},{2,3},{3,2},{4,5},{5,4},{6,7},{7,6},{8,9},{9,8},{10,11... | collective-permute-start | bytes 2064392 | tf_op jit(solution)/shard_map/ppermute | solution.py:767
  511.9 16.2 %collective-permute-start.77 = (bf16[2,2,48,1152]{3,2,1,0:T(8,128)(2,1)S(1)}, bf16[2,2,48,1152]{3,2,1,0:T(8,128)(2,1)S(1)}, u32[]{:S(2)}, u32[]{:S(2)}) collective-permute-start(bf16[2,2,48,1152]{3,2,1,0:T(8,128)(2,1)S(1)} %copy-done.82), channel_id=1, source_target_pairs={{0,24},{4,28},{8,0},{12,4},{16,8},{20,12},{24,16},{28,20},{1,25},{... | collective-permute-start | bytes 1327112 | tf_op jit(solution)/shard_map/ppermute | solution.py:761
  528.1 25.5 %collective-permute-start.80 = (bf16[48,3712]{1,0:T(8,128)(2,1)S(1)}, bf16[48,3712]{1,0:T(8,128)(2,1)S(1)}, u32[]{:S(2)}, u32[]{:S(2)}) collective-permute-start(bf16[48,3712]{1,0:T(8,128)(2,1)S(1)} %pad_maximum_fusion.8), channel_id=1, source_target_pairs={{0,8},{4,12},{8,16},{12,20},{16,24},{20,28},{24,0},{28,4},{1,9},{5... | collective-permute-start | bytes 1069064 | tf_op jit(solution)/shard_map/ppermute | solution.py:761
  529.7 29.0 %collective-permute-start.81 = (bf16[48,3712]{1,0:T(8,128)(2,1)S(1)}, bf16[48,3712]{1,0:T(8,128)(2,1)S(1)}, u32[]{:S(2)}, u32[]{:S(2)}) collective-permute-start(bf16[48,3712]{1,0:T(8,128)(2,1)S(1)} %pad_maximum_fusion.9), channel_id=1, source_target_pairs={{0,16},{4,20},{8,24},{12,28},{16,0},{20,4},{24,8},{28,12},{1,17},{... | collective-permute-start | bytes 1069064 | tf_op jit(solution)/shard_map/ppermute | solution.py:761
  534.1 28.7 %collective-permute-start.82 = (bf16[48,3712]{1,0:T(8,128)(2,1)S(1)}, bf16[48,3712]{1,0:T(8,128)(2,1)S(1)}, u32[]{:S(2)}, u32[]{:S(2)}) collective-permute-start(bf16[48,3712]{1,0:T(8,128)(2,1)S(1)} %pad_maximum_fusion.10), channel_id=1, source_target_pairs={{0,24},{4,28},{8,0},{12,4},{16,8},{20,12},{24,16},{28,20},{1,25},{... | collective-permute-start | bytes 1069064 | tf_op jit(solution)/shard_map/ppermute | solution.py:761
  (137 other events, 1233.3 us)
Sparse Core Ops, SparseCore 0:
  33.2 81.3 all-gather.2
  117.1 65.8 all-gather.4

commit v2 on v1

--- a/solution.py
+++ b/solution.py
@@ -904,6 +904,8 @@
     gain_two = small_params[:, D : 2 * D]
     qkv_bias = small_params[:, 2 * D :]
     normed_one, key_value = project_kv(inputs, w_qkv, gain_one, qkv_bias, cosine, sine)
+    for shift in groups[2]:
+        gate_up_pieces[shift] = after(gate_up_pieces[shift], key_value)
     gate_up_held = [
         jnp.concatenate([gate_up_pieces[t] for t in ts], axis=0)
         for ts in (range(n_chips // 2), range(n_chips // 2, n_chips))
@@ -946,8 +948,22 @@
     upstream_swapped = [swap(piece) for piece in upstream_ring[:2]]
     residual, normed_two, attended_low = out_project(inputs, attended, w_out, gain_two)
     normed_ring, normed_swapped = [normed_two], [swap(normed_two)]
-    gate_up_parts, upstream_ring, upstream_swapped, normed_ring, normed_swapped, residual = fence(
-        gate_up_parts, upstream_ring, upstream_swapped, normed_ring, normed_swapped, residual
+    (
+        gate_up_parts,
+        upstream_ring,
+        upstream_swapped,
+        normed_ring,
+        normed_swapped,
+        residual,
+        w_down,
+    ) = fence(
+        gate_up_parts,
+        upstream_ring,
+        upstream_swapped,
+        normed_ring,
+        normed_swapped,
+        residual,
+        w_down,
     )
 
     pieces, where = [], []

time: 580 us -> 589 us (1.016)
  starting transfers between devices: 74.7 us -> 82.9 us
    ppermute x61, starting transfers between devices: 49.1 us -> 55.8 us  [seq_perm(): lax.ppermute(values, 'seq', [(i, (i + 2 * chips) % count ^ flip) for i in...]
    unnamed x233 -> x257, local copies, waits for them, and re-layouts: 55.7 us -> 53.7 us
  transfers between devices with their start and end apart: 87 -> 87, of which waited for: 42 -> 37; matrix products, arithmetic and copies ran while one was open for 4% -> 4% of each run, Pallas kernels for 35% -> 35%
where the time goes in v2:
time: 589 us; the launch traced here: 582 us
  Pallas kernels  203 us (34%)
  waiting for transfers between devices  199 us (34%)
  starting transfers between devices  82.9 us (14%)
  local copies, waits for them, and re-layouts  60.1 us (10%)
  other arithmetic  21.1 us (4%)
  between operations  15.7 us (3%)
    pallas_call x44, Pallas kernels, kernel_call(): pl.pallas_call(kernel, name=name, out_shape=out_shape, compiler_params=pl...  203 us
    ppermute x61, waiting for transfers between devices, seq_perm(): lax.ppermute(values, 'seq', [(i, (i + 2 * chips) % count ^ flip) for i in...  135 us
    ppermute x24, waiting for transfers between devices, dp_perm(): lax.ppermute(values, 'dp', [(i, i ^ bit) for i in range(lax.axis_size('dp...  63.7 us
    ppermute x61, starting transfers between devices, seq_perm(): lax.ppermute(values, 'seq', [(i, (i + 2 * chips) % count ^ flip) for i in...  55.8 us
    unnamed x257, local copies, waits for them, and re-layouts  53.7 us
    ppermute x24, starting transfers between devices, dp_perm(): lax.ppermute(values, 'dp', [(i, i ^ bit) for i in range(lax.axis_size('dp...  27 us
  transfers between devices with their start and end apart: 87, of which 37 were waited for; matrix products, arithmetic and copies ran while one was open for 4% of the time, Pallas kernels for 35%

profile of v2, /device:TPU:8, one launch (start us, length us, event | category | flops | bytes accessed | tf_op | source)
XLA Modules:
  0.0 582.2 jit_solution(15898026548668367446)
XLA Ops:
  21.7 4.8 collective-permute-done.refs_1_
  26.5 4.2 collective-permute-done.1.refs_2_
  35.7 10.3 %collective-permute-done.5 = bf16[4,48,1024]{2,1,0:T(8,128)(2,1)S(1)} collective-permute-done((bf16[4,48,1024]{2,1,0:T(8,128)(2,1)S(1)}, bf16[4,48,1024]{2,1,0:T(8,128)(2,1)S(1)}, u32[]{:S(2)}, u32[]{:S(2)}) %collective-permute-start.5) | collective-permute-done | bytes 393248 | tf_op jit(solution)/shard_map/ppermute | solution.py:767
  51.7 9.4 %collective-permute-done.9 = bf16[2,2,48,1152]{3,2,1,0:T(8,128)(2,1)} collective-permute-done((bf16[2,2,48,1152]{3,2,1,0:T(8,128)(2,1)}, bf16[2,2,48,1152]{3,2,1,0:T(8,128)(2,1)}, u32[]{:S(2)}, u32[]{:S(2)}) %collective-permute-start.9) | collective-permute-done | bytes 442400 | tf_op jit(solution)/shard_map/ppermute | solution.py:761
  61.2 6.0 %collective-permute-done.8.refs_5_ = bf16[8,48,1024]{2,1,0:T(8,128)(2,1)} collective-permute-done((bf16[8,48,1024]{2,1,0:T(8,128)(2,1)S(1)}, bf16[8,48,1024]{2,1,0:T(8,128)(2,1)}, u32[]{:S(2)}, u32[]{:S(2)}) %collective-permute-start.8) | collective-permute-done | bytes 786464 | tf_op jit(solution)/shard_map/ppermute | solution.py:767
  73.1 3.8 assemble.2
  76.9 2.6 copy-done.7
  81.0 3.2 project_kv.1
  84.2 8.5 %collective-permute-done.14 = bf16[2,2,48,1152]{3,2,1,0:T(8,128)(2,1)} collective-permute-done((bf16[2,2,48,1152]{3,2,1,0:T(8,128)(2,1)}, bf16[2,2,48,1152]{3,2,1,0:T(8,128)(2,1)}, u32[]{:S(2)}, u32[]{:S(2)}) %collective-permute-start.14) | collective-permute-done | bytes 442400 | tf_op jit(solution)/shard_map/ppermute | solution.py:761
  92.7 2.1 pad_maximum_fusion.5
  98.9 4.3 collective-permute-start.16
  103.2 6.7 %collective-permute-done.15.refs_2_ = bf16[256,512]{1,0:T(8,128)(2,1)S(1)} collective-permute-done((bf16[256,512]{1,0:T(8,128)(2,1)S(1)}, bf16[256,512]{1,0:T(8,128)(2,1)S(1)}, u32[]{:S(2)}, u32[]{:S(2)}) %collective-permute-start.15) | collective-permute-done | bytes 262176 | tf_op jit(solution)/shard_map/ppermute | solution.py:761
  109.9 5.2 project_q.1.q_ref
  115.1 14.0 %collective-permute-done.16.refs_4_ = bf16[256,512]{1,0:T(8,128)(2,1)S(1)} collective-permute-done((bf16[256,512]{1,0:T(8,128)(2,1)S(1)}, bf16[256,512]{1,0:T(8,128)(2,1)S(1)}, u32[]{:S(2)}, u32[]{:S(2)}) %collective-permute-start.16) | collective-permute-done | bytes 262176 | tf_op jit(solution)/shard_map/ppermute | solution.py:761
  129.0 2.6 collective-permute-done.17.refs_6_
  150.1 10.9 %attend.1 = (f32[256,1536]{1,0:T(8,128)S(1)}, f32[12,256]{1,0:T(8,128)S(1)}, bf16[2048,512]{1,0:T(8,128)(2,1)S(1)}) custom-call(s32[2]{0:T(128)S(1)} %slice_bitcast_fusion.1.query_bases, s32[16]{0:T(128)S(1)} %select_n.83.key_bases, bf16[256,1536]{1,0:T(8,128)(2,1)S(1)} %copy-done.13, bf16[256,512]{1,0:T(8,128)(2,1)S(1)} %copy-done.71, ...), custom_call_target="tpu_custom_call" | custom-call | flops 1000000 | bytes 1000000 | tf_op jit(solution)/shard_map/attend/pallas_call | solution.py:38
  162.3 5.3 collective-permute-done.24
  171.4 2.3 copy-done.8
  173.8 2.4 out_project.1
  178.3 9.2 %collective-permute-done.29.grad_own = bf16[256,1536]{1,0:T(8,128)(2,1)} collective-permute-done((bf16[256,1536]{1,0:T(8,128)(2,1)}, bf16[256,1536]{1,0:T(8,128)(2,1)}, u32[]{:S(2)}, u32[]{:S(2)}) %collective-permute-start.29) | collective-permute-done | bytes 786464 | tf_op jit(solution)/shard_map/ppermute | solution.py:761
  188.1 19.9 %collective-permute-done.27 = bf16[4,2,48,1152]{3,2,1,0:T(8,128)(2,1)} collective-permute-done((bf16[4,2,48,1152]{3,2,1,0:T(8,128)(2,1)}, bf16[4,2,48,1152]{3,2,1,0:T(8,128)(2,1)}, u32[]{:S(2)}, u32[]{:S(2)}) %collective-permute-start.27) | collective-permute-done | bytes 884768 | tf_op jit(solution)/shard_map/ppermute | solution.py:767
  213.3 5.1 assemble.3
  218.5 2.9 copy-done
  221.4 17.4 %feed_forward.4 = (bf16[256,1536]{1,0:T(8,128)(2,1)S(1)}, bf16[256,1536]{1,0:T(8,128)(2,1)}, bf16[256,1536]{1,0:T(8,128)(2,1)S(1)}, bf16[256,1536]{1,0:T(8,128)(...) custom-call(bf16[256,1536]{1,0:T(8,128)(2,1)} %get-tuple-element.454, ...), custom_call_target="tpu_custom_call" | custom-call | flops 1000000 | bytes 1000000 | tf_op jit(solution)/shard_map/feed_forward/pallas_call | solution.py:38
  239.4 5.3 collective-permute-done.35.grad_own
  246.5 17.3 %feed_forward.5 = (bf16[256,1536]{1,0:T(8,128)(2,1)S(1)}, bf16[256,1536]{1,0:T(8,128)(2,1)S(1)}, bf16[256,1536]{1,0:T(8,128)(2,1)S(1)}, bf16[256,1536]{1,0:T(8,1...) custom-call(bf16[256,1536]{1,0:T(8,128)(2,1)} %collective-permute-do, ...), custom_call_target="tpu_custom_call", output_to_operand_aliasing={{4}: (6, {}), {5}: (7, {}), {6}: (8, {}), {7}: (9, {}), {8}... | custom-call | flops 1000000 | bytes 1000000 | tf_op jit(solution)/shard_map/feed_forward/pallas_call | solution.py:38
  269.9 2.3 collective-permute-start.42
  272.2 16.9 %feed_forward.6 = (bf16[256,1536]{1,0:T(8,128)(2,1)S(1)}, bf16[256,1536]{1,0:T(8,128)(2,1)}, bf16[256,1536]{1,0:T(8,128)(2,1)S(1)}, bf16[256,1536]{1,0:T(8,128)(...) custom-call(bf16[256,1536]{1,0:T(8,128)(2,1)S(1)} %collective-permut, ...), custom_call_target="tpu_custom_call", output_to_operand_aliasing={{4}: (6, {}), {5}: (7, {}), {6}: (8, {}), {7}: (9, {}), {8}... | custom-call | flops 1000000 | bytes 1000000 | tf_op jit(solution)/shard_map/feed_forward/pallas_call | solution.py:38
  289.8 15.0 %collective-permute-done.42.refs_2_ = bf16[256,1536]{1,0:T(8,128)(2,1)S(1)} collective-permute-done((bf16[256,1536]{1,0:T(8,128)(2,1)S(1)}, bf16[256,1536]{1,0:T(8,128)(2,1)S(1)}, u32[]{:S(2)}, u32[]{:S(2)}) %collective-permute-start.42) | collective-permute-done | bytes 786464 | tf_op jit(solution)/shard_map/ppermute | solution.py:761
  307.1 16.7 %feed_forward.7 = (bf16[256,1536]{1,0:T(8,128)(2,1)S(1)}, bf16[256,1536]{1,0:T(8,128)(2,1)}, bf16[256,1536]{1,0:T(8,128)(2,1)S(1)}, bf16[256,1536]{1,0:T(8,128)(...) custom-call(bf16[256,1536]{1,0:T(8,128)(2,1)S(1)} %collective-permut, ...), custom_call_target="tpu_custom_call", output_to_operand_aliasing={{4}: (6, {}), {5}: (7, {}), {6}: (8, {}), {7}: (9, {}), {8}... | custom-call | flops 1000000 | bytes 1000000 | tf_op jit(solution)/shard_map/feed_forward/pallas_call | solution.py:38
  323.8 2.2 copy-done.5
  330.7 2.3 collective-permute-start.47
  333.1 2.8 copy-done.1
  335.9 2.3 copy-done.3
  338.2 2.3 copy-done.4
  340.5 12.4 %weight_grad.6 = (bf16[8,1,48,1152]{3,2,1,0:T(8,128)(2,1)S(1)}, bf16[8,1,48,1152]{3,2,1,0:T(8,128)(2,1)}, bf16[4,2,48,1152]{3,2,1,0:T(8,128)(2,1)S(1)}, bf16[4,2,48,1152]{3,2,1,0:T(8,128)(2,1)}) custom-call(s32[2]{0:T(128)S(1)} %pad_add_fusion.8.sides, bf16[4,512,1536]{2,1,0:T(8,128)(2,1)S(1)} %copy-done.1, bf16[4,512,1152]{2,1,0:T(8,128)(2,1)S(1)} %copy-done.3, ...), custom_call_target="tpu_custom_call" | custom-call | flops 1000000 | bytes 1000000 | tf_op jit(solution)/shard_map/weight_grad/pallas_call | solution.py:38
  355.8 11.6 %weight_grad.7 = (bf16[8,1,48,1152]{3,2,1,0:T(8,128)(2,1)S(1)}, bf16[8,1,48,1152]{3,2,1,0:T(8,128)(2,1)S(1)}, bf16[4,2,48,1152]{3,2,1,0:T(8,128)(2,1)S(1)}, bf16[4,2,48,1152]{3,2,1,0:T(8,128)(2,1)S(1)}) custom-call(s32[2]{0:T(128)S(1)} %pad_add_fusion.8.sides, bf16[4,512,1536]{2,1,0:T(8,128)(2,1)S(1)} %copy-done.1, bf16[4,512,1152]{2,1,0:T(8,128)(2,1)S(1)} %copy-done.3, ...), custom_call_target="tpu_custom_call" | custom-call | flops 1000000 | bytes 1000000 | tf_op jit(solution)/shard_map/weight_grad/pallas_call | solution.py:38
  368.3 3.1 add.779
  375.9 3.6 norm_back.1
  380.7 21.2 %attend_back.1 = (bf16[256,1536]{1,0:T(8,128)(2,1)S(1)}, bf16[1024,512]{1,0:T(8,128)(2,1)S(1)}, bf16[1024,512]{1,0:T(8,128)(2,1)S(1)}) custom-call(s32[2]{0:T(128)S(1)} %copy-done.87, s32[16]{0:T(128)S(1)} %select_n.83.key_bases, bf16[256,1536]{1,0:T(8,128)(2,1)S(1)} %copy-done.14, bf16[2048,512]{1,0:T(8,128)(2,1)S(1)} %copy-done.30, ...), custom_call_target="tpu_custom_call" | custom-call | flops 1000000 | bytes 1000000 | tf_op jit(solution)/shard_map/attend_back/pallas_call | solution.py:38
  402.2 2.5 collective-permute-done.56
  407.1 2.3 collective-permute-start.58
  411.5 4.0 weight_grad.8
  416.9 3.5 weight_grad.9
  420.6 8.6 %weight_grad.10 = bf16[1152,1536]{1,0:T(8,128)(2,1)S(1)} custom-call(s32[1]{0:T(128)} %constant.163.clone.1.chip.sides, bf16[4,512,1152]{2,1,0:T(8,128)(2,1)S(1)} %bitcast.168, bf16[4,512,1536]{2,1,0:T(8,128)(2,1)S(1)} %bitcast.166), custom_call_target="tpu_custom_call" | custom-call | flops 1000000 | bytes 1000000 | tf_op jit(solution)/shard_map/weight_grad/pallas_call | solution.py:38
  437.8 2.5 collective-permute-start.66
  444.9 7.6 %input_back.1 = (bf16[256,512]{1,0:T(8,128)(2,1)}, f32[256,1536]{1,0:T(8,128)}, f32[1,1536]{1,0:T(1,128)}, f32[1,2048]{1,0:T(1,128)}) custom-call(bf16[256,1536]{1,0:T(8,128)(2,1)} %bitcast.178, f32[1,1536]{1,0:T(1,128)} %get-tuple-element.775.gain, bf16[1536,2048]{1,0:T(8,128)(2,1)} %bitcast.171, bf16[256,1536]{1,0:T(8,128)(2,1)} %copy-done.24, ...), custom_call_target="tpu_custom_call" | custom-call | flops 1000000 | bytes 1000000 | tf_op jit(solution)/shard_map/input_back/pallas_call | solution.py:38
  454.9 3.0 collective-permute-done.66
  469.4 2.5 add_halve.14
  471.9 2.4 add_halve.15
  474.3 8.7 %collective-permute-done.70 = bf16[2,288,768]{2,1,0:T(8,128)(2,1)S(1)} collective-permute-done((bf16[2,288,768]{2,1,0:T(8,128)(2,1)}, bf16[2,288,768]{2,1,0:T(8,128)(2,1)S(1)}, u32[]{:S(2)}, u32[]{:S(2)}) %collective-permute-start.70) | collective-permute-done | bytes 884768 | tf_op jit(solution)/shard_map/ppermute | solution.py:767
  485.2 2.6 collective-permute-start.72
  487.8 3.4 collective-permute-start.73
  491.6 8.4 %collective-permute-done.72.refs_1_ = bf16[2,2,48,1152]{3,2,1,0:T(8,128)(2,1)S(1)} collective-permute-done((bf16[2,2,48,1152]{3,2,1,0:T(8,128)(2,1)}, bf16[2,2,48,1152]{3,2,1,0:T(8,128)(2,1)S(1)}, u32[]{:S(2)}, u32[]{:S(2)}) %collective-permute-start.72) | collective-permute-done | bytes 442400 | tf_op jit(solution)/shard_map/ppermute | solution.py:761
  500.1 17.1 %collective-permute-done.73.refs_2_ = bf16[2,2,48,1152]{3,2,1,0:T(8,128)(2,1)S(1)} collective-permute-done((bf16[2,2,48,1152]{3,2,1,0:T(8,128)(2,1)}, bf16[2,2,48,1152]{3,2,1,0:T(8,128)(2,1)S(1)}, u32[]{:S(2)}, u32[]{:S(2)}) %collective-permute-start.73) | collective-permute-done | bytes 442400 | tf_op jit(solution)/shard_map/ppermute | solution.py:761
  520.0 4.4 collective-permute-start.77
  524.4 2.6 fusion.1
  527.0 9.2 %collective-permute-done.79.got = bf16[4,48,1792]{2,1,0:T(8,128)(2,1)S(1)} collective-permute-done((bf16[4,48,1792]{2,1,0:T(8,128)(2,1)S(1)}, bf16[4,48,1792]{2,1,0:T(8,128)(2,1)S(1)}, u32[]{:S(2)}, u32[]{:S(2)}) %collective-permute-start.79) | collective-permute-done | bytes 688160 | tf_op jit(solution)/shard_map/ppermute | solution.py:767
  538.6 4.2 collective-permute-start.81
  545.1 7.6 %adamw_hidden.1 = (f32[2,48,8960]{2,1,0:T(8,128)}, f32[2,48,8960]{2,1,0:T(8,128)}, f32[2,48,8960]{2,1,0:T(8,128)}) custom-call(s32[8]{0:T(128)S(1)} %stack.261.where, f32[2,48,8960]{2,1,0:T(8,128)S(1)} %copy-done.10, f32[2,48,8960]{2,1,0:T(8,128)S(1)} %copy-done.21, f32[2,48,8960]{2,1,0:T(8,128)} %second.1, ...), custom_call_target="tpu_custom_call" | custom-call | flops 1000000 | bytes 1000000 | tf_op jit(solution)/shard_map/adamw_hidden/pallas_call | solution.py:38
  554.7 3.2 multiply_subtract_fusion
  557.9 4.6 collective-permute-done.80
  562.5 5.6 collective-permute-done.81
  568.1 3.9 collective-permute-done.82
  (501 shorter events, 141.7 us)
Async XLA Ops:
  7.2 164.2 %all-gather.3.cloned.1.call-start = ((), (), s32[]{:S(2)}) async-start(), calls=%async_computation | async-start | bytes 4866048 | tf_op jit(solution)/shard_map/all_gather | solution.py:856
  10.6 15.9 %collective-permute-start = (bf16[48,2176]{1,0:T(8,128)(2,1)S(1)}, bf16[48,2176]{1,0:T(8,128)(2,1)S(1)}, u32[]{:S(2)}, u32[]{:S(2)}) collective-permute-start(bf16[48,2176]{1,0:T(8,128)(2,1)S(1)} %pad_maximum_fusion.11.refs_0_), channel_id=1, source_target_pairs={{0,8},{4,12},{8,16},{12,20},{16,24},{20,28},{24,0},{28,4},{1,9},{5... | collective-permute-start | bytes 626696 | tf_op jit(solution)/shard_map/ppermute | solution.py:761
  12.2 18.5 %collective-permute-start.1 = (bf16[48,2176]{1,0:T(8,128)(2,1)S(1)}, bf16[48,2176]{1,0:T(8,128)(2,1)S(1)}, u32[]{:S(2)}, u32[]{:S(2)}) collective-permute-start(bf16[48,2176]{1,0:T(8,128)(2,1)S(1)} %pad_maximum_fusion.11.refs_0_), channel_id=1, source_target_pairs={{0,16},{4,20},{8,24},{12,28},{16,0},{20,4},{24,8},{28,12},{1,17},{... | collective-permute-start | bytes 626696 | tf_op jit(solution)/shard_map/ppermute | solution.py:761
  13.3 19.2 %collective-permute-start.2 = (bf16[48,2176]{1,0:T(8,128)(2,1)S(1)}, bf16[48,2176]{1,0:T(8,128)(2,1)S(1)}, u32[]{:S(2)}, u32[]{:S(2)}) collective-permute-start(bf16[48,2176]{1,0:T(8,128)(2,1)S(1)} %pad_maximum_fusion.11.refs_0_), channel_id=1, source_target_pairs={{0,24},{4,28},{8,0},{12,4},{16,8},{20,12},{24,16},{28,20},{1,25},{... | collective-permute-start | bytes 626696 | tf_op jit(solution)/shard_map/ppermute | solution.py:761
  32.5 175.5 %all-gather.5.cloned.1.call-start = ((), (), s32[]{:S(2)}) async-start(), calls=%async_computation.1 | async-start | bytes 4423680 | tf_op jit(solution)/shard_map/all_gather | solution.py:880
  32.6 13.4 %collective-permute-start.4 = (bf16[4,48,1152]{2,1,0:T(8,128)(2,1)S(1)}, bf16[4,48,1152]{2,1,0:T(8,128)(2,1)S(1)}, u32[]{:S(2)}, u32[]{:S(2)}) collective-permute-start(bf16[4,48,1152]{2,1,0:T(8,128)(2,1)S(1)} %get-tuple-element.392), channel_id=1, source_target_pairs={{0,1},{1,0},{2,3},{3,2},{4,5},{5,4},{6,7},{7,6},{8,9},{9,8},{10,11... | collective-permute-start | bytes 1327112 | tf_op jit(solution)/shard_map/ppermute | solution.py:767
  34.2 12.9 %collective-permute-start.6 = (bf16[2,2,48,1152]{3,2,1,0:T(8,128)(2,1)S(1)}, bf16[2,2,48,1152]{3,2,1,0:T(8,128)(2,1)S(1)}, u32[]{:S(2)}, u32[]{:S(2)}) collective-permute-start(bf16[2,2,48,1152]{3,2,1,0:T(8,128)(2,1)S(1)} %get-tuple-element.391), channel_id=1, source_target_pairs={{0,8},{4,12},{8,16},{12,20},{16,24},{20,28},{24,0},{28,4},{1,9},{5... | collective-permute-start | bytes 1327112 | tf_op jit(solution)/shard_map/ppermute | solution.py:761
  47.2 20.7 %collective-permute-start.7 = (bf16[8,48,1152]{2,1,0:T(8,128)(2,1)S(1)}, bf16[8,48,1152]{2,1,0:T(8,128)(2,1)}, u32[]{:S(2)}, u32[]{:S(2)}) collective-permute-start(bf16[8,48,1152]{2,1,0:T(8,128)(2,1)S(1)} %constant_dynamic-update-slice_fusion.refs_0_), channel_id=1, source_target_pairs={{0,2},{1,3},{2,0},{3,1},{4,6},{5,7},{6,4},{7,5},{8,10},{9,11},{10,... | collective-permute-start | bytes 2654216 | tf_op jit(solution)/shard_map/ppermute | solution.py:767
  48.8 18.3 %collective-permute-start.8 = (bf16[8,48,1024]{2,1,0:T(8,128)(2,1)S(1)}, bf16[8,48,1024]{2,1,0:T(8,128)(2,1)}, u32[]{:S(2)}, u32[]{:S(2)}) collective-permute-start(bf16[8,48,1024]{2,1,0:T(8,128)(2,1)S(1)} %constant_dynamic-update-slice_fusion.2.refs_4_), channel_id=1, source_target_pairs={{0,1},{1,0},{2,3},{3,2},{4,5},{5,4},{6,7},{7,6},{8,9},{9,8},{10,11... | collective-permute-start | bytes 2359304 | tf_op jit(solution)/shard_map/ppermute | solution.py:767
  50.1 19.5 %collective-permute-start.10 = (bf16[8,48,1152]{2,1,0:T(8,128)(2,1)S(1)}, bf16[8,48,1152]{2,1,0:T(8,128)(2,1)S(1)}, u32[]{:S(2)}, u32[]{:S(2)}) collective-permute-start(bf16[8,48,1152]{2,1,0:T(8,128)(2,1)S(1)} %constant_dynamic-update-slice_fusion.refs_0_), channel_id=1, source_target_pairs={{0,4},{4,0},{8,12},{12,8},{16,20},{20,16},{24,28},{28,24},{1,5},{5... | collective-permute-start | bytes 2654216 | tf_op jit(solution)/shard_map/ppermute | solution.py:761
  50.2 18.6 %collective-permute-start.11 = (bf16[8,48,1024]{2,1,0:T(8,128)(2,1)S(1)}, bf16[8,48,1024]{2,1,0:T(8,128)(2,1)S(1)}, u32[]{:S(2)}, u32[]{:S(2)}) collective-permute-start(bf16[8,48,1024]{2,1,0:T(8,128)(2,1)S(1)} %constant_dynamic-update-slice_fusion.2.refs_4_), channel_id=1, source_target_pairs={{0,4},{4,0},{8,12},{12,8},{16,20},{20,16},{24,28},{28,24},{1,5},{5... | collective-permute-start | bytes 2359304 | tf_op jit(solution)/shard_map/ppermute | solution.py:761
  68.6 24.0 %collective-permute-start.14 = (bf16[2,2,48,1152]{3,2,1,0:T(8,128)(2,1)}, bf16[2,2,48,1152]{3,2,1,0:T(8,128)(2,1)}, u32[]{:S(2)}, u32[]{:S(2)}) collective-permute-start(bf16[2,2,48,1152]{3,2,1,0:T(8,128)(2,1)} %copy-done.96), channel_id=1, source_target_pairs={{0,16},{4,20},{8,24},{12,28},{16,0},{20,4},{24,8},{28,12},{1,17},{... | collective-permute-start | bytes 1327112 | tf_op jit(solution)/shard_map/ppermute | solution.py:761
  94.8 41.6 %collective-permute-start.22 = (bf16[4,2,48,1152]{3,2,1,0:T(8,128)(2,1)S(1)}, bf16[4,2,48,1152]{3,2,1,0:T(8,128)(2,1)}, u32[]{:S(2)}, u32[]{:S(2)}) collective-permute-start(bf16[4,2,48,1152]{3,2,1,0:T(8,128)(2,1)S(1)} %pad_maximum_fusion.4), channel_id=1, source_target_pairs={{0,1},{1,0},{2,3},{3,2},{4,5},{5,4},{6,7},{7,6},{8,9},{9,8},{10,11... | collective-permute-start | bytes 2654216 | tf_op jit(solution)/shard_map/ppermute | solution.py:767
  95.9 40.6 %collective-permute-start.23 = (bf16[4,2,48,1152]{3,2,1,0:T(8,128)(2,1)}, bf16[4,2,48,1152]{3,2,1,0:T(8,128)(2,1)}, u32[]{:S(2)}, u32[]{:S(2)}) collective-permute-start(bf16[4,2,48,1152]{3,2,1,0:T(8,128)(2,1)} %pad_maximum_fusion.5), channel_id=1, source_target_pairs={{0,2},{1,3},{2,0},{3,1},{4,6},{5,7},{6,4},{7,5},{8,10},{9,11},{10,... | collective-permute-start | bytes 2654216 | tf_op jit(solution)/shard_map/ppermute | solution.py:767
  98.9 30.1 %collective-permute-start.16 = (bf16[256,512]{1,0:T(8,128)(2,1)S(1)}, bf16[256,512]{1,0:T(8,128)(2,1)S(1)}, u32[]{:S(2)}, u32[]{:S(2)}) collective-permute-start(bf16[256,512]{1,0:T(8,128)(2,1)S(1)} %copy-done.71), channel_id=1, source_target_pairs={{0,16},{4,20},{8,24},{12,28},{16,0},{20,4},{24,8},{28,12},{1,17},{... | collective-permute-start | bytes 786440 | tf_op jit(solution)/shard_map/ppermute | solution.py:761
  103.2 28.4 %collective-permute-start.17 = (bf16[256,512]{1,0:T(8,128)(2,1)S(1)}, bf16[256,512]{1,0:T(8,128)(2,1)S(1)}, u32[]{:S(2)}, u32[]{:S(2)}) collective-permute-start(bf16[256,512]{1,0:T(8,128)(2,1)S(1)} %copy-done.71), channel_id=1, source_target_pairs={{0,24},{4,28},{8,0},{12,4},{16,8},{20,12},{24,16},{28,20},{1,25},{... | collective-permute-start | bytes 786440 | tf_op jit(solution)/shard_map/ppermute | solution.py:761
  109.9 22.4 %collective-permute-start.18 = (bf16[256,512]{1,0:T(8,128)(2,1)S(1)}, bf16[256,512]{1,0:T(8,128)(2,1)S(1)}, u32[]{:S(2)}, u32[]{:S(2)}) collective-permute-start(bf16[256,512]{1,0:T(8,128)(2,1)S(1)} %copy-done.71), channel_id=1, source_target_pairs={{0,4},{4,0},{8,12},{12,8},{16,20},{20,16},{24,28},{28,24},{1,5},{5... | collective-permute-start | bytes 786440 | tf_op jit(solution)/shard_map/ppermute | solution.py:761
  136.5 31.1 %collective-permute-start.24 = (bf16[4,2,48,1152]{3,2,1,0:T(8,128)(2,1)S(1)}, bf16[4,2,48,1152]{3,2,1,0:T(8,128)(2,1)}, u32[]{:S(2)}, u32[]{:S(2)}) collective-permute-start(bf16[4,2,48,1152]{3,2,1,0:T(8,128)(2,1)S(1)} %pad_maximum_fusion.4), channel_id=1, source_target_pairs={{0,2},{1,3},{2,0},{3,1},{4,6},{5,7},{6,4},{7,5},{8,10},{9,11},{10,... | collective-permute-start | bytes 2654216 | tf_op jit(solution)/shard_map/ppermute | solution.py:767
  137.8 31.1 %collective-permute-start.25 = (bf16[4,2,48,1152]{3,2,1,0:T(8,128)(2,1)}, bf16[4,2,48,1152]{3,2,1,0:T(8,128)(2,1)}, u32[]{:S(2)}, u32[]{:S(2)}) collective-permute-start(bf16[4,2,48,1152]{3,2,1,0:T(8,128)(2,1)} %pad_maximum_fusion.5), channel_id=1, source_target_pairs={{0,1},{1,0},{2,3},{3,2},{4,5},{5,4},{6,7},{7,6},{8,9},{9,8},{10,11... | collective-permute-start | bytes 2654216 | tf_op jit(solution)/shard_map/ppermute | solution.py:767
  139.2 23.1 %collective-permute-start.26 = (bf16[256,1536]{1,0:T(8,128)(2,1)}, bf16[256,1536]{1,0:T(8,128)(2,1)}, u32[]{:S(2)}, u32[]{:S(2)}) collective-permute-start(bf16[256,1536]{1,0:T(8,128)(2,1)} %bitcast.38.grad_own.cotangent), channel_id=1, source_target_pairs={{0,8},{4,12},{8,16},{12,20},{16,24},{20,28},{24,0},{28,4},{1,9},{5... | collective-permute-start | bytes 2359304 | tf_op jit(solution)/shard_map/ppermute | solution.py:761
  168.9 18.6 %collective-permute-start.29 = (bf16[256,1536]{1,0:T(8,128)(2,1)}, bf16[256,1536]{1,0:T(8,128)(2,1)}, u32[]{:S(2)}, u32[]{:S(2)}) collective-permute-start(bf16[256,1536]{1,0:T(8,128)(2,1)} %collective-permute-done.26.grad_own), channel_id=1, source_target_pairs={{0,8},{4,12},{8,16},{12,20},{16,24},{20,28},{24,0},{28,4},{1,9},{5... | collective-permute-start | bytes 2359304 | tf_op jit(solution)/shard_map/ppermute | solution.py:761
  168.9 39.1 %collective-permute-start.27 = (bf16[4,2,48,1152]{3,2,1,0:T(8,128)(2,1)}, bf16[4,2,48,1152]{3,2,1,0:T(8,128)(2,1)}, u32[]{:S(2)}, u32[]{:S(2)}) collective-permute-start(bf16[4,2,48,1152]{3,2,1,0:T(8,128)(2,1)} %collective-permute-done.22), channel_id=1, source_target_pairs={{0,2},{1,3},{2,0},{3,1},{4,6},{5,7},{6,4},{7,5},{8,10},{9,11},{10,... | collective-permute-start | bytes 2654216 | tf_op jit(solution)/shard_map/ppermute | solution.py:767
  169.6 38.5 %collective-permute-start.28 = (bf16[4,2,48,1152]{3,2,1,0:T(8,128)(2,1)}, bf16[4,2,48,1152]{3,2,1,0:T(8,128)(2,1)}, u32[]{:S(2)}, u32[]{:S(2)}) collective-permute-start(bf16[4,2,48,1152]{3,2,1,0:T(8,128)(2,1)} %collective-permute-done.23), channel_id=1, source_target_pairs={{0,1},{1,0},{2,3},{3,2},{4,5},{5,4},{6,7},{7,6},{8,9},{9,8},{10,11... | collective-permute-start | bytes 2654216 | tf_op jit(solution)/shard_map/ppermute | solution.py:767
  170.9 17.2 %collective-permute-start.31 = (bf16[256,1536]{1,0:T(8,128)(2,1)}, bf16[256,1536]{1,0:T(8,128)(2,1)}, u32[]{:S(2)}, u32[]{:S(2)}) collective-permute-start(bf16[256,1536]{1,0:T(8,128)(2,1)} %collective-permute-done.26.grad_own), channel_id=1, source_target_pairs={{0,4},{4,0},{8,12},{12,8},{16,20},{20,16},{24,28},{28,24},{1,5},{5... | collective-permute-start | bytes 2359304 | tf_op jit(solution)/shard_map/ppermute | solution.py:761
  170.9 17.2 %collective-permute-start.30 = (bf16[256,1536]{1,0:T(8,128)(2,1)}, bf16[256,1536]{1,0:T(8,128)(2,1)}, u32[]{:S(2)}, u32[]{:S(2)}) collective-permute-start(bf16[256,1536]{1,0:T(8,128)(2,1)} %bitcast.38.grad_own.cotangent), channel_id=1, source_target_pairs={{0,4},{4,0},{8,12},{12,8},{16,20},{20,16},{24,28},{28,24},{1,5},{5... | collective-permute-start | bytes 2359304 | tf_op jit(solution)/shard_map/ppermute | solution.py:761
  187.5 20.6 %collective-permute-start.32 = (bf16[256,1536]{1,0:T(8,128)(2,1)}, bf16[256,1536]{1,0:T(8,128)(2,1)S(1)}, u32[]{:S(2)}, u32[]{:S(2)}) collective-permute-start(bf16[256,1536]{1,0:T(8,128)(2,1)} %get-tuple-element.454.normed_own), channel_id=1, source_target_pairs={{0,4},{4,0},{8,12},{12,8},{16,20},{20,16},{24,28},{28,24},{1,5},{5... | collective-permute-start | bytes 2359304 | tf_op jit(solution)/shard_map/ppermute | solution.py:761
  208.9 30.0 %collective-permute-start.33 = (bf16[256,1536]{1,0:T(8,128)(2,1)}, bf16[256,1536]{1,0:T(8,128)(2,1)}, u32[]{:S(2)}, u32[]{:S(2)}) collective-permute-start(bf16[256,1536]{1,0:T(8,128)(2,1)} %get-tuple-element.454.normed_own), channel_id=1, source_target_pairs={{0,8},{4,12},{8,16},{12,20},{16,24},{20,28},{24,0},{28,4},{1,9},{5... | collective-permute-start | bytes 2359304 | tf_op jit(solution)/shard_map/ppermute | solution.py:761
  211.4 33.3 %collective-permute-start.35 = (bf16[256,1536]{1,0:T(8,128)(2,1)}, bf16[256,1536]{1,0:T(8,128)(2,1)S(1)}, u32[]{:S(2)}, u32[]{:S(2)}) collective-permute-start(bf16[256,1536]{1,0:T(8,128)(2,1)} %collective-permute-done.29.grad_own), channel_id=1, source_target_pairs={{0,8},{4,12},{8,16},{12,20},{16,24},{20,28},{24,0},{28,4},{1,9},{5... | collective-permute-start | bytes 2359304 | tf_op jit(solution)/shard_map/ppermute | solution.py:761
  244.7 19.6 %collective-permute-start.38 = (bf16[256,1536]{1,0:T(8,128)(2,1)}, bf16[256,1536]{1,0:T(8,128)(2,1)S(1)}, u32[]{:S(2)}, u32[]{:S(2)}) collective-permute-start(bf16[256,1536]{1,0:T(8,128)(2,1)} %collective-permute-done.33.normed_own), channel_id=1, source_target_pairs={{0,8},{4,12},{8,16},{12,20},{16,24},{20,28},{24,0},{28,4},{1,9},{5... | collective-permute-start | bytes 2359304 | tf_op jit(solution)/shard_map/ppermute | solution.py:761
  268.4 20.9 %collective-permute-start.43 = (bf16[256,1536]{1,0:T(8,128)(2,1)S(1)}, bf16[256,1536]{1,0:T(8,128)(2,1)S(1)}, u32[]{:S(2)}, u32[]{:S(2)}) collective-permute-start(bf16[256,1536]{1,0:T(8,128)(2,1)S(1)} %collective-permute-done.38.normed_own), channel_id=1, source_target_pairs={{0,8},{4,12},{8,16},{12,20},{16,24},{20,28},{24,0},{28,4},{1,9},{5... | collective-permute-start | bytes 2359304 | tf_op jit(solution)/shard_map/ppermute | solution.py:761
  269.9 34.9 %collective-permute-start.42 = (bf16[256,1536]{1,0:T(8,128)(2,1)S(1)}, bf16[256,1536]{1,0:T(8,128)(2,1)S(1)}, u32[]{:S(2)}, u32[]{:S(2)}) collective-permute-start(bf16[256,1536]{1,0:T(8,128)(2,1)S(1)} %add.775), channel_id=1, source_target_pairs={{0,8},{4,12},{8,16},{12,20},{16,24},{20,28},{24,0},{28,4},{1,9},{5... | collective-permute-start | bytes 2359304 | tf_op jit(solution)/shard_map/ppermute | solution.py:761
  289.2 15.7 %collective-permute-start.41 = (bf16[256,1536]{1,0:T(8,128)(2,1)S(1)}, bf16[256,1536]{1,0:T(8,128)(2,1)S(1)}, u32[]{:S(2)}, u32[]{:S(2)}) collective-permute-start(bf16[256,1536]{1,0:T(8,128)(2,1)S(1)} %get-tuple-element.509), channel_id=1, source_target_pairs={{0,4},{4,0},{8,12},{12,8},{16,20},{20,16},{24,28},{28,24},{1,5},{5... | collective-permute-start | bytes 2359304 | tf_op jit(solution)/shard_map/ppermute | solution.py:761
  289.2 15.9 %collective-permute-start.44 = (bf16[256,1536]{1,0:T(8,128)(2,1)S(1)}, bf16[256,1536]{1,0:T(8,128)(2,1)S(1)}, u32[]{:S(2)}, u32[]{:S(2)}) collective-permute-start(bf16[256,1536]{1,0:T(8,128)(2,1)S(1)} %collective-permute-done.43.normed_own), channel_id=1, source_target_pairs={{0,4},{4,0},{8,12},{12,8},{16,20},{20,16},{24,28},{28,24},{1,5},{5... | collective-permute-start | bytes 2359304 | tf_op jit(solution)/shard_map/ppermute | solution.py:761
  289.7 36.3 %collective-permute-start.48 = (bf16[256,1536]{1,0:T(8,128)(2,1)S(1)}, bf16[256,1536]{1,0:T(8,128)(2,1)S(1)}, u32[]{:S(2)}, u32[]{:S(2)}) collective-permute-start(bf16[256,1536]{1,0:T(8,128)(2,1)S(1)} %get-tuple-element.553), channel_id=1, source_target_pairs={{0,4},{4,0},{8,12},{12,8},{16,20},{20,16},{24,28},{28,24},{1,5},{5... | collective-permute-start | bytes 2359304 | tf_op jit(solution)/shard_map/ppermute | solution.py:761
  305.1 24.4 %collective-permute-start.46 = (bf16[256,1536]{1,0:T(8,128)(2,1)S(1)}, bf16[256,1536]{1,0:T(8,128)(2,1)S(1)}, u32[]{:S(2)}, u32[]{:S(2)}) collective-permute-start(bf16[256,1536]{1,0:T(8,128)(2,1)S(1)} %add.776), channel_id=1, source_target_pairs={{0,8},{4,12},{8,16},{12,20},{16,24},{20,28},{24,0},{28,4},{1,9},{5... | collective-permute-start | bytes 2359304 | tf_op jit(solution)/shard_map/ppermute | solution.py:761
  327.3 27.6 %collective-permute-start.50 = (bf16[256,1536]{1,0:T(8,128)(2,1)}, bf16[256,1536]{1,0:T(8,128)(2,1)S(1)}, u32[]{:S(2)}, u32[]{:S(2)}) collective-permute-start(bf16[256,1536]{1,0:T(8,128)(2,1)} %add.778), channel_id=1, source_target_pairs={{0,8},{4,12},{8,16},{12,20},{16,24},{20,28},{24,0},{28,4},{1,9},{5... | collective-permute-start | bytes 2359304 | tf_op jit(solution)/shard_map/ppermute | solution.py:761
  329.4 38.9 %collective-permute-start.49 = (bf16[256,1536]{1,0:T(8,128)(2,1)}, bf16[256,1536]{1,0:T(8,128)(2,1)}, u32[]{:S(2)}, u32[]{:S(2)}) collective-permute-start(bf16[256,1536]{1,0:T(8,128)(2,1)} %get-tuple-element.555), channel_id=1, source_target_pairs={{0,4},{4,0},{8,12},{12,8},{16,20},{20,16},{24,28},{28,24},{1,5},{5... | collective-permute-start | bytes 2359304 | tf_op jit(solution)/shard_map/ppermute | solution.py:761
  330.7 40.7 %collective-permute-start.47 = (bf16[256,1536]{1,0:T(8,128)(2,1)}, bf16[256,1536]{1,0:T(8,128)(2,1)S(1)}, u32[]{:S(2)}, u32[]{:S(2)}) collective-permute-start(bf16[256,1536]{1,0:T(8,128)(2,1)} %add.777), channel_id=1, source_target_pairs={{0,8},{4,12},{8,16},{12,20},{16,24},{20,28},{24,0},{28,4},{1,9},{5... | collective-permute-start | bytes 2359304 | tf_op jit(solution)/shard_map/ppermute | solution.py:761
  371.4 30.6 %collective-permute-start.51 = (bf16[8,48,1152]{2,1,0:T(8,128)(2,1)}, bf16[8,48,1152]{2,1,0:T(8,128)(2,1)S(1)}, u32[]{:S(2)}, u32[]{:S(2)}) collective-permute-start(bf16[8,48,1152]{2,1,0:T(8,128)(2,1)} %bitcast.69), channel_id=1, source_target_pairs={{0,1},{1,0},{2,3},{3,2},{4,5},{5,4},{6,7},{7,6},{8,9},{9,8},{10,11... | collective-permute-start | bytes 2654216 | tf_op jit(solution)/shard_map/ppermute | solution.py:767
  372.9 29.1 %collective-permute-start.52 = (bf16[8,48,1152]{2,1,0:T(8,128)(2,1)}, bf16[8,48,1152]{2,1,0:T(8,128)(2,1)S(1)}, u32[]{:S(2)}, u32[]{:S(2)}) collective-permute-start(bf16[8,48,1152]{2,1,0:T(8,128)(2,1)} %bitcast.71), channel_id=1, source_target_pairs={{0,2},{1,3},{2,0},{3,1},{4,6},{5,7},{6,4},{7,5},{8,10},{9,11},{10,... | collective-permute-start | bytes 2654216 | tf_op jit(solution)/shard_map/ppermute | solution.py:767
  373.6 28.4 %collective-permute-start.54 = (bf16[256,1536]{1,0:T(8,128)(2,1)}, bf16[256,1536]{1,0:T(8,128)(2,1)S(1)}, u32[]{:S(2)}, u32[]{:S(2)}) collective-permute-start(bf16[256,1536]{1,0:T(8,128)(2,1)} %add.779), channel_id=1, source_target_pairs={{0,8},{4,12},{8,16},{12,20},{16,24},{20,28},{24,0},{28,4},{1,9},{5... | collective-permute-start | bytes 2359304 | tf_op jit(solution)/shard_map/ppermute | solution.py:761
  374.4 27.6 %collective-permute-start.55 = (bf16[256,1536]{1,0:T(8,128)(2,1)}, bf16[256,1536]{1,0:T(8,128)(2,1)S(1)}, u32[]{:S(2)}, u32[]{:S(2)}) collective-permute-start(bf16[256,1536]{1,0:T(8,128)(2,1)} %get-tuple-element.574), channel_id=1, source_target_pairs={{0,4},{4,0},{8,12},{12,8},{16,20},{20,16},{24,28},{28,24},{1,5},{5... | collective-permute-start | bytes 2359304 | tf_op jit(solution)/shard_map/ppermute | solution.py:761
  405.0 25.6 %collective-permute-start.60 = (bf16[8,48,1152]{2,1,0:T(8,128)(2,1)S(1)}, bf16[8,48,1152]{2,1,0:T(8,128)(2,1)S(1)}, u32[]{:S(2)}, u32[]{:S(2)}) collective-permute-start(bf16[8,48,1152]{2,1,0:T(8,128)(2,1)S(1)} %bitcast.222), channel_id=1, source_target_pairs={{0,1},{1,0},{2,3},{3,2},{4,5},{5,4},{6,7},{7,6},{8,9},{9,8},{10,11... | collective-permute-start | bytes 2654216 | tf_op jit(solution)/shard_map/ppermute | solution.py:767
  406.6 24.1 %collective-permute-start.61 = (bf16[8,48,1152]{2,1,0:T(8,128)(2,1)S(1)}, bf16[8,48,1152]{2,1,0:T(8,128)(2,1)S(1)}, u32[]{:S(2)}, u32[]{:S(2)}) collective-permute-start(bf16[8,48,1152]{2,1,0:T(8,128)(2,1)S(1)} %bitcast.221), channel_id=1, source_target_pairs={{0,2},{1,3},{2,0},{3,1},{4,6},{5,7},{6,4},{7,5},{8,10},{9,11},{10,... | collective-permute-start | bytes 2654216 | tf_op jit(solution)/shard_map/ppermute | solution.py:767
  407.1 22.0 %collective-permute-start.57 = (bf16[256,512]{1,0:T(8,128)(2,1)S(1)}, bf16[256,512]{1,0:T(8,128)(2,1)S(1)}, u32[]{:S(2)}, u32[]{:S(2)}) collective-permute-start(bf16[256,512]{1,0:T(8,128)(2,1)S(1)} %get-tuple-element.594), channel_id=1, source_target_pairs={{0,24},{4,28},{8,0},{12,4},{16,8},{20,12},{24,16},{28,20},{1,25},{... | collective-permute-start | bytes 786440 | tf_op jit(solution)/shard_map/ppermute | solution.py:761
  407.1 22.1 %collective-permute-start.58 = (bf16[256,512]{1,0:T(8,128)(2,1)S(1)}, bf16[256,512]{1,0:T(8,128)(2,1)S(1)}, u32[]{:S(2)}, u32[]{:S(2)}) collective-permute-start(bf16[256,512]{1,0:T(8,128)(2,1)S(1)} %get-tuple-element.595), channel_id=1, source_target_pairs={{0,16},{4,20},{8,24},{12,28},{16,0},{20,4},{24,8},{28,12},{1,17},{... | collective-permute-start | bytes 786440 | tf_op jit(solution)/shard_map/ppermute | solution.py:761
  409.4 21.3 %collective-permute-start.59 = (bf16[256,512]{1,0:T(8,128)(2,1)S(1)}, bf16[256,512]{1,0:T(8,128)(2,1)S(1)}, u32[]{:S(2)}, u32[]{:S(2)}) collective-permute-start(bf16[256,512]{1,0:T(8,128)(2,1)S(1)} %get-tuple-element.596), channel_id=1, source_target_pairs={{0,8},{4,12},{8,16},{12,20},{16,24},{20,28},{24,0},{28,4},{1,9},{5... | collective-permute-start | bytes 786440 | tf_op jit(solution)/shard_map/ppermute | solution.py:761
  430.6 28.1 %collective-permute-start.64 = (bf16[16,48,1536]{2,1,0:T(8,128)(2,1)}, bf16[16,48,1536]{2,1,0:T(8,128)(2,1)}, u32[]{:S(2)}, u32[]{:S(2)}) collective-permute-start(bf16[16,48,1536]{2,1,0:T(8,128)(2,1)} %bitcast.84), channel_id=1, source_target_pairs={{0,4},{4,0},{8,12},{12,8},{16,20},{20,16},{24,28},{28,24},{1,5},{5... | collective-permute-start | bytes 7077896 | tf_op jit(solution)/shard_map/ppermute | solution.py:761
  430.7 28.1 %collective-permute-start.65 = (bf16[16,48,1536]{2,1,0:T(8,128)(2,1)}, bf16[16,48,1536]{2,1,0:T(8,128)(2,1)}, u32[]{:S(2)}, u32[]{:S(2)}) collective-permute-start(bf16[16,48,1536]{2,1,0:T(8,128)(2,1)} %bitcast.88), channel_id=1, source_target_pairs={{0,4},{4,0},{8,12},{12,8},{16,20},{20,16},{24,28},{28,24},{1,5},{5... | collective-permute-start | bytes 7077896 | tf_op jit(solution)/shard_map/ppermute | solution.py:761
  433.6 24.3 %collective-permute-start.62 = (bf16[8,48,1152]{2,1,0:T(8,128)(2,1)}, bf16[8,48,1152]{2,1,0:T(8,128)(2,1)}, u32[]{:S(2)}, u32[]{:S(2)}) collective-permute-start(bf16[8,48,1152]{2,1,0:T(8,128)(2,1)} %bitcast.91), channel_id=1, source_target_pairs={{0,2},{1,3},{2,0},{3,1},{4,6},{5,7},{6,4},{7,5},{8,10},{9,11},{10,... | collective-permute-start | bytes 2654216 | tf_op jit(solution)/shard_map/ppermute | solution.py:767
  437.2 21.6 %collective-permute-start.63 = (bf16[8,48,1152]{2,1,0:T(8,128)(2,1)}, bf16[8,48,1152]{2,1,0:T(8,128)(2,1)}, u32[]{:S(2)}, u32[]{:S(2)}) collective-permute-start(bf16[8,48,1152]{2,1,0:T(8,128)(2,1)} %bitcast.97), channel_id=1, source_target_pairs={{0,1},{1,0},{2,3},{3,2},{4,5},{5,4},{6,7},{7,6},{8,9},{9,8},{10,11... | collective-permute-start | bytes 2654216 | tf_op jit(solution)/shard_map/ppermute | solution.py:767
  437.8 20.1 %collective-permute-start.66 = (bf16[256,1536]{1,0:T(8,128)(2,1)}, bf16[256,1536]{1,0:T(8,128)(2,1)}, u32[]{:S(2)}, u32[]{:S(2)}) collective-permute-start(bf16[256,1536]{1,0:T(8,128)(2,1)} %add.780), channel_id=1, source_target_pairs={{0,8},{4,12},{8,16},{12,20},{16,24},{20,28},{24,0},{28,4},{1,9},{5... | collective-permute-start | bytes 2359304 | tf_op jit(solution)/shard_map/ppermute | solution.py:761
  460.7 22.3 %collective-permute-start.70 = (bf16[2,288,768]{2,1,0:T(8,128)(2,1)}, bf16[2,288,768]{2,1,0:T(8,128)(2,1)S(1)}, u32[]{:S(2)}, u32[]{:S(2)}) collective-permute-start(bf16[2,288,768]{2,1,0:T(8,128)(2,1)} %get-tuple-element.668), channel_id=1, source_target_pairs={{0,1},{1,0},{2,3},{3,2},{4,5},{5,4},{6,7},{7,6},{8,9},{9,8},{10,11... | collective-permute-start | bytes 2654216 | tf_op jit(solution)/shard_map/ppermute | solution.py:767
  461.6 21.6 %collective-permute-start.71 = (bf16[2,288,768]{2,1,0:T(8,128)(2,1)S(1)}, bf16[2,288,768]{2,1,0:T(8,128)(2,1)S(1)}, u32[]{:S(2)}, u32[]{:S(2)}) collective-permute-start(bf16[2,288,768]{2,1,0:T(8,128)(2,1)S(1)} %copy-done.91), channel_id=1, source_target_pairs={{0,2},{1,3},{2,0},{3,1},{4,6},{5,7},{6,4},{7,5},{8,10},{9,11},{10,... | collective-permute-start | bytes 2654216 | tf_op jit(solution)/shard_map/ppermute | solution.py:767
  483.1 34.1 %collective-permute-start.74 = (bf16[8,48,1920]{2,1,0:T(8,128)(2,1)S(1)}, bf16[8,48,1920]{2,1,0:T(8,128)(2,1)S(1)}, u32[]{:S(2)}, u32[]{:S(2)}) collective-permute-start(bf16[8,48,1920]{2,1,0:T(8,128)(2,1)S(1)} %bitcast.219), channel_id=1, source_target_pairs={{0,1},{1,0},{2,3},{3,2},{4,5},{5,4},{6,7},{7,6},{8,9},{9,8},{10,11... | collective-permute-start | bytes 4423688 | tf_op jit(solution)/shard_map/ppermute | solution.py:767
  484.6 32.6 %collective-permute-start.75 = (bf16[8,48,1792]{2,1,0:T(8,128)(2,1)S(1)}, bf16[8,48,1792]{2,1,0:T(8,128)(2,1)S(1)}, u32[]{:S(2)}, u32[]{:S(2)}) collective-permute-start(bf16[8,48,1792]{2,1,0:T(8,128)(2,1)S(1)} %bitcast.220), channel_id=1, source_target_pairs={{0,2},{1,3},{2,0},{3,1},{4,6},{5,7},{6,4},{7,5},{8,10},{9,11},{10,... | collective-permute-start | bytes 4128776 | tf_op jit(solution)/shard_map/ppermute | solution.py:767
  485.2 14.9 %collective-permute-start.72 = (bf16[2,2,48,1152]{3,2,1,0:T(8,128)(2,1)}, bf16[2,2,48,1152]{3,2,1,0:T(8,128)(2,1)S(1)}, u32[]{:S(2)}, u32[]{:S(2)}) collective-permute-start(bf16[2,2,48,1152]{3,2,1,0:T(8,128)(2,1)} %copy-done.100), channel_id=1, source_target_pairs={{0,8},{4,12},{8,16},{12,20},{16,24},{20,28},{24,0},{28,4},{1,9},{5... | collective-permute-start | bytes 1327112 | tf_op jit(solution)/shard_map/ppermute | solution.py:761
  487.8 29.4 %collective-permute-start.73 = (bf16[2,2,48,1152]{3,2,1,0:T(8,128)(2,1)}, bf16[2,2,48,1152]{3,2,1,0:T(8,128)(2,1)S(1)}, u32[]{:S(2)}, u32[]{:S(2)}) collective-permute-start(bf16[2,2,48,1152]{3,2,1,0:T(8,128)(2,1)} %copy-done.99), channel_id=1, source_target_pairs={{0,16},{4,20},{8,24},{12,28},{16,0},{20,4},{24,8},{28,12},{1,17},{... | collective-permute-start | bytes 1327112 | tf_op jit(solution)/shard_map/ppermute | solution.py:761
  517.6 18.8 %collective-permute-start.78 = (bf16[4,48,1920]{2,1,0:T(8,128)(2,1)S(1)}, bf16[4,48,1920]{2,1,0:T(8,128)(2,1)S(1)}, u32[]{:S(2)}, u32[]{:S(2)}) collective-permute-start(bf16[4,48,1920]{2,1,0:T(8,128)(2,1)S(1)} %bitcast.223), channel_id=1, source_target_pairs={{0,2},{1,3},{2,0},{3,1},{4,6},{5,7},{6,4},{7,5},{8,10},{9,11},{10,... | collective-permute-start | bytes 2211848 | tf_op jit(solution)/shard_map/ppermute | solution.py:767
  519.3 16.9 %collective-permute-start.79 = (bf16[4,48,1792]{2,1,0:T(8,128)(2,1)S(1)}, bf16[4,48,1792]{2,1,0:T(8,128)(2,1)S(1)}, u32[]{:S(2)}, u32[]{:S(2)}) collective-permute-start(bf16[4,48,1792]{2,1,0:T(8,128)(2,1)S(1)} %bitcast.224), channel_id=1, source_target_pairs={{0,1},{1,0},{2,3},{3,2},{4,5},{5,4},{6,7},{7,6},{8,9},{9,8},{10,11... | collective-permute-start | bytes 2064392 | tf_op jit(solution)/shard_map/ppermute | solution.py:767
  520.0 16.5 %collective-permute-start.77 = (bf16[2,2,48,1152]{3,2,1,0:T(8,128)(2,1)S(1)}, bf16[2,2,48,1152]{3,2,1,0:T(8,128)(2,1)S(1)}, u32[]{:S(2)}, u32[]{:S(2)}) collective-permute-start(bf16[2,2,48,1152]{3,2,1,0:T(8,128)(2,1)S(1)} %copy-done.98), channel_id=1, source_target_pairs={{0,24},{4,28},{8,0},{12,4},{16,8},{20,12},{24,16},{28,20},{1,25},{... | collective-permute-start | bytes 1327112 | tf_op jit(solution)/shard_map/ppermute | solution.py:761
  536.6 25.9 %collective-permute-start.80 = (bf16[48,3712]{1,0:T(8,128)(2,1)S(1)}, bf16[48,3712]{1,0:T(8,128)(2,1)S(1)}, u32[]{:S(2)}, u32[]{:S(2)}) collective-permute-start(bf16[48,3712]{1,0:T(8,128)(2,1)S(1)} %pad_maximum_fusion.8), channel_id=1, source_target_pairs={{0,8},{4,12},{8,16},{12,20},{16,24},{20,28},{24,0},{28,4},{1,9},{5... | collective-permute-start | bytes 1069064 | tf_op jit(solution)/shard_map/ppermute | solution.py:761
  538.6 29.5 %collective-permute-start.81 = (bf16[48,3712]{1,0:T(8,128)(2,1)S(1)}, bf16[48,3712]{1,0:T(8,128)(2,1)S(1)}, u32[]{:S(2)}, u32[]{:S(2)}) collective-permute-start(bf16[48,3712]{1,0:T(8,128)(2,1)S(1)} %pad_maximum_fusion.9), channel_id=1, source_target_pairs={{0,16},{4,20},{8,24},{12,28},{16,0},{20,4},{24,8},{28,12},{1,17},{... | collective-permute-start | bytes 1069064 | tf_op jit(solution)/shard_map/ppermute | solution.py:761
  542.9 29.1 %collective-permute-start.82 = (bf16[48,3712]{1,0:T(8,128)(2,1)S(1)}, bf16[48,3712]{1,0:T(8,128)(2,1)S(1)}, u32[]{:S(2)}, u32[]{:S(2)}) collective-permute-start(bf16[48,3712]{1,0:T(8,128)(2,1)S(1)} %pad_maximum_fusion.10), channel_id=1, source_target_pairs={{0,24},{4,28},{8,0},{12,4},{16,8},{20,12},{24,16},{28,20},{1,25},{... | collective-permute-start | bytes 1069064 | tf_op jit(solution)/shard_map/ppermute | solution.py:761
  (149 other events, 1063.5 us)
Sparse Core Ops, SparseCore 0:
  32.6 93.9 all-gather.2
  129.0 78.3 all-gather.4

commit v3 on v1

--- a/solution.py
+++ b/solution.py
@@ -846,7 +846,9 @@
     core_side = core_at.reshape(1).astype(jnp.int32)
     chip_side = chip_at.reshape(1).astype(jnp.int32)
     bit_sides = {bit: ((dp_at // bit) % 2).reshape(1).astype(jnp.int32) for bit in bits}
-    cut_kept, cut_sent = cut_hidden(gate_up_master, core_side, n_chips, n_dp, ff_pad)
+    cut_kept, cut_sent = cut_hidden(
+        after(gate_up_master, qkv_ring[1]), core_side, n_chips, n_dp, ff_pad
+    )
     to_send = turn_pairs([cut_kept], [swap(cut_sent)], chip_side, n_chips)
     qkv_ring, to_send, cosine, sine = fence(qkv_ring, to_send, cosine, sine)
 

time: 580 us -> 587 us (1.012)
    unnamed x233 -> x229, local copies, waits for them, and re-layouts: 55.7 us -> 55.4 us
  transfers between devices with their start and end apart: 87 -> 87, of which waited for: 42 -> 43; matrix products, arithmetic and copies ran while one was open for 4% -> 4% of each run, Pallas kernels for 35% -> 35%
where the time goes in v3:
time: 587 us; the launch traced here: 580 us
  Pallas kernels  203 us (35%)
  waiting for transfers between devices  199 us (34%)
  starting transfers between devices  80.4 us (14%)
  local copies, waits for them, and re-layouts  61.8 us (11%)
  other arithmetic  20.5 us (3%)
  between operations  15.6 us (3%)
    pallas_call x44, Pallas kernels, kernel_call(): pl.pallas_call(kernel, name=name, out_shape=out_shape, compiler_params=pl...  203 us
    ppermute x61, waiting for transfers between devices, seq_perm(): lax.ppermute(values, 'seq', [(i, (i + 2 * chips) % count ^ flip) for i in...  142 us
    ppermute x24, waiting for transfers between devices, dp_perm(): lax.ppermute(values, 'dp', [(i, i ^ bit) for i in range(lax.axis_size('dp...  56.1 us
    unnamed x229, local copies, waits for them, and re-layouts  55.4 us
    ppermute x61, starting transfers between devices, seq_perm(): lax.ppermute(values, 'seq', [(i, (i + 2 * chips) % count ^ flip) for i in...  53.4 us
    ppermute x24, starting transfers between devices, dp_perm(): lax.ppermute(values, 'dp', [(i, i ^ bit) for i in range(lax.axis_size('dp...  26.9 us
  transfers between devices with their start and end apart: 87, of which 43 were waited for; matrix products, arithmetic and copies ran while one was open for 4% of the time, Pallas kernels for 35%

profile of v3, /device:TPU:8, one launch (start us, length us, event | category | flops | bytes accessed | tf_op | source)
XLA Modules:
  0.0 579.9 jit_solution(16545960551987834248)
XLA Ops:
  10.6 5.3 collective-permute-done.refs_1_
  19.7 2.6 collective-permute-start.1
  27.2 9.1 %collective-permute-done.1.refs_2_ = bf16[48,2176]{1,0:T(8,128)(2,1)S(1)} collective-permute-done((bf16[48,2176]{1,0:T(8,128)(2,1)S(1)}, bf16[48,2176]{1,0:T(8,128)(2,1)S(1)}, u32[]{:S(2)}, u32[]{:S(2)}) %collective-permute-start.1) | collective-permute-done | bytes 208928 | tf_op jit(solution)/shard_map/ppermute | solution.py:761
  40.5 9.4 %collective-permute-done.5 = bf16[4,48,1024]{2,1,0:T(8,128)(2,1)S(1)} collective-permute-done((bf16[4,48,1024]{2,1,0:T(8,128)(2,1)S(1)}, bf16[4,48,1024]{2,1,0:T(8,128)(2,1)S(1)}, u32[]{:S(2)}, u32[]{:S(2)}) %collective-permute-start.5) | collective-permute-done | bytes 393248 | tf_op jit(solution)/shard_map/ppermute | solution.py:767
  49.8 2.1 collective-permute-done.6
  56.5 8.9 %collective-permute-done.9 = bf16[2,2,48,1152]{3,2,1,0:T(8,128)(2,1)S(1)} collective-permute-done((bf16[2,2,48,1152]{3,2,1,0:T(8,128)(2,1)S(1)}, bf16[2,2,48,1152]{3,2,1,0:T(8,128)(2,1)S(1)}, u32[]{:S(2)}, u32[]{:S(2)}) %collective-permute-start.9) | collective-permute-done | bytes 442400 | tf_op jit(solution)/shard_map/ppermute | solution.py:761
  65.5 6.1 %collective-permute-done.8.refs_5_ = bf16[8,48,1024]{2,1,0:T(8,128)(2,1)} collective-permute-done((bf16[8,48,1024]{2,1,0:T(8,128)(2,1)S(1)}, bf16[8,48,1024]{2,1,0:T(8,128)(2,1)}, u32[]{:S(2)}, u32[]{:S(2)}) %collective-permute-start.8) | collective-permute-done | bytes 786464 | tf_op jit(solution)/shard_map/ppermute | solution.py:767
  73.0 2.6 collective-permute-start.14
  80.6 18.1 %collective-permute-done.14 = bf16[2,2,48,1152]{3,2,1,0:T(8,128)(2,1)} collective-permute-done((bf16[2,2,48,1152]{3,2,1,0:T(8,128)(2,1)}, bf16[2,2,48,1152]{3,2,1,0:T(8,128)(2,1)}, u32[]{:S(2)}, u32[]{:S(2)}) %collective-permute-start.14) | collective-permute-done | bytes 442400 | tf_op jit(solution)/shard_map/ppermute | solution.py:761
  100.0 4.7 assemble.2
  104.7 2.6 copy-done.7
  108.7 3.3 project_kv.1
  116.0 3.9 collective-permute-start.16
  120.0 5.0 collective-permute-done.15.refs_2_
  125.0 5.1 project_q.1.q_ref
  130.1 9.9 %collective-permute-done.16.refs_4_ = bf16[256,512]{1,0:T(8,128)(2,1)S(1)} collective-permute-done((bf16[256,512]{1,0:T(8,128)(2,1)}, bf16[256,512]{1,0:T(8,128)(2,1)S(1)}, u32[]{:S(2)}, u32[]{:S(2)}) %collective-permute-start.16) | collective-permute-done | bytes 262176 | tf_op jit(solution)/shard_map/ppermute | solution.py:761
  140.0 2.2 collective-permute-done.17.refs_6_
  154.6 11.5 %attend.1 = (f32[256,1536]{1,0:T(8,128)S(1)}, f32[12,256]{1,0:T(8,128)S(1)}, bf16[2048,512]{1,0:T(8,128)(2,1)S(1)}) custom-call(s32[2]{0:T(128)S(1)} %slice_bitcast_fusion.1.query_bases, s32[16]{0:T(128)S(1)} %select_n.83.key_bases, bf16[256,1536]{1,0:T(8,128)(2,1)S(1)} %copy-done.13, bf16[256,512]{1,0:T(8,128)(2,1)S(1)} %copy-done.64, ...), custom_call_target="tpu_custom_call" | custom-call | flops 1000000 | bytes 1000000 | tf_op jit(solution)/shard_map/attend/pallas_call | solution.py:38
  168.5 13.9 %collective-permute-done.24 = bf16[4,2,48,1152]{3,2,1,0:T(8,128)(2,1)} collective-permute-done((bf16[4,2,48,1152]{3,2,1,0:T(8,128)(2,1)S(1)}, bf16[4,2,48,1152]{3,2,1,0:T(8,128)(2,1)}, u32[]{:S(2)}, u32[]{:S(2)}) %collective-permute-start.24) | collective-permute-done | bytes 884768 | tf_op jit(solution)/shard_map/ppermute | solution.py:767
  182.4 2.3 collective-permute-done.25
  187.2 2.3 copy-done.8
  190.9 2.4 out_project.1
  194.3 7.7 %collective-permute-done.29.grad_own = bf16[256,1536]{1,0:T(8,128)(2,1)} collective-permute-done((bf16[256,1536]{1,0:T(8,128)(2,1)}, bf16[256,1536]{1,0:T(8,128)(2,1)}, u32[]{:S(2)}, u32[]{:S(2)}) %collective-permute-start.29) | collective-permute-done | bytes 786464 | tf_op jit(solution)/shard_map/ppermute | solution.py:761
  202.6 3.0 collective-permute-done.27
  212.0 5.5 assemble.3
  217.5 2.9 copy-done
  220.5 2.0 copy-done.6
  223.6 17.2 %feed_forward.4 = (bf16[256,1536]{1,0:T(8,128)(2,1)S(1)}, bf16[256,1536]{1,0:T(8,128)(2,1)S(1)}, bf16[256,1536]{1,0:T(8,128)(2,1)S(1)}, bf16[256,1536]{1,0:T(8,1...) custom-call(bf16[256,1536]{1,0:T(8,128)(2,1)} %get-tuple-element.452, ...), custom_call_target="tpu_custom_call" | custom-call | flops 1000000 | bytes 1000000 | tf_op jit(solution)/shard_map/feed_forward/pallas_call | solution.py:38
  243.9 2.0 collective-permute-done.36.grad_other
  247.7 17.3 %feed_forward.5 = (bf16[256,1536]{1,0:T(8,128)(2,1)S(1)}, bf16[256,1536]{1,0:T(8,128)(2,1)S(1)}, bf16[256,1536]{1,0:T(8,128)(2,1)S(1)}, bf16[256,1536]{1,0:T(8,1...) custom-call(bf16[256,1536]{1,0:T(8,128)(2,1)} %collective-permute-do, ...), custom_call_target="tpu_custom_call", output_to_operand_aliasing={{4}: (6, {}), {5}: (7, {}), {6}: (8, {}), {7}: (9, {}), {8}... | custom-call | flops 1000000 | bytes 1000000 | tf_op jit(solution)/shard_map/feed_forward/pallas_call | solution.py:38
  269.6 2.5 collective-permute-start.43
  272.9 16.9 %feed_forward.6 = (bf16[256,1536]{1,0:T(8,128)(2,1)S(1)}, bf16[256,1536]{1,0:T(8,128)(2,1)}, bf16[256,1536]{1,0:T(8,128)(2,1)S(1)}, bf16[256,1536]{1,0:T(8,128)(...) custom-call(bf16[256,1536]{1,0:T(8,128)(2,1)S(1)} %collective-permut, ...), custom_call_target="tpu_custom_call", output_to_operand_aliasing={{4}: (6, {}), {5}: (7, {}), {6}: (8, {}), {7}: (9, {}), {8}... | custom-call | flops 1000000 | bytes 1000000 | tf_op jit(solution)/shard_map/feed_forward/pallas_call | solution.py:38
  290.6 15.9 %collective-permute-done.42.refs_2_ = bf16[256,1536]{1,0:T(8,128)(2,1)S(1)} collective-permute-done((bf16[256,1536]{1,0:T(8,128)(2,1)S(1)}, bf16[256,1536]{1,0:T(8,128)(2,1)S(1)}, u32[]{:S(2)}, u32[]{:S(2)}) %collective-permute-start.42) | collective-permute-done | bytes 786464 | tf_op jit(solution)/shard_map/ppermute | solution.py:761
  306.8 2.6 collective-permute-start.46
  309.4 16.8 %feed_forward.7 = (bf16[256,1536]{1,0:T(8,128)(2,1)S(1)}, bf16[256,1536]{1,0:T(8,128)(2,1)}, bf16[256,1536]{1,0:T(8,128)(2,1)S(1)}, bf16[256,1536]{1,0:T(8,128)(...) custom-call(bf16[256,1536]{1,0:T(8,128)(2,1)S(1)} %collective-permut, ...), custom_call_target="tpu_custom_call", output_to_operand_aliasing={{4}: (6, {}), {5}: (7, {}), {6}: (8, {}), {7}: (9, {}), {8}... | custom-call | flops 1000000 | bytes 1000000 | tf_op jit(solution)/shard_map/feed_forward/pallas_call | solution.py:38
  326.2 2.2 copy-done.5
  331.9 3.6 collective-permute-start.47
  335.5 2.8 copy-done.1
  338.3 2.3 copy-done.3
  340.6 2.3 copy-done.4
  343.0 12.4 %weight_grad.6 = (bf16[8,1,48,1152]{3,2,1,0:T(8,128)(2,1)S(1)}, bf16[8,1,48,1152]{3,2,1,0:T(8,128)(2,1)}, bf16[4,2,48,1152]{3,2,1,0:T(8,128)(2,1)S(1)}, bf16[4,2,48,1152]{3,2,1,0:T(8,128)(2,1)}) custom-call(s32[2]{0:T(128)S(1)} %pad_add_fusion.8.sides, bf16[4,512,1536]{2,1,0:T(8,128)(2,1)S(1)} %copy-done.1, bf16[4,512,1152]{2,1,0:T(8,128)(2,1)S(1)} %copy-done.3, ...), custom_call_target="tpu_custom_call" | custom-call | flops 1000000 | bytes 1000000 | tf_op jit(solution)/shard_map/weight_grad/pallas_call | solution.py:38
  355.4 11.6 %weight_grad.7 = (bf16[8,1,48,1152]{3,2,1,0:T(8,128)(2,1)S(1)}, bf16[8,1,48,1152]{3,2,1,0:T(8,128)(2,1)S(1)}, bf16[4,2,48,1152]{3,2,1,0:T(8,128)(2,1)S(1)}, bf16[4,2,48,1152]{3,2,1,0:T(8,128)(2,1)S(1)}) custom-call(s32[2]{0:T(128)S(1)} %pad_add_fusion.8.sides, bf16[4,512,1536]{2,1,0:T(8,128)(2,1)S(1)} %copy-done.1, bf16[4,512,1152]{2,1,0:T(8,128)(2,1)S(1)} %copy-done.3, ...), custom_call_target="tpu_custom_call" | custom-call | flops 1000000 | bytes 1000000 | tf_op jit(solution)/shard_map/weight_grad/pallas_call | solution.py:38
  374.2 3.5 norm_back.1
  378.7 21.0 %attend_back.1 = (bf16[256,1536]{1,0:T(8,128)(2,1)S(1)}, bf16[1024,512]{1,0:T(8,128)(2,1)S(1)}, bf16[1024,512]{1,0:T(8,128)(2,1)S(1)}) custom-call(s32[2]{0:T(128)S(1)} %copy-done.70, s32[16]{0:T(128)S(1)} %select_n.83.key_bases, bf16[256,1536]{1,0:T(8,128)(2,1)S(1)} %copy-done.14, bf16[2048,512]{1,0:T(8,128)(2,1)S(1)} %copy-done.33, ...), custom_call_target="tpu_custom_call" | custom-call | flops 1000000 | bytes 1000000 | tf_op jit(solution)/shard_map/attend_back/pallas_call | solution.py:38
  400.0 2.5 collective-permute-done.56
  411.5 3.9 weight_grad.8
  417.0 3.6 weight_grad.9
  422.0 8.4 %weight_grad.10 = bf16[1152,1536]{1,0:T(8,128)(2,1)S(1)} custom-call(s32[1]{0:T(128)} %constant.163.clone.1.chip.sides, bf16[4,512,1152]{2,1,0:T(8,128)(2,1)S(1)} %bitcast.168, bf16[4,512,1536]{2,1,0:T(8,128)(2,1)S(1)} %bitcast.166), custom_call_target="tpu_custom_call" | custom-call | flops 1000000 | bytes 1000000 | tf_op jit(solution)/shard_map/weight_grad/pallas_call | solution.py:38
  443.7 7.6 %input_back.1 = (bf16[256,512]{1,0:T(8,128)(2,1)}, f32[256,1536]{1,0:T(8,128)}, f32[1,1536]{1,0:T(1,128)}, f32[1,2048]{1,0:T(1,128)}) custom-call(bf16[256,1536]{1,0:T(8,128)(2,1)} %bitcast.178, f32[1,1536]{1,0:T(1,128)} %get-tuple-element.773.gain, bf16[1536,2048]{1,0:T(8,128)(2,1)} %bitcast.171, bf16[256,1536]{1,0:T(8,128)(2,1)} %copy-done.27, ...), custom_call_target="tpu_custom_call" | custom-call | flops 1000000 | bytes 1000000 | tf_op jit(solution)/shard_map/input_back/pallas_call | solution.py:38
  453.8 3.1 collective-permute-done.66
  469.9 2.5 add_halve.14
  472.4 2.4 add_halve.15
  474.9 6.8 %collective-permute-done.70 = bf16[2,288,768]{2,1,0:T(8,128)(2,1)S(1)} collective-permute-done((bf16[2,288,768]{2,1,0:T(8,128)(2,1)S(1)}, bf16[2,288,768]{2,1,0:T(8,128)(2,1)S(1)}, u32[]{:S(2)}, u32[]{:S(2)}) %collective-permute-start.70) | collective-permute-done | bytes 884768 | tf_op jit(solution)/shard_map/ppermute | solution.py:767
  489.2 17.4 %collective-permute-done.72.refs_1_ = bf16[2,2,48,1152]{3,2,1,0:T(8,128)(2,1)S(1)} collective-permute-done((bf16[2,2,48,1152]{3,2,1,0:T(8,128)(2,1)S(1)}, bf16[2,2,48,1152]{3,2,1,0:T(8,128)(2,1)S(1)}, u32[]{:S(2)}, u32[]{:S(2)}) %collective-permute-start.72) | collective-permute-done | bytes 442400 | tf_op jit(solution)/shard_map/ppermute | solution.py:761
  506.6 9.2 %collective-permute-done.73.refs_2_ = bf16[2,2,48,1152]{3,2,1,0:T(8,128)(2,1)S(1)} collective-permute-done((bf16[2,2,48,1152]{3,2,1,0:T(8,128)(2,1)S(1)}, bf16[2,2,48,1152]{3,2,1,0:T(8,128)(2,1)S(1)}, u32[]{:S(2)}, u32[]{:S(2)}) %collective-permute-start.73) | collective-permute-done | bytes 442400 | tf_op jit(solution)/shard_map/ppermute | solution.py:761
  518.7 3.5 collective-permute-start.77
  522.3 2.6 fusion.1
  524.8 9.0 %collective-permute-done.79.got = bf16[4,48,1792]{2,1,0:T(8,128)(2,1)S(1)} collective-permute-done((bf16[4,48,1792]{2,1,0:T(8,128)(2,1)S(1)}, bf16[4,48,1792]{2,1,0:T(8,128)(2,1)S(1)}, u32[]{:S(2)}, u32[]{:S(2)}) %collective-permute-start.79) | collective-permute-done | bytes 688160 | tf_op jit(solution)/shard_map/ppermute | solution.py:767
  536.4 4.4 collective-permute-start.81
  543.0 7.6 %adamw_hidden.1 = (f32[2,48,8960]{2,1,0:T(8,128)}, f32[2,48,8960]{2,1,0:T(8,128)}, f32[2,48,8960]{2,1,0:T(8,128)}) custom-call(s32[8]{0:T(128)S(1)} %stack.261.where, f32[2,48,8960]{2,1,0:T(8,128)S(1)} %copy-done.10, f32[2,48,8960]{2,1,0:T(8,128)S(1)} %copy-done.23, f32[2,48,8960]{2,1,0:T(8,128)} %second.1, ...), custom_call_target="tpu_custom_call" | custom-call | flops 1000000 | bytes 1000000 | tf_op jit(solution)/shard_map/adamw_hidden/pallas_call | solution.py:38
  552.6 3.2 multiply_subtract_fusion
  555.8 4.5 collective-permute-done.80
  560.3 5.4 collective-permute-done.81
  565.6 4.0 collective-permute-done.82
  (473 shorter events, 145.4 us)
Async XLA Ops:
  7.2 180.0 %all-gather.3.cloned.1.call-start = ((), (), s32[]{:S(2)}) async-start(), calls=%async_computation | async-start | bytes 4866048 | tf_op jit(solution)/shard_map/all_gather | solution.py:858
  19.7 16.5 %collective-permute-start.1 = (bf16[48,2176]{1,0:T(8,128)(2,1)S(1)}, bf16[48,2176]{1,0:T(8,128)(2,1)S(1)}, u32[]{:S(2)}, u32[]{:S(2)}) collective-permute-start(bf16[48,2176]{1,0:T(8,128)(2,1)S(1)} %pad_maximum_fusion.11.refs_0_), channel_id=1, source_target_pairs={{0,16},{4,20},{8,24},{12,28},{16,0},{20,4},{24,8},{28,12},{1,17},{... | collective-permute-start | bytes 626696 | tf_op jit(solution)/shard_map/ppermute | solution.py:761
  22.3 14.9 %collective-permute-start.2 = (bf16[48,2176]{1,0:T(8,128)(2,1)S(1)}, bf16[48,2176]{1,0:T(8,128)(2,1)S(1)}, u32[]{:S(2)}, u32[]{:S(2)}) collective-permute-start(bf16[48,2176]{1,0:T(8,128)(2,1)S(1)} %pad_maximum_fusion.11.refs_0_), channel_id=1, source_target_pairs={{0,24},{4,28},{8,0},{12,4},{16,8},{20,12},{24,16},{28,20},{1,25},{... | collective-permute-start | bytes 626696 | tf_op jit(solution)/shard_map/ppermute | solution.py:761
  37.2 183.2 %all-gather.5.cloned.1.call-start = ((), (), s32[]{:S(2)}) async-start(), calls=%async_computation.1 | async-start | bytes 4423680 | tf_op jit(solution)/shard_map/all_gather | solution.py:882
  37.4 12.5 %collective-permute-start.4 = (bf16[4,48,1152]{2,1,0:T(8,128)(2,1)S(1)}, bf16[4,48,1152]{2,1,0:T(8,128)(2,1)S(1)}, u32[]{:S(2)}, u32[]{:S(2)}) collective-permute-start(bf16[4,48,1152]{2,1,0:T(8,128)(2,1)S(1)} %get-tuple-element.392), channel_id=1, source_target_pairs={{0,1},{1,0},{2,3},{3,2},{4,5},{5,4},{6,7},{7,6},{8,9},{9,8},{10,11... | collective-permute-start | bytes 1327112 | tf_op jit(solution)/shard_map/ppermute | solution.py:767
  38.9 13.0 %collective-permute-start.6 = (bf16[2,2,48,1152]{3,2,1,0:T(8,128)(2,1)S(1)}, bf16[2,2,48,1152]{3,2,1,0:T(8,128)(2,1)}, u32[]{:S(2)}, u32[]{:S(2)}) collective-permute-start(bf16[2,2,48,1152]{3,2,1,0:T(8,128)(2,1)S(1)} %get-tuple-element.391), channel_id=1, source_target_pairs={{0,8},{4,12},{8,16},{12,20},{16,24},{20,28},{24,0},{28,4},{1,9},{5... | collective-permute-start | bytes 1327112 | tf_op jit(solution)/shard_map/ppermute | solution.py:761
  52.0 20.5 %collective-permute-start.7 = (bf16[8,48,1152]{2,1,0:T(8,128)(2,1)S(1)}, bf16[8,48,1152]{2,1,0:T(8,128)(2,1)}, u32[]{:S(2)}, u32[]{:S(2)}) collective-permute-start(bf16[8,48,1152]{2,1,0:T(8,128)(2,1)S(1)} %constant_dynamic-update-slice_fusion.refs_0_), channel_id=1, source_target_pairs={{0,2},{1,3},{2,0},{3,1},{4,6},{5,7},{6,4},{7,5},{8,10},{9,11},{10,... | collective-permute-start | bytes 2654216 | tf_op jit(solution)/shard_map/ppermute | solution.py:767
  53.7 17.9 %collective-permute-start.8 = (bf16[8,48,1024]{2,1,0:T(8,128)(2,1)S(1)}, bf16[8,48,1024]{2,1,0:T(8,128)(2,1)}, u32[]{:S(2)}, u32[]{:S(2)}) collective-permute-start(bf16[8,48,1024]{2,1,0:T(8,128)(2,1)S(1)} %constant_dynamic-update-slice_fusion.2.refs_4_), channel_id=1, source_target_pairs={{0,1},{1,0},{2,3},{3,2},{4,5},{5,4},{6,7},{7,6},{8,9},{9,8},{10,11... | collective-permute-start | bytes 2359304 | tf_op jit(solution)/shard_map/ppermute | solution.py:767
  56.0 24.6 %collective-permute-start.10 = (bf16[8,48,1152]{2,1,0:T(8,128)(2,1)S(1)}, bf16[8,48,1152]{2,1,0:T(8,128)(2,1)}, u32[]{:S(2)}, u32[]{:S(2)}) collective-permute-start(bf16[8,48,1152]{2,1,0:T(8,128)(2,1)S(1)} %constant_dynamic-update-slice_fusion.refs_0_), channel_id=1, source_target_pairs={{0,4},{4,0},{8,12},{12,8},{16,20},{20,16},{24,28},{28,24},{1,5},{5... | collective-permute-start | bytes 2654216 | tf_op jit(solution)/shard_map/ppermute | solution.py:761
  56.0 23.7 %collective-permute-start.11 = (bf16[8,48,1024]{2,1,0:T(8,128)(2,1)S(1)}, bf16[8,48,1024]{2,1,0:T(8,128)(2,1)S(1)}, u32[]{:S(2)}, u32[]{:S(2)}) collective-permute-start(bf16[8,48,1024]{2,1,0:T(8,128)(2,1)S(1)} %constant_dynamic-update-slice_fusion.2.refs_4_), channel_id=1, source_target_pairs={{0,4},{4,0},{8,12},{12,8},{16,20},{20,16},{24,28},{28,24},{1,5},{5... | collective-permute-start | bytes 2359304 | tf_op jit(solution)/shard_map/ppermute | solution.py:761
  72.5 27.4 %collective-permute-start.12 = (bf16[8,48,1152]{2,1,0:T(8,128)(2,1)}, bf16[8,48,1152]{2,1,0:T(8,128)(2,1)}, u32[]{:S(2)}, u32[]{:S(2)}) collective-permute-start(bf16[8,48,1152]{2,1,0:T(8,128)(2,1)} %collective-permute-done.7.refs_1_), channel_id=1, source_target_pairs={{0,4},{4,0},{8,12},{12,8},{16,20},{20,16},{24,28},{28,24},{1,5},{5... | collective-permute-start | bytes 2654216 | tf_op jit(solution)/shard_map/ppermute | solution.py:761
  72.5 27.4 %collective-permute-start.13 = (bf16[8,48,1024]{2,1,0:T(8,128)(2,1)}, bf16[8,48,1024]{2,1,0:T(8,128)(2,1)}, u32[]{:S(2)}, u32[]{:S(2)}) collective-permute-start(bf16[8,48,1024]{2,1,0:T(8,128)(2,1)} %collective-permute-done.8.refs_5_), channel_id=1, source_target_pairs={{0,4},{4,0},{8,12},{12,8},{16,20},{20,16},{24,28},{28,24},{1,5},{5... | collective-permute-start | bytes 2359304 | tf_op jit(solution)/shard_map/ppermute | solution.py:761
  73.0 25.6 %collective-permute-start.14 = (bf16[2,2,48,1152]{3,2,1,0:T(8,128)(2,1)}, bf16[2,2,48,1152]{3,2,1,0:T(8,128)(2,1)}, u32[]{:S(2)}, u32[]{:S(2)}) collective-permute-start(bf16[2,2,48,1152]{3,2,1,0:T(8,128)(2,1)} %get-tuple-element.413), channel_id=1, source_target_pairs={{0,16},{4,20},{8,24},{12,28},{16,0},{20,4},{24,8},{28,12},{1,17},{... | collective-permute-start | bytes 1327112 | tf_op jit(solution)/shard_map/ppermute | solution.py:761
  112.0 33.7 %collective-permute-start.22 = (bf16[4,2,48,1152]{3,2,1,0:T(8,128)(2,1)S(1)}, bf16[4,2,48,1152]{3,2,1,0:T(8,128)(2,1)}, u32[]{:S(2)}, u32[]{:S(2)}) collective-permute-start(bf16[4,2,48,1152]{3,2,1,0:T(8,128)(2,1)S(1)} %pad_maximum_fusion.4), channel_id=1, source_target_pairs={{0,1},{1,0},{2,3},{3,2},{4,5},{5,4},{6,7},{7,6},{8,9},{9,8},{10,11... | collective-permute-start | bytes 2654216 | tf_op jit(solution)/shard_map/ppermute | solution.py:767
  113.6 32.1 %collective-permute-start.23 = (bf16[4,2,48,1152]{3,2,1,0:T(8,128)(2,1)S(1)}, bf16[4,2,48,1152]{3,2,1,0:T(8,128)(2,1)}, u32[]{:S(2)}, u32[]{:S(2)}) collective-permute-start(bf16[4,2,48,1152]{3,2,1,0:T(8,128)(2,1)S(1)} %pad_maximum_fusion.5), channel_id=1, source_target_pairs={{0,2},{1,3},{2,0},{3,1},{4,6},{5,7},{6,4},{7,5},{8,10},{9,11},{10,... | collective-permute-start | bytes 2654216 | tf_op jit(solution)/shard_map/ppermute | solution.py:767
  116.0 23.9 %collective-permute-start.16 = (bf16[256,512]{1,0:T(8,128)(2,1)}, bf16[256,512]{1,0:T(8,128)(2,1)S(1)}, u32[]{:S(2)}, u32[]{:S(2)}) collective-permute-start(bf16[256,512]{1,0:T(8,128)(2,1)} %get-tuple-element.428.refs_0_), channel_id=1, source_target_pairs={{0,16},{4,20},{8,24},{12,28},{16,0},{20,4},{24,8},{28,12},{1,17},{... | collective-permute-start | bytes 786440 | tf_op jit(solution)/shard_map/ppermute | solution.py:761
  119.9 22.3 %collective-permute-start.17 = (bf16[256,512]{1,0:T(8,128)(2,1)}, bf16[256,512]{1,0:T(8,128)(2,1)}, u32[]{:S(2)}, u32[]{:S(2)}) collective-permute-start(bf16[256,512]{1,0:T(8,128)(2,1)} %get-tuple-element.428.refs_0_), channel_id=1, source_target_pairs={{0,24},{4,28},{8,0},{12,4},{16,8},{20,12},{24,16},{28,20},{1,25},{... | collective-permute-start | bytes 786440 | tf_op jit(solution)/shard_map/ppermute | solution.py:761
  125.0 17.9 %collective-permute-start.18 = (bf16[256,512]{1,0:T(8,128)(2,1)}, bf16[256,512]{1,0:T(8,128)(2,1)S(1)}, u32[]{:S(2)}, u32[]{:S(2)}) collective-permute-start(bf16[256,512]{1,0:T(8,128)(2,1)} %get-tuple-element.428.refs_0_), channel_id=1, source_target_pairs={{0,4},{4,0},{8,12},{12,8},{16,20},{20,16},{24,28},{28,24},{1,5},{5... | collective-permute-start | bytes 786440 | tf_op jit(solution)/shard_map/ppermute | solution.py:761
  145.6 36.7 %collective-permute-start.24 = (bf16[4,2,48,1152]{3,2,1,0:T(8,128)(2,1)S(1)}, bf16[4,2,48,1152]{3,2,1,0:T(8,128)(2,1)}, u32[]{:S(2)}, u32[]{:S(2)}) collective-permute-start(bf16[4,2,48,1152]{3,2,1,0:T(8,128)(2,1)S(1)} %pad_maximum_fusion.4), channel_id=1, source_target_pairs={{0,2},{1,3},{2,0},{3,1},{4,6},{5,7},{6,4},{7,5},{8,10},{9,11},{10,... | collective-permute-start | bytes 2654216 | tf_op jit(solution)/shard_map/ppermute | solution.py:767
  146.9 37.8 %collective-permute-start.25 = (bf16[4,2,48,1152]{3,2,1,0:T(8,128)(2,1)S(1)}, bf16[4,2,48,1152]{3,2,1,0:T(8,128)(2,1)}, u32[]{:S(2)}, u32[]{:S(2)}) collective-permute-start(bf16[4,2,48,1152]{3,2,1,0:T(8,128)(2,1)S(1)} %pad_maximum_fusion.5), channel_id=1, source_target_pairs={{0,1},{1,0},{2,3},{3,2},{4,5},{5,4},{6,7},{7,6},{8,9},{9,8},{10,11... | collective-permute-start | bytes 2654216 | tf_op jit(solution)/shard_map/ppermute | solution.py:767
  147.5 21.0 %collective-permute-start.26 = (bf16[256,1536]{1,0:T(8,128)(2,1)}, bf16[256,1536]{1,0:T(8,128)(2,1)}, u32[]{:S(2)}, u32[]{:S(2)}) collective-permute-start(bf16[256,1536]{1,0:T(8,128)(2,1)} %bitcast.186), channel_id=1, source_target_pairs={{0,8},{4,12},{8,16},{12,20},{16,24},{20,28},{24,0},{28,4},{1,9},{5... | collective-permute-start | bytes 2359304 | tf_op jit(solution)/shard_map/ppermute | solution.py:761
  184.7 17.3 %collective-permute-start.29 = (bf16[256,1536]{1,0:T(8,128)(2,1)}, bf16[256,1536]{1,0:T(8,128)(2,1)}, u32[]{:S(2)}, u32[]{:S(2)}) collective-permute-start(bf16[256,1536]{1,0:T(8,128)(2,1)} %collective-permute-done.26.grad_own), channel_id=1, source_target_pairs={{0,8},{4,12},{8,16},{12,20},{16,24},{20,28},{24,0},{28,4},{1,9},{5... | collective-permute-start | bytes 2359304 | tf_op jit(solution)/shard_map/ppermute | solution.py:761
  184.7 20.9 %collective-permute-start.27 = (bf16[4,2,48,1152]{3,2,1,0:T(8,128)(2,1)}, bf16[4,2,48,1152]{3,2,1,0:T(8,128)(2,1)}, u32[]{:S(2)}, u32[]{:S(2)}) collective-permute-start(bf16[4,2,48,1152]{3,2,1,0:T(8,128)(2,1)} %collective-permute-done.22), channel_id=1, source_target_pairs={{0,2},{1,3},{2,0},{3,1},{4,6},{5,7},{6,4},{7,5},{8,10},{9,11},{10,... | collective-permute-start | bytes 2654216 | tf_op jit(solution)/shard_map/ppermute | solution.py:767
  184.7 21.8 %collective-permute-start.28 = (bf16[4,2,48,1152]{3,2,1,0:T(8,128)(2,1)}, bf16[4,2,48,1152]{3,2,1,0:T(8,128)(2,1)}, u32[]{:S(2)}, u32[]{:S(2)}) collective-permute-start(bf16[4,2,48,1152]{3,2,1,0:T(8,128)(2,1)} %collective-permute-done.23), channel_id=1, source_target_pairs={{0,1},{1,0},{2,3},{3,2},{4,5},{5,4},{6,7},{7,6},{8,9},{9,8},{10,11... | collective-permute-start | bytes 2654216 | tf_op jit(solution)/shard_map/ppermute | solution.py:767
  186.7 16.0 %collective-permute-start.31 = (bf16[256,1536]{1,0:T(8,128)(2,1)}, bf16[256,1536]{1,0:T(8,128)(2,1)}, u32[]{:S(2)}, u32[]{:S(2)}) collective-permute-start(bf16[256,1536]{1,0:T(8,128)(2,1)} %collective-permute-done.26.grad_own), channel_id=1, source_target_pairs={{0,4},{4,0},{8,12},{12,8},{16,20},{20,16},{24,28},{28,24},{1,5},{5... | collective-permute-start | bytes 2359304 | tf_op jit(solution)/shard_map/ppermute | solution.py:761
  186.7 15.9 %collective-permute-start.30 = (bf16[256,1536]{1,0:T(8,128)(2,1)}, bf16[256,1536]{1,0:T(8,128)(2,1)}, u32[]{:S(2)}, u32[]{:S(2)}) collective-permute-start(bf16[256,1536]{1,0:T(8,128)(2,1)} %bitcast.187), channel_id=1, source_target_pairs={{0,4},{4,0},{8,12},{12,8},{16,20},{20,16},{24,28},{28,24},{1,5},{5... | collective-permute-start | bytes 2359304 | tf_op jit(solution)/shard_map/ppermute | solution.py:761
  207.5 36.0 %collective-permute-start.33 = (bf16[256,1536]{1,0:T(8,128)(2,1)}, bf16[256,1536]{1,0:T(8,128)(2,1)}, u32[]{:S(2)}, u32[]{:S(2)}) collective-permute-start(bf16[256,1536]{1,0:T(8,128)(2,1)} %get-tuple-element.452.normed_own), channel_id=1, source_target_pairs={{0,8},{4,12},{8,16},{12,20},{16,24},{20,28},{24,0},{28,4},{1,9},{5... | collective-permute-start | bytes 2359304 | tf_op jit(solution)/shard_map/ppermute | solution.py:761
  209.1 34.8 %collective-permute-start.35 = (bf16[256,1536]{1,0:T(8,128)(2,1)}, bf16[256,1536]{1,0:T(8,128)(2,1)}, u32[]{:S(2)}, u32[]{:S(2)}) collective-permute-start(bf16[256,1536]{1,0:T(8,128)(2,1)} %collective-permute-done.29.grad_own), channel_id=1, source_target_pairs={{0,8},{4,12},{8,16},{12,20},{16,24},{20,28},{24,0},{28,4},{1,9},{5... | collective-permute-start | bytes 2359304 | tf_op jit(solution)/shard_map/ppermute | solution.py:761
  247.1 19.9 %collective-permute-start.38 = (bf16[256,1536]{1,0:T(8,128)(2,1)}, bf16[256,1536]{1,0:T(8,128)(2,1)S(1)}, u32[]{:S(2)}, u32[]{:S(2)}) collective-permute-start(bf16[256,1536]{1,0:T(8,128)(2,1)} %collective-permute-done.33.normed_own), channel_id=1, source_target_pairs={{0,8},{4,12},{8,16},{12,20},{16,24},{20,28},{24,0},{28,4},{1,9},{5... | collective-permute-start | bytes 2359304 | tf_op jit(solution)/shard_map/ppermute | solution.py:761
  269.6 20.5 %collective-permute-start.43 = (bf16[256,1536]{1,0:T(8,128)(2,1)S(1)}, bf16[256,1536]{1,0:T(8,128)(2,1)S(1)}, u32[]{:S(2)}, u32[]{:S(2)}) collective-permute-start(bf16[256,1536]{1,0:T(8,128)(2,1)S(1)} %collective-permute-done.38.normed_own), channel_id=1, source_target_pairs={{0,8},{4,12},{8,16},{12,20},{16,24},{20,28},{24,0},{28,4},{1,9},{5... | collective-permute-start | bytes 2359304 | tf_op jit(solution)/shard_map/ppermute | solution.py:761
  272.1 34.3 %collective-permute-start.42 = (bf16[256,1536]{1,0:T(8,128)(2,1)S(1)}, bf16[256,1536]{1,0:T(8,128)(2,1)S(1)}, u32[]{:S(2)}, u32[]{:S(2)}) collective-permute-start(bf16[256,1536]{1,0:T(8,128)(2,1)S(1)} %add.775), channel_id=1, source_target_pairs={{0,8},{4,12},{8,16},{12,20},{16,24},{20,28},{24,0},{28,4},{1,9},{5... | collective-permute-start | bytes 2359304 | tf_op jit(solution)/shard_map/ppermute | solution.py:761
  289.9 16.6 %collective-permute-start.41 = (bf16[256,1536]{1,0:T(8,128)(2,1)S(1)}, bf16[256,1536]{1,0:T(8,128)(2,1)S(1)}, u32[]{:S(2)}, u32[]{:S(2)}) collective-permute-start(bf16[256,1536]{1,0:T(8,128)(2,1)S(1)} %get-tuple-element.507), channel_id=1, source_target_pairs={{0,4},{4,0},{8,12},{12,8},{16,20},{20,16},{24,28},{28,24},{1,5},{5... | collective-permute-start | bytes 2359304 | tf_op jit(solution)/shard_map/ppermute | solution.py:761
  290.1 16.7 %collective-permute-start.44 = (bf16[256,1536]{1,0:T(8,128)(2,1)S(1)}, bf16[256,1536]{1,0:T(8,128)(2,1)S(1)}, u32[]{:S(2)}, u32[]{:S(2)}) collective-permute-start(bf16[256,1536]{1,0:T(8,128)(2,1)S(1)} %collective-permute-done.43.normed_own), channel_id=1, source_target_pairs={{0,4},{4,0},{8,12},{12,8},{16,20},{20,16},{24,28},{28,24},{1,5},{5... | collective-permute-start | bytes 2359304 | tf_op jit(solution)/shard_map/ppermute | solution.py:761
  290.4 38.0 %collective-permute-start.48 = (bf16[256,1536]{1,0:T(8,128)(2,1)S(1)}, bf16[256,1536]{1,0:T(8,128)(2,1)S(1)}, u32[]{:S(2)}, u32[]{:S(2)}) collective-permute-start(bf16[256,1536]{1,0:T(8,128)(2,1)S(1)} %get-tuple-element.551), channel_id=1, source_target_pairs={{0,4},{4,0},{8,12},{12,8},{16,20},{20,16},{24,28},{28,24},{1,5},{5... | collective-permute-start | bytes 2359304 | tf_op jit(solution)/shard_map/ppermute | solution.py:761
  306.8 23.6 %collective-permute-start.46 = (bf16[256,1536]{1,0:T(8,128)(2,1)S(1)}, bf16[256,1536]{1,0:T(8,128)(2,1)S(1)}, u32[]{:S(2)}, u32[]{:S(2)}) collective-permute-start(bf16[256,1536]{1,0:T(8,128)(2,1)S(1)} %add.776), channel_id=1, source_target_pairs={{0,8},{4,12},{8,16},{12,20},{16,24},{20,28},{24,0},{28,4},{1,9},{5... | collective-permute-start | bytes 2359304 | tf_op jit(solution)/shard_map/ppermute | solution.py:761
  329.6 25.8 %collective-permute-start.50 = (bf16[256,1536]{1,0:T(8,128)(2,1)}, bf16[256,1536]{1,0:T(8,128)(2,1)}, u32[]{:S(2)}, u32[]{:S(2)}) collective-permute-start(bf16[256,1536]{1,0:T(8,128)(2,1)} %add.778), channel_id=1, source_target_pairs={{0,8},{4,12},{8,16},{12,20},{16,24},{20,28},{24,0},{28,4},{1,9},{5... | collective-permute-start | bytes 2359304 | tf_op jit(solution)/shard_map/ppermute | solution.py:761
  330.2 36.8 %collective-permute-start.49 = (bf16[256,1536]{1,0:T(8,128)(2,1)}, bf16[256,1536]{1,0:T(8,128)(2,1)}, u32[]{:S(2)}, u32[]{:S(2)}) collective-permute-start(bf16[256,1536]{1,0:T(8,128)(2,1)} %get-tuple-element.553), channel_id=1, source_target_pairs={{0,4},{4,0},{8,12},{12,8},{16,20},{20,16},{24,28},{28,24},{1,5},{5... | collective-permute-start | bytes 2359304 | tf_op jit(solution)/shard_map/ppermute | solution.py:761
  331.9 37.7 %collective-permute-start.47 = (bf16[256,1536]{1,0:T(8,128)(2,1)}, bf16[256,1536]{1,0:T(8,128)(2,1)}, u32[]{:S(2)}, u32[]{:S(2)}) collective-permute-start(bf16[256,1536]{1,0:T(8,128)(2,1)} %add.777), channel_id=1, source_target_pairs={{0,8},{4,12},{8,16},{12,20},{16,24},{20,28},{24,0},{28,4},{1,9},{5... | collective-permute-start | bytes 2359304 | tf_op jit(solution)/shard_map/ppermute | solution.py:761
  369.6 30.1 %collective-permute-start.51 = (bf16[8,48,1152]{2,1,0:T(8,128)(2,1)}, bf16[8,48,1152]{2,1,0:T(8,128)(2,1)S(1)}, u32[]{:S(2)}, u32[]{:S(2)}) collective-permute-start(bf16[8,48,1152]{2,1,0:T(8,128)(2,1)} %bitcast.69), channel_id=1, source_target_pairs={{0,1},{1,0},{2,3},{3,2},{4,5},{5,4},{6,7},{7,6},{8,9},{9,8},{10,11... | collective-permute-start | bytes 2654216 | tf_op jit(solution)/shard_map/ppermute | solution.py:767
  370.4 29.4 %collective-permute-start.52 = (bf16[8,48,1152]{2,1,0:T(8,128)(2,1)}, bf16[8,48,1152]{2,1,0:T(8,128)(2,1)S(1)}, u32[]{:S(2)}, u32[]{:S(2)}) collective-permute-start(bf16[8,48,1152]{2,1,0:T(8,128)(2,1)} %bitcast.71), channel_id=1, source_target_pairs={{0,2},{1,3},{2,0},{3,1},{4,6},{5,7},{6,4},{7,5},{8,10},{9,11},{10,... | collective-permute-start | bytes 2654216 | tf_op jit(solution)/shard_map/ppermute | solution.py:767
  371.9 27.8 %collective-permute-start.54 = (bf16[256,1536]{1,0:T(8,128)(2,1)S(1)}, bf16[256,1536]{1,0:T(8,128)(2,1)S(1)}, u32[]{:S(2)}, u32[]{:S(2)}) collective-permute-start(bf16[256,1536]{1,0:T(8,128)(2,1)S(1)} %add.779), channel_id=1, source_target_pairs={{0,8},{4,12},{8,16},{12,20},{16,24},{20,28},{24,0},{28,4},{1,9},{5... | collective-permute-start | bytes 2359304 | tf_op jit(solution)/shard_map/ppermute | solution.py:761
  372.8 26.9 %collective-permute-start.55 = (bf16[256,1536]{1,0:T(8,128)(2,1)}, bf16[256,1536]{1,0:T(8,128)(2,1)S(1)}, u32[]{:S(2)}, u32[]{:S(2)}) collective-permute-start(bf16[256,1536]{1,0:T(8,128)(2,1)} %get-tuple-element.572), channel_id=1, source_target_pairs={{0,4},{4,0},{8,12},{12,8},{16,20},{20,16},{24,28},{28,24},{1,5},{5... | collective-permute-start | bytes 2359304 | tf_op jit(solution)/shard_map/ppermute | solution.py:761
  403.4 27.0 %collective-permute-start.60 = (bf16[8,48,1152]{2,1,0:T(8,128)(2,1)}, bf16[8,48,1152]{2,1,0:T(8,128)(2,1)S(1)}, u32[]{:S(2)}, u32[]{:S(2)}) collective-permute-start(bf16[8,48,1152]{2,1,0:T(8,128)(2,1)} %bitcast.227), channel_id=1, source_target_pairs={{0,1},{1,0},{2,3},{3,2},{4,5},{5,4},{6,7},{7,6},{8,9},{9,8},{10,11... | collective-permute-start | bytes 2654216 | tf_op jit(solution)/shard_map/ppermute | solution.py:767
  403.9 26.6 %collective-permute-start.61 = (bf16[8,48,1152]{2,1,0:T(8,128)(2,1)}, bf16[8,48,1152]{2,1,0:T(8,128)(2,1)S(1)}, u32[]{:S(2)}, u32[]{:S(2)}) collective-permute-start(bf16[8,48,1152]{2,1,0:T(8,128)(2,1)} %bitcast.226), channel_id=1, source_target_pairs={{0,2},{1,3},{2,0},{3,1},{4,6},{5,7},{6,4},{7,5},{8,10},{9,11},{10,... | collective-permute-start | bytes 2654216 | tf_op jit(solution)/shard_map/ppermute | solution.py:767
  405.4 25.0 %collective-permute-start.57 = (bf16[256,512]{1,0:T(8,128)(2,1)S(1)}, bf16[256,512]{1,0:T(8,128)(2,1)S(1)}, u32[]{:S(2)}, u32[]{:S(2)}) collective-permute-start(bf16[256,512]{1,0:T(8,128)(2,1)S(1)} %get-tuple-element.592), channel_id=1, source_target_pairs={{0,24},{4,28},{8,0},{12,4},{16,8},{20,12},{24,16},{28,20},{1,25},{... | collective-permute-start | bytes 786440 | tf_op jit(solution)/shard_map/ppermute | solution.py:761
  406.0 24.5 %collective-permute-start.58 = (bf16[256,512]{1,0:T(8,128)(2,1)S(1)}, bf16[256,512]{1,0:T(8,128)(2,1)S(1)}, u32[]{:S(2)}, u32[]{:S(2)}) collective-permute-start(bf16[256,512]{1,0:T(8,128)(2,1)S(1)} %get-tuple-element.593), channel_id=1, source_target_pairs={{0,16},{4,20},{8,24},{12,28},{16,0},{20,4},{24,8},{28,12},{1,17},{... | collective-permute-start | bytes 786440 | tf_op jit(solution)/shard_map/ppermute | solution.py:761
  407.8 22.7 %collective-permute-start.59 = (bf16[256,512]{1,0:T(8,128)(2,1)S(1)}, bf16[256,512]{1,0:T(8,128)(2,1)S(1)}, u32[]{:S(2)}, u32[]{:S(2)}) collective-permute-start(bf16[256,512]{1,0:T(8,128)(2,1)S(1)} %get-tuple-element.594), channel_id=1, source_target_pairs={{0,8},{4,12},{8,16},{12,20},{16,24},{20,28},{24,0},{28,4},{1,9},{5... | collective-permute-start | bytes 786440 | tf_op jit(solution)/shard_map/ppermute | solution.py:761
  430.5 27.2 %collective-permute-start.64 = (bf16[16,48,1536]{2,1,0:T(8,128)(2,1)}, bf16[16,48,1536]{2,1,0:T(8,128)(2,1)}, u32[]{:S(2)}, u32[]{:S(2)}) collective-permute-start(bf16[16,48,1536]{2,1,0:T(8,128)(2,1)} %bitcast.84), channel_id=1, source_target_pairs={{0,4},{4,0},{8,12},{12,8},{16,20},{20,16},{24,28},{28,24},{1,5},{5... | collective-permute-start | bytes 7077896 | tf_op jit(solution)/shard_map/ppermute | solution.py:761
  430.6 27.1 %collective-permute-start.65 = (bf16[16,48,1536]{2,1,0:T(8,128)(2,1)}, bf16[16,48,1536]{2,1,0:T(8,128)(2,1)}, u32[]{:S(2)}, u32[]{:S(2)}) collective-permute-start(bf16[16,48,1536]{2,1,0:T(8,128)(2,1)} %bitcast.88), channel_id=1, source_target_pairs={{0,4},{4,0},{8,12},{12,8},{16,20},{20,16},{24,28},{28,24},{1,5},{5... | collective-permute-start | bytes 7077896 | tf_op jit(solution)/shard_map/ppermute | solution.py:761
  433.3 23.6 %collective-permute-start.62 = (bf16[8,48,1152]{2,1,0:T(8,128)(2,1)}, bf16[8,48,1152]{2,1,0:T(8,128)(2,1)}, u32[]{:S(2)}, u32[]{:S(2)}) collective-permute-start(bf16[8,48,1152]{2,1,0:T(8,128)(2,1)} %bitcast.91), channel_id=1, source_target_pairs={{0,2},{1,3},{2,0},{3,1},{4,6},{5,7},{6,4},{7,5},{8,10},{9,11},{10,... | collective-permute-start | bytes 2654216 | tf_op jit(solution)/shard_map/ppermute | solution.py:767
  436.0 21.7 %collective-permute-start.63 = (bf16[8,48,1152]{2,1,0:T(8,128)(2,1)}, bf16[8,48,1152]{2,1,0:T(8,128)(2,1)}, u32[]{:S(2)}, u32[]{:S(2)}) collective-permute-start(bf16[8,48,1152]{2,1,0:T(8,128)(2,1)} %bitcast.97), channel_id=1, source_target_pairs={{0,1},{1,0},{2,3},{3,2},{4,5},{5,4},{6,7},{7,6},{8,9},{9,8},{10,11... | collective-permute-start | bytes 2654216 | tf_op jit(solution)/shard_map/ppermute | solution.py:767
  437.6 19.3 %collective-permute-start.66 = (bf16[256,1536]{1,0:T(8,128)(2,1)}, bf16[256,1536]{1,0:T(8,128)(2,1)}, u32[]{:S(2)}, u32[]{:S(2)}) collective-permute-start(bf16[256,1536]{1,0:T(8,128)(2,1)} %add.780), channel_id=1, source_target_pairs={{0,8},{4,12},{8,16},{12,20},{16,24},{20,28},{24,0},{28,4},{1,9},{5... | collective-permute-start | bytes 2359304 | tf_op jit(solution)/shard_map/ppermute | solution.py:761
  460.5 21.2 %collective-permute-start.70 = (bf16[2,288,768]{2,1,0:T(8,128)(2,1)S(1)}, bf16[2,288,768]{2,1,0:T(8,128)(2,1)S(1)}, u32[]{:S(2)}, u32[]{:S(2)}) collective-permute-start(bf16[2,288,768]{2,1,0:T(8,128)(2,1)S(1)} %copy-done.76), channel_id=1, source_target_pairs={{0,1},{1,0},{2,3},{3,2},{4,5},{5,4},{6,7},{7,6},{8,9},{9,8},{10,11... | collective-permute-start | bytes 2654216 | tf_op jit(solution)/shard_map/ppermute | solution.py:767
  462.1 20.9 %collective-permute-start.71 = (bf16[2,288,768]{2,1,0:T(8,128)(2,1)S(1)}, bf16[2,288,768]{2,1,0:T(8,128)(2,1)S(1)}, u32[]{:S(2)}, u32[]{:S(2)}) collective-permute-start(bf16[2,288,768]{2,1,0:T(8,128)(2,1)S(1)} %copy-done.73), channel_id=1, source_target_pairs={{0,2},{1,3},{2,0},{3,1},{4,6},{5,7},{6,4},{7,5},{8,10},{9,11},{10,... | collective-permute-start | bytes 2654216 | tf_op jit(solution)/shard_map/ppermute | solution.py:767
  483.0 32.8 %collective-permute-start.74 = (bf16[8,48,1920]{2,1,0:T(8,128)(2,1)S(1)}, bf16[8,48,1920]{2,1,0:T(8,128)(2,1)S(1)}, u32[]{:S(2)}, u32[]{:S(2)}) collective-permute-start(bf16[8,48,1920]{2,1,0:T(8,128)(2,1)S(1)} %bitcast.224), channel_id=1, source_target_pairs={{0,1},{1,0},{2,3},{3,2},{4,5},{5,4},{6,7},{7,6},{8,9},{9,8},{10,11... | collective-permute-start | bytes 4423688 | tf_op jit(solution)/shard_map/ppermute | solution.py:767
  483.4 32.3 %collective-permute-start.75 = (bf16[8,48,1792]{2,1,0:T(8,128)(2,1)S(1)}, bf16[8,48,1792]{2,1,0:T(8,128)(2,1)S(1)}, u32[]{:S(2)}, u32[]{:S(2)}) collective-permute-start(bf16[8,48,1792]{2,1,0:T(8,128)(2,1)S(1)} %bitcast.225), channel_id=1, source_target_pairs={{0,2},{1,3},{2,0},{3,1},{4,6},{5,7},{6,4},{7,5},{8,10},{9,11},{10,... | collective-permute-start | bytes 4128776 | tf_op jit(solution)/shard_map/ppermute | solution.py:767
  484.9 21.6 %collective-permute-start.72 = (bf16[2,2,48,1152]{3,2,1,0:T(8,128)(2,1)S(1)}, bf16[2,2,48,1152]{3,2,1,0:T(8,128)(2,1)S(1)}, u32[]{:S(2)}, u32[]{:S(2)}) collective-permute-start(bf16[2,2,48,1152]{3,2,1,0:T(8,128)(2,1)S(1)} %copy-done.88), channel_id=1, source_target_pairs={{0,8},{4,12},{8,16},{12,20},{16,24},{20,28},{24,0},{28,4},{1,9},{5... | collective-permute-start | bytes 1327112 | tf_op jit(solution)/shard_map/ppermute | solution.py:761
  486.8 29.0 %collective-permute-start.73 = (bf16[2,2,48,1152]{3,2,1,0:T(8,128)(2,1)S(1)}, bf16[2,2,48,1152]{3,2,1,0:T(8,128)(2,1)S(1)}, u32[]{:S(2)}, u32[]{:S(2)}) collective-permute-start(bf16[2,2,48,1152]{3,2,1,0:T(8,128)(2,1)S(1)} %copy-done.86), channel_id=1, source_target_pairs={{0,16},{4,20},{8,24},{12,28},{16,0},{20,4},{24,8},{28,12},{1,17},{... | collective-permute-start | bytes 1327112 | tf_op jit(solution)/shard_map/ppermute | solution.py:761
  516.1 18.1 %collective-permute-start.78 = (bf16[4,48,1920]{2,1,0:T(8,128)(2,1)S(1)}, bf16[4,48,1920]{2,1,0:T(8,128)(2,1)S(1)}, u32[]{:S(2)}, u32[]{:S(2)}) collective-permute-start(bf16[4,48,1920]{2,1,0:T(8,128)(2,1)S(1)} %bitcast.228), channel_id=1, source_target_pairs={{0,2},{1,3},{2,0},{3,1},{4,6},{5,7},{6,4},{7,5},{8,10},{9,11},{10,... | collective-permute-start | bytes 2211848 | tf_op jit(solution)/shard_map/ppermute | solution.py:767
  517.0 16.8 %collective-permute-start.79 = (bf16[4,48,1792]{2,1,0:T(8,128)(2,1)S(1)}, bf16[4,48,1792]{2,1,0:T(8,128)(2,1)S(1)}, u32[]{:S(2)}, u32[]{:S(2)}) collective-permute-start(bf16[4,48,1792]{2,1,0:T(8,128)(2,1)S(1)} %bitcast.229), channel_id=1, source_target_pairs={{0,1},{1,0},{2,3},{3,2},{4,5},{5,4},{6,7},{7,6},{8,9},{9,8},{10,11... | collective-permute-start | bytes 2064392 | tf_op jit(solution)/shard_map/ppermute | solution.py:767
  518.7 15.7 %collective-permute-start.77 = (bf16[2,2,48,1152]{3,2,1,0:T(8,128)(2,1)S(1)}, bf16[2,2,48,1152]{3,2,1,0:T(8,128)(2,1)S(1)}, u32[]{:S(2)}, u32[]{:S(2)}) collective-permute-start(bf16[2,2,48,1152]{3,2,1,0:T(8,128)(2,1)S(1)} %copy-done.82), channel_id=1, source_target_pairs={{0,24},{4,28},{8,0},{12,4},{16,8},{20,12},{24,16},{28,20},{1,25},{... | collective-permute-start | bytes 1327112 | tf_op jit(solution)/shard_map/ppermute | solution.py:761
  534.5 25.8 %collective-permute-start.80 = (bf16[48,3712]{1,0:T(8,128)(2,1)S(1)}, bf16[48,3712]{1,0:T(8,128)(2,1)S(1)}, u32[]{:S(2)}, u32[]{:S(2)}) collective-permute-start(bf16[48,3712]{1,0:T(8,128)(2,1)S(1)} %pad_maximum_fusion.8), channel_id=1, source_target_pairs={{0,8},{4,12},{8,16},{12,20},{16,24},{20,28},{24,0},{28,4},{1,9},{5... | collective-permute-start | bytes 1069064 | tf_op jit(solution)/shard_map/ppermute | solution.py:761
  536.4 29.3 %collective-permute-start.81 = (bf16[48,3712]{1,0:T(8,128)(2,1)S(1)}, bf16[48,3712]{1,0:T(8,128)(2,1)S(1)}, u32[]{:S(2)}, u32[]{:S(2)}) collective-permute-start(bf16[48,3712]{1,0:T(8,128)(2,1)S(1)} %pad_maximum_fusion.9), channel_id=1, source_target_pairs={{0,16},{4,20},{8,24},{12,28},{16,0},{20,4},{24,8},{28,12},{1,17},{... | collective-permute-start | bytes 1069064 | tf_op jit(solution)/shard_map/ppermute | solution.py:761
  540.8 28.9 %collective-permute-start.82 = (bf16[48,3712]{1,0:T(8,128)(2,1)S(1)}, bf16[48,3712]{1,0:T(8,128)(2,1)S(1)}, u32[]{:S(2)}, u32[]{:S(2)}) collective-permute-start(bf16[48,3712]{1,0:T(8,128)(2,1)S(1)} %pad_maximum_fusion.10), channel_id=1, source_target_pairs={{0,24},{4,28},{8,0},{12,4},{16,8},{20,12},{24,16},{28,20},{1,25},{... | collective-permute-start | bytes 1069064 | tf_op jit(solution)/shard_map/ppermute | solution.py:761
  (135 other events, 1224.6 us)
Sparse Core Ops, SparseCore 0:
  37.4 84.5 all-gather.2
  124.3 64.6 all-gather.4

commit v4 on v1

--- a/solution.py
+++ b/solution.py
@@ -904,6 +904,8 @@
     gain_two = small_params[:, D : 2 * D]
     qkv_bias = small_params[:, 2 * D :]
     normed_one, key_value = project_kv(inputs, w_qkv, gain_one, qkv_bias, cosine, sine)
+    for shift in groups[2]:
+        gate_up_pieces[shift] = after(gate_up_pieces[shift], key_value)
     gate_up_held = [
         jnp.concatenate([gate_up_pieces[t] for t in ts], axis=0)
         for ts in (range(n_chips // 2), range(n_chips // 2, n_chips))

time: 580 us -> 591 us (1.019)
  waiting for transfers between devices: 199 us -> 207 us
    ppermute x24, waiting for transfers between devices: 58.6 us -> 67.6 us  [dp_perm(): lax.ppermute(values, 'dp', [(i, i ^ bit) for i in range(lax.axis_size('dp...]
    unnamed x233 -> x231, local copies, waits for them, and re-layouts: 55.7 us -> 56.4 us
  transfers between devices with their start and end apart: 87 -> 87, of which waited for: 42 -> 41; matrix products, arithmetic and copies ran while one was open for 4% -> 3% of each run, Pallas kernels for 35% -> 34%
where the time goes in v4:
time: 591 us; the launch traced here: 584 us
  waiting for transfers between devices  207 us (35%)
  Pallas kernels  202 us (34%)
  starting transfers between devices  77.5 us (13%)
  local copies, waits for them, and re-layouts  62.8 us (11%)
  other arithmetic  18.5 us (3%)
  between operations  15.6 us (3%)
    pallas_call x44, Pallas kernels, kernel_call(): pl.pallas_call(kernel, name=name, out_shape=out_shape, compiler_params=pl...  202 us
    ppermute x61, waiting for transfers between devices, seq_perm(): lax.ppermute(values, 'seq', [(i, (i + 2 * chips) % count ^ flip) for i in...  139 us
    ppermute x24, waiting for transfers between devices, dp_perm(): lax.ppermute(values, 'dp', [(i, i ^ bit) for i in range(lax.axis_size('dp...  67.6 us
    unnamed x231, local copies, waits for them, and re-layouts  56.4 us
    ppermute x61, starting transfers between devices, seq_perm(): lax.ppermute(values, 'seq', [(i, (i + 2 * chips) % count ^ flip) for i in...  50.4 us
    ppermute x24, starting transfers between devices, dp_perm(): lax.ppermute(values, 'dp', [(i, i ^ bit) for i in range(lax.axis_size('dp...  27 us
  transfers between devices with their start and end apart: 87, of which 41 were waited for; matrix products, arithmetic and copies ran while one was open for 3% of the time, Pallas kernels for 34%

profile of v4, /device:TPU:8, one launch (start us, length us, event | category | flops | bytes accessed | tf_op | source)
XLA Modules:
  0.0 583.9 jit_solution(15461490006478009586)
XLA Ops:
  7.3 2.0 copy-done.9
  13.9 1.9 collective-permute-start.2
  21.0 6.1 %collective-permute-done.refs_1_ = bf16[48,2176]{1,0:T(8,128)(2,1)S(1)} collective-permute-done((bf16[48,2176]{1,0:T(8,128)(2,1)S(1)}, bf16[48,2176]{1,0:T(8,128)(2,1)S(1)}, u32[]{:S(2)}, u32[]{:S(2)}) %collective-permute-start) | collective-permute-done | bytes 208928 | tf_op jit(solution)/shard_map/ppermute | solution.py:761
  27.1 4.2 collective-permute-done.1.refs_2_
  36.3 10.3 %collective-permute-done.5 = bf16[4,48,1024]{2,1,0:T(8,128)(2,1)S(1)} collective-permute-done((bf16[4,48,1024]{2,1,0:T(8,128)(2,1)S(1)}, bf16[4,48,1024]{2,1,0:T(8,128)(2,1)S(1)}, u32[]{:S(2)}, u32[]{:S(2)}) %collective-permute-start.5) | collective-permute-done | bytes 393248 | tf_op jit(solution)/shard_map/ppermute | solution.py:767
  51.4 10.6 %collective-permute-done.9 = bf16[2,2,48,1152]{3,2,1,0:T(8,128)(2,1)S(1)} collective-permute-done((bf16[2,2,48,1152]{3,2,1,0:T(8,128)(2,1)S(1)}, bf16[2,2,48,1152]{3,2,1,0:T(8,128)(2,1)S(1)}, u32[]{:S(2)}, u32[]{:S(2)}) %collective-permute-start.9) | collective-permute-done | bytes 442400 | tf_op jit(solution)/shard_map/ppermute | solution.py:761
  62.0 6.4 %collective-permute-done.8.refs_5_ = bf16[8,48,1024]{2,1,0:T(8,128)(2,1)} collective-permute-done((bf16[8,48,1024]{2,1,0:T(8,128)(2,1)S(1)}, bf16[8,48,1024]{2,1,0:T(8,128)(2,1)}, u32[]{:S(2)}, u32[]{:S(2)}) %collective-permute-start.8) | collective-permute-done | bytes 786464 | tf_op jit(solution)/shard_map/ppermute | solution.py:767
  74.1 4.2 assemble.2
  78.4 2.6 copy-done.7
  82.4 3.3 project_kv.1
  85.7 9.6 %collective-permute-done.14 = bf16[2,2,48,1152]{3,2,1,0:T(8,128)(2,1)} collective-permute-done((bf16[2,2,48,1152]{3,2,1,0:T(8,128)(2,1)}, bf16[2,2,48,1152]{3,2,1,0:T(8,128)(2,1)}, u32[]{:S(2)}, u32[]{:S(2)}) %collective-permute-start.14) | collective-permute-done | bytes 442400 | tf_op jit(solution)/shard_map/ppermute | solution.py:761
  100.4 4.2 collective-permute-start.16
  104.6 6.9 %collective-permute-done.15.refs_2_ = bf16[256,512]{1,0:T(8,128)(2,1)S(1)} collective-permute-done((bf16[256,512]{1,0:T(8,128)(2,1)S(1)}, bf16[256,512]{1,0:T(8,128)(2,1)S(1)}, u32[]{:S(2)}, u32[]{:S(2)}) %collective-permute-start.15) | collective-permute-done | bytes 262176 | tf_op jit(solution)/shard_map/ppermute | solution.py:761
  111.5 5.1 project_q.1.q_ref
  116.6 14.3 %collective-permute-done.16.refs_4_ = bf16[256,512]{1,0:T(8,128)(2,1)S(1)} collective-permute-done((bf16[256,512]{1,0:T(8,128)(2,1)S(1)}, bf16[256,512]{1,0:T(8,128)(2,1)S(1)}, u32[]{:S(2)}, u32[]{:S(2)}) %collective-permute-start.16) | collective-permute-done | bytes 262176 | tf_op jit(solution)/shard_map/ppermute | solution.py:761
  130.9 2.8 collective-permute-done.17.refs_6_
  146.1 11.5 %attend.1 = (f32[256,1536]{1,0:T(8,128)S(1)}, f32[12,256]{1,0:T(8,128)S(1)}, bf16[2048,512]{1,0:T(8,128)(2,1)S(1)}) custom-call(s32[2]{0:T(128)S(1)} %slice_bitcast_fusion.1.query_bases, s32[16]{0:T(128)S(1)} %select_n.83.key_bases, bf16[256,1536]{1,0:T(8,128)(2,1)S(1)} %copy-done.13, bf16[256,512]{1,0:T(8,128)(2,1)S(1)} %copy-done.61, ...), custom_call_target="tpu_custom_call" | custom-call | flops 1000000 | bytes 1000000 | tf_op jit(solution)/shard_map/attend/pallas_call | solution.py:38
  160.0 8.6 %collective-permute-done.24 = bf16[4,2,48,1152]{3,2,1,0:T(8,128)(2,1)} collective-permute-done((bf16[4,2,48,1152]{3,2,1,0:T(8,128)(2,1)S(1)}, bf16[4,2,48,1152]{3,2,1,0:T(8,128)(2,1)}, u32[]{:S(2)}, u32[]{:S(2)}) %collective-permute-start.24) | collective-permute-done | bytes 884768 | tf_op jit(solution)/shard_map/ppermute | solution.py:767
  172.3 2.3 copy-done.8
  176.1 2.4 out_project.1
  179.4 9.2 %collective-permute-done.29.grad_own = bf16[256,1536]{1,0:T(8,128)(2,1)} collective-permute-done((bf16[256,1536]{1,0:T(8,128)(2,1)}, bf16[256,1536]{1,0:T(8,128)(2,1)}, u32[]{:S(2)}, u32[]{:S(2)}) %collective-permute-start.29) | collective-permute-done | bytes 786464 | tf_op jit(solution)/shard_map/ppermute | solution.py:761
  189.3 20.4 %collective-permute-done.27 = bf16[4,2,48,1152]{3,2,1,0:T(8,128)(2,1)} collective-permute-done((bf16[4,2,48,1152]{3,2,1,0:T(8,128)(2,1)}, bf16[4,2,48,1152]{3,2,1,0:T(8,128)(2,1)}, u32[]{:S(2)}, u32[]{:S(2)}) %collective-permute-start.27) | collective-permute-done | bytes 884768 | tf_op jit(solution)/shard_map/ppermute | solution.py:767
  215.0 5.5 assemble.3
  220.5 2.9 copy-done
  223.4 2.0 copy-done.6
  226.6 17.2 %feed_forward.4 = (bf16[256,1536]{1,0:T(8,128)(2,1)S(1)}, bf16[256,1536]{1,0:T(8,128)(2,1)S(1)}, bf16[256,1536]{1,0:T(8,128)(2,1)S(1)}, bf16[256,1536]{1,0:T(8,1...) custom-call(bf16[256,1536]{1,0:T(8,128)(2,1)} %get-tuple-element.452, ...), custom_call_target="tpu_custom_call" | custom-call | flops 1000000 | bytes 1000000 | tf_op jit(solution)/shard_map/feed_forward/pallas_call | solution.py:38
  246.9 2.0 collective-permute-done.36.grad_other
  250.0 2.0 collective-permute-start.38
  252.1 17.3 %feed_forward.5 = (bf16[256,1536]{1,0:T(8,128)(2,1)S(1)}, bf16[256,1536]{1,0:T(8,128)(2,1)S(1)}, bf16[256,1536]{1,0:T(8,128)(2,1)S(1)}, bf16[256,1536]{1,0:T(8,1...) custom-call(bf16[256,1536]{1,0:T(8,128)(2,1)} %collective-permute-do, ...), custom_call_target="tpu_custom_call", output_to_operand_aliasing={{4}: (6, {}), {5}: (7, {}), {6}: (8, {}), {7}: (9, {}), {8}... | custom-call | flops 1000000 | bytes 1000000 | tf_op jit(solution)/shard_map/feed_forward/pallas_call | solution.py:38
  270.1 2.0 collective-permute-done.37.refs_1_
  277.0 16.9 %feed_forward.6 = (bf16[256,1536]{1,0:T(8,128)(2,1)S(1)}, bf16[256,1536]{1,0:T(8,128)(2,1)}, bf16[256,1536]{1,0:T(8,128)(2,1)S(1)}, bf16[256,1536]{1,0:T(8,128)(...) custom-call(bf16[256,1536]{1,0:T(8,128)(2,1)S(1)} %collective-permut, ...), custom_call_target="tpu_custom_call", output_to_operand_aliasing={{4}: (6, {}), {5}: (7, {}), {6}: (8, {}), {7}: (9, {}), {8}... | custom-call | flops 1000000 | bytes 1000000 | tf_op jit(solution)/shard_map/feed_forward/pallas_call | solution.py:38
  294.9 15.6 %collective-permute-done.42.refs_2_ = bf16[256,1536]{1,0:T(8,128)(2,1)S(1)} collective-permute-done((bf16[256,1536]{1,0:T(8,128)(2,1)S(1)}, bf16[256,1536]{1,0:T(8,128)(2,1)S(1)}, u32[]{:S(2)}, u32[]{:S(2)}) %collective-permute-start.42) | collective-permute-done | bytes 786464 | tf_op jit(solution)/shard_map/ppermute | solution.py:761
  310.8 1.9 collective-permute-start.46
  312.8 16.8 %feed_forward.7 = (bf16[256,1536]{1,0:T(8,128)(2,1)S(1)}, bf16[256,1536]{1,0:T(8,128)(2,1)}, bf16[256,1536]{1,0:T(8,128)(2,1)S(1)}, bf16[256,1536]{1,0:T(8,128)(...) custom-call(bf16[256,1536]{1,0:T(8,128)(2,1)S(1)} %collective-permut, ...), custom_call_target="tpu_custom_call", output_to_operand_aliasing={{4}: (6, {}), {5}: (7, {}), {6}: (8, {}), {7}: (9, {}), {8}... | custom-call | flops 1000000 | bytes 1000000 | tf_op jit(solution)/shard_map/feed_forward/pallas_call | solution.py:38
  329.6 2.2 copy-done.5
  335.8 3.7 collective-permute-start.47
  339.6 2.8 copy-done.1
  342.4 2.3 copy-done.3
  344.7 2.3 copy-done.4
  347.0 12.4 %weight_grad.6 = (bf16[8,1,48,1152]{3,2,1,0:T(8,128)(2,1)S(1)}, bf16[8,1,48,1152]{3,2,1,0:T(8,128)(2,1)}, bf16[4,2,48,1152]{3,2,1,0:T(8,128)(2,1)S(1)}, bf16[4,2,48,1152]{3,2,1,0:T(8,128)(2,1)}) custom-call(s32[2]{0:T(128)S(1)} %pad_add_fusion.8.sides, bf16[4,512,1536]{2,1,0:T(8,128)(2,1)S(1)} %copy-done.1, bf16[4,512,1152]{2,1,0:T(8,128)(2,1)S(1)} %copy-done.3, ...), custom_call_target="tpu_custom_call" | custom-call | flops 1000000 | bytes 1000000 | tf_op jit(solution)/shard_map/weight_grad/pallas_call | solution.py:38
  359.5 11.6 %weight_grad.7 = (bf16[8,1,48,1152]{3,2,1,0:T(8,128)(2,1)S(1)}, bf16[8,1,48,1152]{3,2,1,0:T(8,128)(2,1)S(1)}, bf16[4,2,48,1152]{3,2,1,0:T(8,128)(2,1)S(1)}, bf16[4,2,48,1152]{3,2,1,0:T(8,128)(2,1)S(1)}) custom-call(s32[2]{0:T(128)S(1)} %pad_add_fusion.8.sides, bf16[4,512,1536]{2,1,0:T(8,128)(2,1)S(1)} %copy-done.1, bf16[4,512,1152]{2,1,0:T(8,128)(2,1)S(1)} %copy-done.3, ...), custom_call_target="tpu_custom_call" | custom-call | flops 1000000 | bytes 1000000 | tf_op jit(solution)/shard_map/weight_grad/pallas_call | solution.py:38
  378.4 3.5 norm_back.1
  382.8 21.0 %attend_back.1 = (bf16[256,1536]{1,0:T(8,128)(2,1)S(1)}, bf16[1024,512]{1,0:T(8,128)(2,1)S(1)}, bf16[1024,512]{1,0:T(8,128)(2,1)S(1)}) custom-call(s32[2]{0:T(128)S(1)} %copy-done.67, s32[16]{0:T(128)S(1)} %select_n.83.key_bases, bf16[256,1536]{1,0:T(8,128)(2,1)S(1)} %copy-done.14, bf16[2048,512]{1,0:T(8,128)(2,1)S(1)} %copy-done.33, ...), custom_call_target="tpu_custom_call" | custom-call | flops 1000000 | bytes 1000000 | tf_op jit(solution)/shard_map/attend_back/pallas_call | solution.py:38
  404.1 2.5 collective-permute-done.56
  415.6 3.9 weight_grad.8
  421.0 3.6 weight_grad.9
  426.0 8.4 %weight_grad.10 = bf16[1152,1536]{1,0:T(8,128)(2,1)S(1)} custom-call(s32[1]{0:T(128)} %constant.163.clone.1.chip.sides, bf16[4,512,1152]{2,1,0:T(8,128)(2,1)S(1)} %bitcast.168, bf16[4,512,1536]{2,1,0:T(8,128)(2,1)S(1)} %bitcast.166), custom_call_target="tpu_custom_call" | custom-call | flops 1000000 | bytes 1000000 | tf_op jit(solution)/shard_map/weight_grad/pallas_call | solution.py:38
  447.8 7.6 %input_back.1 = (bf16[256,512]{1,0:T(8,128)(2,1)}, f32[256,1536]{1,0:T(8,128)}, f32[1,1536]{1,0:T(1,128)}, f32[1,2048]{1,0:T(1,128)}) custom-call(bf16[256,1536]{1,0:T(8,128)(2,1)} %bitcast.178, f32[1,1536]{1,0:T(1,128)} %get-tuple-element.773.gain, bf16[1536,2048]{1,0:T(8,128)(2,1)} %bitcast.171, bf16[256,1536]{1,0:T(8,128)(2,1)} %copy-done.27, ...), custom_call_target="tpu_custom_call" | custom-call | flops 1000000 | bytes 1000000 | tf_op jit(solution)/shard_map/input_back/pallas_call | solution.py:38
  457.9 3.1 collective-permute-done.66
  474.4 2.5 add_halve.14
  476.9 2.4 add_halve.15
  479.4 7.2 %collective-permute-done.70 = bf16[2,288,768]{2,1,0:T(8,128)(2,1)S(1)} collective-permute-done((bf16[2,288,768]{2,1,0:T(8,128)(2,1)S(1)}, bf16[2,288,768]{2,1,0:T(8,128)(2,1)S(1)}, u32[]{:S(2)}, u32[]{:S(2)}) %collective-permute-start.70) | collective-permute-done | bytes 884768 | tf_op jit(solution)/shard_map/ppermute | solution.py:767
  490.8 2.4 collective-permute-start.73
  493.6 17.0 %collective-permute-done.72.refs_1_ = bf16[2,2,48,1152]{3,2,1,0:T(8,128)(2,1)S(1)} collective-permute-done((bf16[2,2,48,1152]{3,2,1,0:T(8,128)(2,1)S(1)}, bf16[2,2,48,1152]{3,2,1,0:T(8,128)(2,1)S(1)}, u32[]{:S(2)}, u32[]{:S(2)}) %collective-permute-start.72) | collective-permute-done | bytes 442400 | tf_op jit(solution)/shard_map/ppermute | solution.py:761
  510.6 9.2 %collective-permute-done.73.refs_2_ = bf16[2,2,48,1152]{3,2,1,0:T(8,128)(2,1)S(1)} collective-permute-done((bf16[2,2,48,1152]{3,2,1,0:T(8,128)(2,1)S(1)}, bf16[2,2,48,1152]{3,2,1,0:T(8,128)(2,1)S(1)}, u32[]{:S(2)}, u32[]{:S(2)}) %collective-permute-start.73) | collective-permute-done | bytes 442400 | tf_op jit(solution)/shard_map/ppermute | solution.py:761
  522.8 3.5 collective-permute-start.77
  526.4 2.6 fusion.1
  529.0 9.7 %collective-permute-done.79.got = bf16[4,48,1792]{2,1,0:T(8,128)(2,1)S(1)} collective-permute-done((bf16[4,48,1792]{2,1,0:T(8,128)(2,1)S(1)}, bf16[4,48,1792]{2,1,0:T(8,128)(2,1)S(1)}, u32[]{:S(2)}, u32[]{:S(2)}) %collective-permute-start.79) | collective-permute-done | bytes 688160 | tf_op jit(solution)/shard_map/ppermute | solution.py:767
  540.7 4.4 collective-permute-start.81
  547.0 7.6 %adamw_hidden.1 = (f32[2,48,8960]{2,1,0:T(8,128)}, f32[2,48,8960]{2,1,0:T(8,128)}, f32[2,48,8960]{2,1,0:T(8,128)}) custom-call(s32[8]{0:T(128)S(1)} %stack.261.where, f32[2,48,8960]{2,1,0:T(8,128)S(1)} %copy-done.10, f32[2,48,8960]{2,1,0:T(8,128)S(1)} %copy-done.23, f32[2,48,8960]{2,1,0:T(8,128)} %second.1, ...), custom_call_target="tpu_custom_call" | custom-call | flops 1000000 | bytes 1000000 | tf_op jit(solution)/shard_map/adamw_hidden/pallas_call | solution.py:38
  556.6 3.2 multiply_subtract_fusion
  559.8 4.9 collective-permute-done.80
  564.7 4.9 collective-permute-done.81
  569.7 4.0 collective-permute-done.82
  (475 shorter events, 140.5 us)
Async XLA Ops:
  7.2 165.1 %all-gather.3.cloned.1.call-start = ((), (), s32[]{:S(2)}) async-start(), calls=%async_computation | async-start | bytes 4866048 | tf_op jit(solution)/shard_map/all_gather | solution.py:856
  11.1 15.9 %collective-permute-start = (bf16[48,2176]{1,0:T(8,128)(2,1)S(1)}, bf16[48,2176]{1,0:T(8,128)(2,1)S(1)}, u32[]{:S(2)}, u32[]{:S(2)}) collective-permute-start(bf16[48,2176]{1,0:T(8,128)(2,1)S(1)} %pad_maximum_fusion.11.refs_0_), channel_id=1, source_target_pairs={{0,8},{4,12},{8,16},{12,20},{16,24},{20,28},{24,0},{28,4},{1,9},{5... | collective-permute-start | bytes 626696 | tf_op jit(solution)/shard_map/ppermute | solution.py:761
  12.8 18.5 %collective-permute-start.1 = (bf16[48,2176]{1,0:T(8,128)(2,1)S(1)}, bf16[48,2176]{1,0:T(8,128)(2,1)S(1)}, u32[]{:S(2)}, u32[]{:S(2)}) collective-permute-start(bf16[48,2176]{1,0:T(8,128)(2,1)S(1)} %pad_maximum_fusion.11.refs_0_), channel_id=1, source_target_pairs={{0,16},{4,20},{8,24},{12,28},{16,0},{20,4},{24,8},{28,12},{1,17},{... | collective-permute-start | bytes 626696 | tf_op jit(solution)/shard_map/ppermute | solution.py:761
  13.9 19.2 %collective-permute-start.2 = (bf16[48,2176]{1,0:T(8,128)(2,1)S(1)}, bf16[48,2176]{1,0:T(8,128)(2,1)S(1)}, u32[]{:S(2)}, u32[]{:S(2)}) collective-permute-start(bf16[48,2176]{1,0:T(8,128)(2,1)S(1)} %pad_maximum_fusion.11.refs_0_), channel_id=1, source_target_pairs={{0,24},{4,28},{8,0},{12,4},{16,8},{20,12},{24,16},{28,20},{1,25},{... | collective-permute-start | bytes 626696 | tf_op jit(solution)/shard_map/ppermute | solution.py:761
  33.1 190.3 %all-gather.5.cloned.1.call-start = ((), (), s32[]{:S(2)}) async-start(), calls=%async_computation.1 | async-start | bytes 4423680 | tf_op jit(solution)/shard_map/all_gather | solution.py:880
  33.3 13.4 %collective-permute-start.4 = (bf16[4,48,1152]{2,1,0:T(8,128)(2,1)S(1)}, bf16[4,48,1152]{2,1,0:T(8,128)(2,1)S(1)}, u32[]{:S(2)}, u32[]{:S(2)}) collective-permute-start(bf16[4,48,1152]{2,1,0:T(8,128)(2,1)S(1)} %get-tuple-element.391), channel_id=1, source_target_pairs={{0,1},{1,0},{2,3},{3,2},{4,5},{5,4},{6,7},{7,6},{8,9},{9,8},{10,11... | collective-permute-start | bytes 1327112 | tf_op jit(solution)/shard_map/ppermute | solution.py:767
  34.8 12.9 %collective-permute-start.6 = (bf16[2,2,48,1152]{3,2,1,0:T(8,128)(2,1)S(1)}, bf16[2,2,48,1152]{3,2,1,0:T(8,128)(2,1)S(1)}, u32[]{:S(2)}, u32[]{:S(2)}) collective-permute-start(bf16[2,2,48,1152]{3,2,1,0:T(8,128)(2,1)S(1)} %get-tuple-element.390), channel_id=1, source_target_pairs={{0,8},{4,12},{8,16},{12,20},{16,24},{20,28},{24,0},{28,4},{1,9},{5... | collective-permute-start | bytes 1327112 | tf_op jit(solution)/shard_map/ppermute | solution.py:761
  48.5 20.6 %collective-permute-start.7 = (bf16[8,48,1152]{2,1,0:T(8,128)(2,1)S(1)}, bf16[8,48,1152]{2,1,0:T(8,128)(2,1)}, u32[]{:S(2)}, u32[]{:S(2)}) collective-permute-start(bf16[8,48,1152]{2,1,0:T(8,128)(2,1)S(1)} %constant_dynamic-update-slice_fusion.refs_0_), channel_id=1, source_target_pairs={{0,2},{1,3},{2,0},{3,1},{4,6},{5,7},{6,4},{7,5},{8,10},{9,11},{10,... | collective-permute-start | bytes 2654216 | tf_op jit(solution)/shard_map/ppermute | solution.py:767
  50.1 18.3 %collective-permute-start.8 = (bf16[8,48,1024]{2,1,0:T(8,128)(2,1)S(1)}, bf16[8,48,1024]{2,1,0:T(8,128)(2,1)}, u32[]{:S(2)}, u32[]{:S(2)}) collective-permute-start(bf16[8,48,1024]{2,1,0:T(8,128)(2,1)S(1)} %constant_dynamic-update-slice_fusion.2.refs_4_), channel_id=1, source_target_pairs={{0,1},{1,0},{2,3},{3,2},{4,5},{5,4},{6,7},{7,6},{8,9},{9,8},{10,11... | collective-permute-start | bytes 2359304 | tf_op jit(solution)/shard_map/ppermute | solution.py:767
  51.4 22.2 %collective-permute-start.10 = (bf16[8,48,1152]{2,1,0:T(8,128)(2,1)S(1)}, bf16[8,48,1152]{2,1,0:T(8,128)(2,1)}, u32[]{:S(2)}, u32[]{:S(2)}) collective-permute-start(bf16[8,48,1152]{2,1,0:T(8,128)(2,1)S(1)} %constant_dynamic-update-slice_fusion.refs_0_), channel_id=1, source_target_pairs={{0,4},{4,0},{8,12},{12,8},{16,20},{20,16},{24,28},{28,24},{1,5},{5... | collective-permute-start | bytes 2654216 | tf_op jit(solution)/shard_map/ppermute | solution.py:761
  72.3 23.0 %collective-permute-start.14 = (bf16[2,2,48,1152]{3,2,1,0:T(8,128)(2,1)}, bf16[2,2,48,1152]{3,2,1,0:T(8,128)(2,1)}, u32[]{:S(2)}, u32[]{:S(2)}) collective-permute-start(bf16[2,2,48,1152]{3,2,1,0:T(8,128)(2,1)} %get-tuple-element.412), channel_id=1, source_target_pairs={{0,16},{4,20},{8,24},{12,28},{16,0},{20,4},{24,8},{28,12},{1,17},{... | collective-permute-start | bytes 1327112 | tf_op jit(solution)/shard_map/ppermute | solution.py:761
  96.4 40.7 %collective-permute-start.22 = (bf16[4,2,48,1152]{3,2,1,0:T(8,128)(2,1)S(1)}, bf16[4,2,48,1152]{3,2,1,0:T(8,128)(2,1)}, u32[]{:S(2)}, u32[]{:S(2)}) collective-permute-start(bf16[4,2,48,1152]{3,2,1,0:T(8,128)(2,1)S(1)} %pad_maximum_fusion.4), channel_id=1, source_target_pairs={{0,1},{1,0},{2,3},{3,2},{4,5},{5,4},{6,7},{7,6},{8,9},{9,8},{10,11... | collective-permute-start | bytes 2654216 | tf_op jit(solution)/shard_map/ppermute | solution.py:767
  97.6 39.5 %collective-permute-start.23 = (bf16[4,2,48,1152]{3,2,1,0:T(8,128)(2,1)S(1)}, bf16[4,2,48,1152]{3,2,1,0:T(8,128)(2,1)}, u32[]{:S(2)}, u32[]{:S(2)}) collective-permute-start(bf16[4,2,48,1152]{3,2,1,0:T(8,128)(2,1)S(1)} %pad_maximum_fusion.5), channel_id=1, source_target_pairs={{0,2},{1,3},{2,0},{3,1},{4,6},{5,7},{6,4},{7,5},{8,10},{9,11},{10,... | collective-permute-start | bytes 2654216 | tf_op jit(solution)/shard_map/ppermute | solution.py:767
  99.1 12.4 %collective-permute-start.15 = (bf16[256,512]{1,0:T(8,128)(2,1)S(1)}, bf16[256,512]{1,0:T(8,128)(2,1)S(1)}, u32[]{:S(2)}, u32[]{:S(2)}) collective-permute-start(bf16[256,512]{1,0:T(8,128)(2,1)S(1)} %copy-done.61), channel_id=1, source_target_pairs={{0,8},{4,12},{8,16},{12,20},{16,24},{20,28},{24,0},{28,4},{1,9},{5... | collective-permute-start | bytes 786440 | tf_op jit(solution)/shard_map/ppermute | solution.py:761
  100.4 30.5 %collective-permute-start.16 = (bf16[256,512]{1,0:T(8,128)(2,1)S(1)}, bf16[256,512]{1,0:T(8,128)(2,1)S(1)}, u32[]{:S(2)}, u32[]{:S(2)}) collective-permute-start(bf16[256,512]{1,0:T(8,128)(2,1)S(1)} %copy-done.61), channel_id=1, source_target_pairs={{0,16},{4,20},{8,24},{12,28},{16,0},{20,4},{24,8},{28,12},{1,17},{... | collective-permute-start | bytes 786440 | tf_op jit(solution)/shard_map/ppermute | solution.py:761
  104.6 29.1 %collective-permute-start.17 = (bf16[256,512]{1,0:T(8,128)(2,1)S(1)}, bf16[256,512]{1,0:T(8,128)(2,1)}, u32[]{:S(2)}, u32[]{:S(2)}) collective-permute-start(bf16[256,512]{1,0:T(8,128)(2,1)S(1)} %copy-done.61), channel_id=1, source_target_pairs={{0,24},{4,28},{8,0},{12,4},{16,8},{20,12},{24,16},{28,20},{1,25},{... | collective-permute-start | bytes 786440 | tf_op jit(solution)/shard_map/ppermute | solution.py:761
  111.5 22.9 %collective-permute-start.18 = (bf16[256,512]{1,0:T(8,128)(2,1)S(1)}, bf16[256,512]{1,0:T(8,128)(2,1)S(1)}, u32[]{:S(2)}, u32[]{:S(2)}) collective-permute-start(bf16[256,512]{1,0:T(8,128)(2,1)S(1)} %copy-done.61), channel_id=1, source_target_pairs={{0,4},{4,0},{8,12},{12,8},{16,20},{20,16},{24,28},{28,24},{1,5},{5... | collective-permute-start | bytes 786440 | tf_op jit(solution)/shard_map/ppermute | solution.py:761
  137.1 31.5 %collective-permute-start.24 = (bf16[4,2,48,1152]{3,2,1,0:T(8,128)(2,1)S(1)}, bf16[4,2,48,1152]{3,2,1,0:T(8,128)(2,1)}, u32[]{:S(2)}, u32[]{:S(2)}) collective-permute-start(bf16[4,2,48,1152]{3,2,1,0:T(8,128)(2,1)S(1)} %pad_maximum_fusion.4), channel_id=1, source_target_pairs={{0,2},{1,3},{2,0},{3,1},{4,6},{5,7},{6,4},{7,5},{8,10},{9,11},{10,... | collective-permute-start | bytes 2654216 | tf_op jit(solution)/shard_map/ppermute | solution.py:767
  138.4 31.2 %collective-permute-start.25 = (bf16[4,2,48,1152]{3,2,1,0:T(8,128)(2,1)S(1)}, bf16[4,2,48,1152]{3,2,1,0:T(8,128)(2,1)}, u32[]{:S(2)}, u32[]{:S(2)}) collective-permute-start(bf16[4,2,48,1152]{3,2,1,0:T(8,128)(2,1)S(1)} %pad_maximum_fusion.5), channel_id=1, source_target_pairs={{0,1},{1,0},{2,3},{3,2},{4,5},{5,4},{6,7},{7,6},{8,9},{9,8},{10,11... | collective-permute-start | bytes 2654216 | tf_op jit(solution)/shard_map/ppermute | solution.py:767
  139.8 20.2 %collective-permute-start.26 = (bf16[256,1536]{1,0:T(8,128)(2,1)}, bf16[256,1536]{1,0:T(8,128)(2,1)}, u32[]{:S(2)}, u32[]{:S(2)}) collective-permute-start(bf16[256,1536]{1,0:T(8,128)(2,1)} %bitcast.186), channel_id=1, source_target_pairs={{0,8},{4,12},{8,16},{12,20},{16,24},{20,28},{24,0},{28,4},{1,9},{5... | collective-permute-start | bytes 2359304 | tf_op jit(solution)/shard_map/ppermute | solution.py:761
  169.6 19.0 %collective-permute-start.29 = (bf16[256,1536]{1,0:T(8,128)(2,1)}, bf16[256,1536]{1,0:T(8,128)(2,1)}, u32[]{:S(2)}, u32[]{:S(2)}) collective-permute-start(bf16[256,1536]{1,0:T(8,128)(2,1)} %collective-permute-done.26.grad_own), channel_id=1, source_target_pairs={{0,8},{4,12},{8,16},{12,20},{16,24},{20,28},{24,0},{28,4},{1,9},{5... | collective-permute-start | bytes 2359304 | tf_op jit(solution)/shard_map/ppermute | solution.py:761
  169.6 40.1 %collective-permute-start.27 = (bf16[4,2,48,1152]{3,2,1,0:T(8,128)(2,1)}, bf16[4,2,48,1152]{3,2,1,0:T(8,128)(2,1)}, u32[]{:S(2)}, u32[]{:S(2)}) collective-permute-start(bf16[4,2,48,1152]{3,2,1,0:T(8,128)(2,1)} %collective-permute-done.22), channel_id=1, source_target_pairs={{0,2},{1,3},{2,0},{3,1},{4,6},{5,7},{6,4},{7,5},{8,10},{9,11},{10,... | collective-permute-start | bytes 2654216 | tf_op jit(solution)/shard_map/ppermute | solution.py:767
  170.4 39.6 %collective-permute-start.28 = (bf16[4,2,48,1152]{3,2,1,0:T(8,128)(2,1)}, bf16[4,2,48,1152]{3,2,1,0:T(8,128)(2,1)}, u32[]{:S(2)}, u32[]{:S(2)}) collective-permute-start(bf16[4,2,48,1152]{3,2,1,0:T(8,128)(2,1)} %collective-permute-done.23), channel_id=1, source_target_pairs={{0,1},{1,0},{2,3},{3,2},{4,5},{5,4},{6,7},{7,6},{8,9},{9,8},{10,11... | collective-permute-start | bytes 2654216 | tf_op jit(solution)/shard_map/ppermute | solution.py:767
  171.8 17.4 %collective-permute-start.31 = (bf16[256,1536]{1,0:T(8,128)(2,1)}, bf16[256,1536]{1,0:T(8,128)(2,1)}, u32[]{:S(2)}, u32[]{:S(2)}) collective-permute-start(bf16[256,1536]{1,0:T(8,128)(2,1)} %collective-permute-done.26.grad_own), channel_id=1, source_target_pairs={{0,4},{4,0},{8,12},{12,8},{16,20},{20,16},{24,28},{28,24},{1,5},{5... | collective-permute-start | bytes 2359304 | tf_op jit(solution)/shard_map/ppermute | solution.py:761
  171.8 17.4 %collective-permute-start.30 = (bf16[256,1536]{1,0:T(8,128)(2,1)}, bf16[256,1536]{1,0:T(8,128)(2,1)}, u32[]{:S(2)}, u32[]{:S(2)}) collective-permute-start(bf16[256,1536]{1,0:T(8,128)(2,1)} %bitcast.187), channel_id=1, source_target_pairs={{0,4},{4,0},{8,12},{12,8},{16,20},{20,16},{24,28},{28,24},{1,5},{5... | collective-permute-start | bytes 2359304 | tf_op jit(solution)/shard_map/ppermute | solution.py:761
  188.6 21.3 %collective-permute-start.32 = (bf16[256,1536]{1,0:T(8,128)(2,1)}, bf16[256,1536]{1,0:T(8,128)(2,1)S(1)}, u32[]{:S(2)}, u32[]{:S(2)}) collective-permute-start(bf16[256,1536]{1,0:T(8,128)(2,1)} %get-tuple-element.452.normed_own), channel_id=1, source_target_pairs={{0,4},{4,0},{8,12},{12,8},{16,20},{20,16},{24,28},{28,24},{1,5},{5... | collective-permute-start | bytes 2359304 | tf_op jit(solution)/shard_map/ppermute | solution.py:761
  210.8 35.6 %collective-permute-start.33 = (bf16[256,1536]{1,0:T(8,128)(2,1)}, bf16[256,1536]{1,0:T(8,128)(2,1)}, u32[]{:S(2)}, u32[]{:S(2)}) collective-permute-start(bf16[256,1536]{1,0:T(8,128)(2,1)} %get-tuple-element.452.normed_own), channel_id=1, source_target_pairs={{0,8},{4,12},{8,16},{12,20},{16,24},{20,28},{24,0},{28,4},{1,9},{5... | collective-permute-start | bytes 2359304 | tf_op jit(solution)/shard_map/ppermute | solution.py:761
  213.2 33.8 %collective-permute-start.35 = (bf16[256,1536]{1,0:T(8,128)(2,1)}, bf16[256,1536]{1,0:T(8,128)(2,1)}, u32[]{:S(2)}, u32[]{:S(2)}) collective-permute-start(bf16[256,1536]{1,0:T(8,128)(2,1)} %collective-permute-done.29.grad_own), channel_id=1, source_target_pairs={{0,8},{4,12},{8,16},{12,20},{16,24},{20,28},{24,0},{28,4},{1,9},{5... | collective-permute-start | bytes 2359304 | tf_op jit(solution)/shard_map/ppermute | solution.py:761
  250.0 19.9 %collective-permute-start.38 = (bf16[256,1536]{1,0:T(8,128)(2,1)}, bf16[256,1536]{1,0:T(8,128)(2,1)S(1)}, u32[]{:S(2)}, u32[]{:S(2)}) collective-permute-start(bf16[256,1536]{1,0:T(8,128)(2,1)} %collective-permute-done.33.normed_own), channel_id=1, source_target_pairs={{0,8},{4,12},{8,16},{12,20},{16,24},{20,28},{24,0},{28,4},{1,9},{5... | collective-permute-start | bytes 2359304 | tf_op jit(solution)/shard_map/ppermute | solution.py:761
  274.0 20.4 %collective-permute-start.43 = (bf16[256,1536]{1,0:T(8,128)(2,1)S(1)}, bf16[256,1536]{1,0:T(8,128)(2,1)S(1)}, u32[]{:S(2)}, u32[]{:S(2)}) collective-permute-start(bf16[256,1536]{1,0:T(8,128)(2,1)S(1)} %collective-permute-done.38.normed_own), channel_id=1, source_target_pairs={{0,8},{4,12},{8,16},{12,20},{16,24},{20,28},{24,0},{28,4},{1,9},{5... | collective-permute-start | bytes 2359304 | tf_op jit(solution)/shard_map/ppermute | solution.py:761
  275.5 35.0 %collective-permute-start.42 = (bf16[256,1536]{1,0:T(8,128)(2,1)S(1)}, bf16[256,1536]{1,0:T(8,128)(2,1)S(1)}, u32[]{:S(2)}, u32[]{:S(2)}) collective-permute-start(bf16[256,1536]{1,0:T(8,128)(2,1)S(1)} %add.775), channel_id=1, source_target_pairs={{0,8},{4,12},{8,16},{12,20},{16,24},{20,28},{24,0},{28,4},{1,9},{5... | collective-permute-start | bytes 2359304 | tf_op jit(solution)/shard_map/ppermute | solution.py:761
  293.9 16.6 %collective-permute-start.41 = (bf16[256,1536]{1,0:T(8,128)(2,1)S(1)}, bf16[256,1536]{1,0:T(8,128)(2,1)S(1)}, u32[]{:S(2)}, u32[]{:S(2)}) collective-permute-start(bf16[256,1536]{1,0:T(8,128)(2,1)S(1)} %get-tuple-element.507), channel_id=1, source_target_pairs={{0,4},{4,0},{8,12},{12,8},{16,20},{20,16},{24,28},{28,24},{1,5},{5... | collective-permute-start | bytes 2359304 | tf_op jit(solution)/shard_map/ppermute | solution.py:761
  294.4 16.4 %collective-permute-start.44 = (bf16[256,1536]{1,0:T(8,128)(2,1)S(1)}, bf16[256,1536]{1,0:T(8,128)(2,1)S(1)}, u32[]{:S(2)}, u32[]{:S(2)}) collective-permute-start(bf16[256,1536]{1,0:T(8,128)(2,1)S(1)} %collective-permute-done.43.normed_own), channel_id=1, source_target_pairs={{0,4},{4,0},{8,12},{12,8},{16,20},{20,16},{24,28},{28,24},{1,5},{5... | collective-permute-start | bytes 2359304 | tf_op jit(solution)/shard_map/ppermute | solution.py:761
  294.5 37.3 %collective-permute-start.48 = (bf16[256,1536]{1,0:T(8,128)(2,1)S(1)}, bf16[256,1536]{1,0:T(8,128)(2,1)S(1)}, u32[]{:S(2)}, u32[]{:S(2)}) collective-permute-start(bf16[256,1536]{1,0:T(8,128)(2,1)S(1)} %get-tuple-element.551), channel_id=1, source_target_pairs={{0,4},{4,0},{8,12},{12,8},{16,20},{20,16},{24,28},{28,24},{1,5},{5... | collective-permute-start | bytes 2359304 | tf_op jit(solution)/shard_map/ppermute | solution.py:761
  310.8 23.8 %collective-permute-start.46 = (bf16[256,1536]{1,0:T(8,128)(2,1)S(1)}, bf16[256,1536]{1,0:T(8,128)(2,1)S(1)}, u32[]{:S(2)}, u32[]{:S(2)}) collective-permute-start(bf16[256,1536]{1,0:T(8,128)(2,1)S(1)} %add.776), channel_id=1, source_target_pairs={{0,8},{4,12},{8,16},{12,20},{16,24},{20,28},{24,0},{28,4},{1,9},{5... | collective-permute-start | bytes 2359304 | tf_op jit(solution)/shard_map/ppermute | solution.py:761
  333.0 26.4 %collective-permute-start.50 = (bf16[256,1536]{1,0:T(8,128)(2,1)}, bf16[256,1536]{1,0:T(8,128)(2,1)}, u32[]{:S(2)}, u32[]{:S(2)}) collective-permute-start(bf16[256,1536]{1,0:T(8,128)(2,1)} %add.778), channel_id=1, source_target_pairs={{0,8},{4,12},{8,16},{12,20},{16,24},{20,28},{24,0},{28,4},{1,9},{5... | collective-permute-start | bytes 2359304 | tf_op jit(solution)/shard_map/ppermute | solution.py:761
  334.3 36.8 %collective-permute-start.49 = (bf16[256,1536]{1,0:T(8,128)(2,1)}, bf16[256,1536]{1,0:T(8,128)(2,1)}, u32[]{:S(2)}, u32[]{:S(2)}) collective-permute-start(bf16[256,1536]{1,0:T(8,128)(2,1)} %get-tuple-element.553), channel_id=1, source_target_pairs={{0,4},{4,0},{8,12},{12,8},{16,20},{20,16},{24,28},{28,24},{1,5},{5... | collective-permute-start | bytes 2359304 | tf_op jit(solution)/shard_map/ppermute | solution.py:761
  335.8 37.9 %collective-permute-start.47 = (bf16[256,1536]{1,0:T(8,128)(2,1)}, bf16[256,1536]{1,0:T(8,128)(2,1)}, u32[]{:S(2)}, u32[]{:S(2)}) collective-permute-start(bf16[256,1536]{1,0:T(8,128)(2,1)} %add.777), channel_id=1, source_target_pairs={{0,8},{4,12},{8,16},{12,20},{16,24},{20,28},{24,0},{28,4},{1,9},{5... | collective-permute-start | bytes 2359304 | tf_op jit(solution)/shard_map/ppermute | solution.py:761
  373.6 30.2 %collective-permute-start.51 = (bf16[8,48,1152]{2,1,0:T(8,128)(2,1)}, bf16[8,48,1152]{2,1,0:T(8,128)(2,1)S(1)}, u32[]{:S(2)}, u32[]{:S(2)}) collective-permute-start(bf16[8,48,1152]{2,1,0:T(8,128)(2,1)} %bitcast.69), channel_id=1, source_target_pairs={{0,1},{1,0},{2,3},{3,2},{4,5},{5,4},{6,7},{7,6},{8,9},{9,8},{10,11... | collective-permute-start | bytes 2654216 | tf_op jit(solution)/shard_map/ppermute | solution.py:767
  374.9 29.0 %collective-permute-start.52 = (bf16[8,48,1152]{2,1,0:T(8,128)(2,1)}, bf16[8,48,1152]{2,1,0:T(8,128)(2,1)S(1)}, u32[]{:S(2)}, u32[]{:S(2)}) collective-permute-start(bf16[8,48,1152]{2,1,0:T(8,128)(2,1)} %bitcast.71), channel_id=1, source_target_pairs={{0,2},{1,3},{2,0},{3,1},{4,6},{5,7},{6,4},{7,5},{8,10},{9,11},{10,... | collective-permute-start | bytes 2654216 | tf_op jit(solution)/shard_map/ppermute | solution.py:767
  376.1 27.8 %collective-permute-start.54 = (bf16[256,1536]{1,0:T(8,128)(2,1)S(1)}, bf16[256,1536]{1,0:T(8,128)(2,1)S(1)}, u32[]{:S(2)}, u32[]{:S(2)}) collective-permute-start(bf16[256,1536]{1,0:T(8,128)(2,1)S(1)} %add.779), channel_id=1, source_target_pairs={{0,8},{4,12},{8,16},{12,20},{16,24},{20,28},{24,0},{28,4},{1,9},{5... | collective-permute-start | bytes 2359304 | tf_op jit(solution)/shard_map/ppermute | solution.py:761
  377.0 26.9 %collective-permute-start.55 = (bf16[256,1536]{1,0:T(8,128)(2,1)}, bf16[256,1536]{1,0:T(8,128)(2,1)S(1)}, u32[]{:S(2)}, u32[]{:S(2)}) collective-permute-start(bf16[256,1536]{1,0:T(8,128)(2,1)} %get-tuple-element.572), channel_id=1, source_target_pairs={{0,4},{4,0},{8,12},{12,8},{16,20},{20,16},{24,28},{28,24},{1,5},{5... | collective-permute-start | bytes 2359304 | tf_op jit(solution)/shard_map/ppermute | solution.py:761
  407.6 26.9 %collective-permute-start.60 = (bf16[8,48,1152]{2,1,0:T(8,128)(2,1)}, bf16[8,48,1152]{2,1,0:T(8,128)(2,1)S(1)}, u32[]{:S(2)}, u32[]{:S(2)}) collective-permute-start(bf16[8,48,1152]{2,1,0:T(8,128)(2,1)} %bitcast.227), channel_id=1, source_target_pairs={{0,1},{1,0},{2,3},{3,2},{4,5},{5,4},{6,7},{7,6},{8,9},{9,8},{10,11... | collective-permute-start | bytes 2654216 | tf_op jit(solution)/shard_map/ppermute | solution.py:767
  408.9 25.7 %collective-permute-start.61 = (bf16[8,48,1152]{2,1,0:T(8,128)(2,1)}, bf16[8,48,1152]{2,1,0:T(8,128)(2,1)S(1)}, u32[]{:S(2)}, u32[]{:S(2)}) collective-permute-start(bf16[8,48,1152]{2,1,0:T(8,128)(2,1)} %bitcast.226), channel_id=1, source_target_pairs={{0,2},{1,3},{2,0},{3,1},{4,6},{5,7},{6,4},{7,5},{8,10},{9,11},{10,... | collective-permute-start | bytes 2654216 | tf_op jit(solution)/shard_map/ppermute | solution.py:767
  409.5 25.0 %collective-permute-start.57 = (bf16[256,512]{1,0:T(8,128)(2,1)S(1)}, bf16[256,512]{1,0:T(8,128)(2,1)S(1)}, u32[]{:S(2)}, u32[]{:S(2)}) collective-permute-start(bf16[256,512]{1,0:T(8,128)(2,1)S(1)} %get-tuple-element.592), channel_id=1, source_target_pairs={{0,24},{4,28},{8,0},{12,4},{16,8},{20,12},{24,16},{28,20},{1,25},{... | collective-permute-start | bytes 786440 | tf_op jit(solution)/shard_map/ppermute | solution.py:761
  410.0 24.4 %collective-permute-start.58 = (bf16[256,512]{1,0:T(8,128)(2,1)S(1)}, bf16[256,512]{1,0:T(8,128)(2,1)S(1)}, u32[]{:S(2)}, u32[]{:S(2)}) collective-permute-start(bf16[256,512]{1,0:T(8,128)(2,1)S(1)} %get-tuple-element.593), channel_id=1, source_target_pairs={{0,16},{4,20},{8,24},{12,28},{16,0},{20,4},{24,8},{28,12},{1,17},{... | collective-permute-start | bytes 786440 | tf_op jit(solution)/shard_map/ppermute | solution.py:761
  411.8 22.7 %collective-permute-start.59 = (bf16[256,512]{1,0:T(8,128)(2,1)S(1)}, bf16[256,512]{1,0:T(8,128)(2,1)S(1)}, u32[]{:S(2)}, u32[]{:S(2)}) collective-permute-start(bf16[256,512]{1,0:T(8,128)(2,1)S(1)} %get-tuple-element.594), channel_id=1, source_target_pairs={{0,8},{4,12},{8,16},{12,20},{16,24},{20,28},{24,0},{28,4},{1,9},{5... | collective-permute-start | bytes 786440 | tf_op jit(solution)/shard_map/ppermute | solution.py:761
  434.5 28.0 %collective-permute-start.64 = (bf16[16,48,1536]{2,1,0:T(8,128)(2,1)}, bf16[16,48,1536]{2,1,0:T(8,128)(2,1)}, u32[]{:S(2)}, u32[]{:S(2)}) collective-permute-start(bf16[16,48,1536]{2,1,0:T(8,128)(2,1)} %bitcast.84), channel_id=1, source_target_pairs={{0,4},{4,0},{8,12},{12,8},{16,20},{20,16},{24,28},{28,24},{1,5},{5... | collective-permute-start | bytes 7077896 | tf_op jit(solution)/shard_map/ppermute | solution.py:761
  434.6 27.9 %collective-permute-start.65 = (bf16[16,48,1536]{2,1,0:T(8,128)(2,1)}, bf16[16,48,1536]{2,1,0:T(8,128)(2,1)}, u32[]{:S(2)}, u32[]{:S(2)}) collective-permute-start(bf16[16,48,1536]{2,1,0:T(8,128)(2,1)} %bitcast.88), channel_id=1, source_target_pairs={{0,4},{4,0},{8,12},{12,8},{16,20},{20,16},{24,28},{28,24},{1,5},{5... | collective-permute-start | bytes 7077896 | tf_op jit(solution)/shard_map/ppermute | solution.py:761
  437.3 23.7 %collective-permute-start.62 = (bf16[8,48,1152]{2,1,0:T(8,128)(2,1)}, bf16[8,48,1152]{2,1,0:T(8,128)(2,1)}, u32[]{:S(2)}, u32[]{:S(2)}) collective-permute-start(bf16[8,48,1152]{2,1,0:T(8,128)(2,1)} %bitcast.91), channel_id=1, source_target_pairs={{0,2},{1,3},{2,0},{3,1},{4,6},{5,7},{6,4},{7,5},{8,10},{9,11},{10,... | collective-permute-start | bytes 2654216 | tf_op jit(solution)/shard_map/ppermute | solution.py:767
  440.9 21.7 %collective-permute-start.63 = (bf16[8,48,1152]{2,1,0:T(8,128)(2,1)}, bf16[8,48,1152]{2,1,0:T(8,128)(2,1)}, u32[]{:S(2)}, u32[]{:S(2)}) collective-permute-start(bf16[8,48,1152]{2,1,0:T(8,128)(2,1)} %bitcast.97), channel_id=1, source_target_pairs={{0,1},{1,0},{2,3},{3,2},{4,5},{5,4},{6,7},{7,6},{8,9},{9,8},{10,11... | collective-permute-start | bytes 2654216 | tf_op jit(solution)/shard_map/ppermute | solution.py:767
  441.7 19.3 %collective-permute-start.66 = (bf16[256,1536]{1,0:T(8,128)(2,1)}, bf16[256,1536]{1,0:T(8,128)(2,1)}, u32[]{:S(2)}, u32[]{:S(2)}) collective-permute-start(bf16[256,1536]{1,0:T(8,128)(2,1)} %add.780), channel_id=1, source_target_pairs={{0,8},{4,12},{8,16},{12,20},{16,24},{20,28},{24,0},{28,4},{1,9},{5... | collective-permute-start | bytes 2359304 | tf_op jit(solution)/shard_map/ppermute | solution.py:761
  465.3 21.2 %collective-permute-start.70 = (bf16[2,288,768]{2,1,0:T(8,128)(2,1)S(1)}, bf16[2,288,768]{2,1,0:T(8,128)(2,1)S(1)}, u32[]{:S(2)}, u32[]{:S(2)}) collective-permute-start(bf16[2,288,768]{2,1,0:T(8,128)(2,1)S(1)} %copy-done.73), channel_id=1, source_target_pairs={{0,1},{1,0},{2,3},{3,2},{4,5},{5,4},{6,7},{7,6},{8,9},{9,8},{10,11... | collective-permute-start | bytes 2654216 | tf_op jit(solution)/shard_map/ppermute | solution.py:767
  466.2 20.9 %collective-permute-start.71 = (bf16[2,288,768]{2,1,0:T(8,128)(2,1)S(1)}, bf16[2,288,768]{2,1,0:T(8,128)(2,1)S(1)}, u32[]{:S(2)}, u32[]{:S(2)}) collective-permute-start(bf16[2,288,768]{2,1,0:T(8,128)(2,1)S(1)} %copy-done.70), channel_id=1, source_target_pairs={{0,2},{1,3},{2,0},{3,1},{4,6},{5,7},{6,4},{7,5},{8,10},{9,11},{10,... | collective-permute-start | bytes 2654216 | tf_op jit(solution)/shard_map/ppermute | solution.py:767
  487.1 32.7 %collective-permute-start.74 = (bf16[8,48,1920]{2,1,0:T(8,128)(2,1)S(1)}, bf16[8,48,1920]{2,1,0:T(8,128)(2,1)S(1)}, u32[]{:S(2)}, u32[]{:S(2)}) collective-permute-start(bf16[8,48,1920]{2,1,0:T(8,128)(2,1)S(1)} %bitcast.224), channel_id=1, source_target_pairs={{0,1},{1,0},{2,3},{3,2},{4,5},{5,4},{6,7},{7,6},{8,9},{9,8},{10,11... | collective-permute-start | bytes 4423688 | tf_op jit(solution)/shard_map/ppermute | solution.py:767
  488.3 31.5 %collective-permute-start.75 = (bf16[8,48,1792]{2,1,0:T(8,128)(2,1)S(1)}, bf16[8,48,1792]{2,1,0:T(8,128)(2,1)S(1)}, u32[]{:S(2)}, u32[]{:S(2)}) collective-permute-start(bf16[8,48,1792]{2,1,0:T(8,128)(2,1)S(1)} %bitcast.225), channel_id=1, source_target_pairs={{0,2},{1,3},{2,0},{3,1},{4,6},{5,7},{6,4},{7,5},{8,10},{9,11},{10,... | collective-permute-start | bytes 4128776 | tf_op jit(solution)/shard_map/ppermute | solution.py:767
  488.9 21.7 %collective-permute-start.72 = (bf16[2,2,48,1152]{3,2,1,0:T(8,128)(2,1)S(1)}, bf16[2,2,48,1152]{3,2,1,0:T(8,128)(2,1)S(1)}, u32[]{:S(2)}, u32[]{:S(2)}) collective-permute-start(bf16[2,2,48,1152]{3,2,1,0:T(8,128)(2,1)S(1)} %copy-done.85), channel_id=1, source_target_pairs={{0,8},{4,12},{8,16},{12,20},{16,24},{20,28},{24,0},{28,4},{1,9},{5... | collective-permute-start | bytes 1327112 | tf_op jit(solution)/shard_map/ppermute | solution.py:761
  490.8 29.0 %collective-permute-start.73 = (bf16[2,2,48,1152]{3,2,1,0:T(8,128)(2,1)S(1)}, bf16[2,2,48,1152]{3,2,1,0:T(8,128)(2,1)S(1)}, u32[]{:S(2)}, u32[]{:S(2)}) collective-permute-start(bf16[2,2,48,1152]{3,2,1,0:T(8,128)(2,1)S(1)} %copy-done.83), channel_id=1, source_target_pairs={{0,16},{4,20},{8,24},{12,28},{16,0},{20,4},{24,8},{28,12},{1,17},{... | collective-permute-start | bytes 1327112 | tf_op jit(solution)/shard_map/ppermute | solution.py:761
  520.2 18.7 %collective-permute-start.78 = (bf16[4,48,1920]{2,1,0:T(8,128)(2,1)S(1)}, bf16[4,48,1920]{2,1,0:T(8,128)(2,1)S(1)}, u32[]{:S(2)}, u32[]{:S(2)}) collective-permute-start(bf16[4,48,1920]{2,1,0:T(8,128)(2,1)S(1)} %bitcast.228), channel_id=1, source_target_pairs={{0,2},{1,3},{2,0},{3,1},{4,6},{5,7},{6,4},{7,5},{8,10},{9,11},{10,... | collective-permute-start | bytes 2211848 | tf_op jit(solution)/shard_map/ppermute | solution.py:767
  521.9 16.8 %collective-permute-start.79 = (bf16[4,48,1792]{2,1,0:T(8,128)(2,1)S(1)}, bf16[4,48,1792]{2,1,0:T(8,128)(2,1)S(1)}, u32[]{:S(2)}, u32[]{:S(2)}) collective-permute-start(bf16[4,48,1792]{2,1,0:T(8,128)(2,1)S(1)} %bitcast.229), channel_id=1, source_target_pairs={{0,1},{1,0},{2,3},{3,2},{4,5},{5,4},{6,7},{7,6},{8,9},{9,8},{10,11... | collective-permute-start | bytes 2064392 | tf_op jit(solution)/shard_map/ppermute | solution.py:767
  522.8 16.3 %collective-permute-start.77 = (bf16[2,2,48,1152]{3,2,1,0:T(8,128)(2,1)S(1)}, bf16[2,2,48,1152]{3,2,1,0:T(8,128)(2,1)S(1)}, u32[]{:S(2)}, u32[]{:S(2)}) collective-permute-start(bf16[2,2,48,1152]{3,2,1,0:T(8,128)(2,1)S(1)} %copy-done.79), channel_id=1, source_target_pairs={{0,24},{4,28},{8,0},{12,4},{16,8},{20,12},{24,16},{28,20},{1,25},{... | collective-permute-start | bytes 1327112 | tf_op jit(solution)/shard_map/ppermute | solution.py:761
  539.1 25.6 %collective-permute-start.80 = (bf16[48,3712]{1,0:T(8,128)(2,1)S(1)}, bf16[48,3712]{1,0:T(8,128)(2,1)S(1)}, u32[]{:S(2)}, u32[]{:S(2)}) collective-permute-start(bf16[48,3712]{1,0:T(8,128)(2,1)S(1)} %pad_maximum_fusion.8), channel_id=1, source_target_pairs={{0,8},{4,12},{8,16},{12,20},{16,24},{20,28},{24,0},{28,4},{1,9},{5... | collective-permute-start | bytes 1069064 | tf_op jit(solution)/shard_map/ppermute | solution.py:761
  540.7 29.0 %collective-permute-start.81 = (bf16[48,3712]{1,0:T(8,128)(2,1)S(1)}, bf16[48,3712]{1,0:T(8,128)(2,1)S(1)}, u32[]{:S(2)}, u32[]{:S(2)}) collective-permute-start(bf16[48,3712]{1,0:T(8,128)(2,1)S(1)} %pad_maximum_fusion.9), channel_id=1, source_target_pairs={{0,16},{4,20},{8,24},{12,28},{16,0},{20,4},{24,8},{28,12},{1,17},{... | collective-permute-start | bytes 1069064 | tf_op jit(solution)/shard_map/ppermute | solution.py:761
  545.1 28.6 %collective-permute-start.82 = (bf16[48,3712]{1,0:T(8,128)(2,1)S(1)}, bf16[48,3712]{1,0:T(8,128)(2,1)S(1)}, u32[]{:S(2)}, u32[]{:S(2)}) collective-permute-start(bf16[48,3712]{1,0:T(8,128)(2,1)S(1)} %pad_maximum_fusion.10), channel_id=1, source_target_pairs={{0,24},{4,28},{8,0},{12,4},{16,8},{20,12},{24,16},{28,20},{1,25},{... | collective-permute-start | bytes 1069064 | tf_op jit(solution)/shard_map/ppermute | solution.py:761
  (136 other events, 1141.8 us)
Sparse Core Ops, SparseCore 0:
  33.2 95.6 all-gather.2
  131.3 78.1 all-gather.4
